TPU v7x, 32 devices: a whole 2x2x4 slice. The times are simulated.
32 devices in a mesh: seq: 4 (over y, x), fsdp: 8 (over z, core).
Axes of the slice: x: 2, y: 2, z: 4, core: 2. Of those that a mesh axis runs over, the one named last changes fastest.
Arguments:
- hidden_in: bfloat16 [8, 512, 2048], P('fsdp', 'seq'), may hold values from -6 to 6
- gain_attn: bfloat16 [2048], P('fsdp'), may hold values from 0.5 to 1.5
- attn_weights: bfloat16 [2048, 4, 2048], P('fsdp'), may hold values from -0.375 to 0.375
- gain_mlp: bfloat16 [2048], P('fsdp'), may hold values from 0.5 to 1.5
- mlp_weights: bfloat16 [8192, 3, 2048], P('fsdp'), may hold values from -0.13258252 to 0.13258252
- out_grad: bfloat16 [8, 512, 2048], P('fsdp', 'seq'), may hold values from -6 to 6
- block_slots: int32 [4, 2], replicated, may hold values from 0 to 7, as said below
- doc_ids: int32 [8, 512], P('fsdp'), may hold values from 0 to 2, as said below
Outputs:
- block_out: bfloat16 [8, 512, 2048], P('fsdp', 'seq')
- grad_in: bfloat16 [8, 512, 2048], P('fsdp', 'seq')
- grad_gain_attn: float32 [2048], P('fsdp')
- grad_attn_weights: float32 [2048, 4, 2048], P('fsdp')
- grad_gain_mlp: float32 [2048], P('fsdp')
- grad_mlp_weights: float32 [8192, 3, 2048], P('fsdp')
Inputs may be any that keep to these rules, and one draw needn't show every extreme that they name: `block_slots`: row i holds the two query blocks given to index i of seq; one of them is p and the other 7 - p, and each of the 8 blocks stands in one row. `doc_ids`: along each sequence the document numbers never fall, and all three occur.
All inputs are finite; a program needn't handle non-finite values.
Results may differ from a plain program's by a relative error of at most 0.023.
Values may be sent and summed in bfloat16 or wider, within the bound.
A program may use at most 384 MiB of HBM per device.

v0:
```python
import jax
import jax.numpy as jnp
from jax import lax
from jax.sharding import PartitionSpec as P

HEAD = 64


NORM_EPS = 1e-05
ROPE_BASE = 130000.0
MASKED_OUT = -1e30


def angles(positions):
    freqs = ROPE_BASE ** (-jnp.arange(0, HEAD, 2).astype(jnp.float32) / HEAD)
    turn = positions.astype(jnp.float32)[:, None] * freqs[None, :]
    return (jnp.cos(turn)[:, None, :], jnp.sin(turn)[:, None, :])


def rotate(field, cosine, sine):
    half = field.shape[-1] // 2
    front = field[..., :half]
    back_half = field[..., half:]
    return jnp.concatenate(
        [front * cosine - back_half * sine, back_half * cosine + front * sine], -1
    )


def norm_back(grad_normed, value, scale, gain):
    weighted = grad_normed * gain
    inner_mean = jnp.mean(weighted * value, axis=-1, keepdims=True)
    return scale * (weighted - value * scale * scale * inner_mean)


def gate_up_back(grad_act, gate_val, up_val):
    sigma = jax.nn.sigmoid(gate_val)
    grad_gate = grad_act * up_val * sigma * (1.0 + gate_val * (1.0 - sigma))
    grad_up = grad_act * gate_val * sigma
    return jnp.stack([grad_gate, grad_up], 1).astype(jnp.bfloat16)


def on_device(
    hidden_in, gain_attn, attn_weights, gain_mlp, mlp_weights, out_grad, block_slots, doc_ids
):
    tok_rows = hidden_in.shape[1]
    model_width = hidden_in.shape[2]
    length = doc_ids.shape[1]
    head_count = model_width // HEAD
    block_rows = tok_rows // 2
    slot_table = block_slots.reshape(-1)
    seq_index = lax.axis_index("seq")
    within = jnp.arange(block_rows, dtype=jnp.int32)
    key_pos = (slot_table[:, None] * block_rows + within[None, :]).reshape(-1)
    own_slots = lax.dynamic_slice_in_dim(block_slots, seq_index, 1, 0).reshape(-1)
    query_pos = (own_slots[:, None] * block_rows + within[None, :]).reshape(-1)
    doc_line = doc_ids[0]
    key_doc = doc_line[key_pos]
    query_doc = doc_line[query_pos]
    cosine, sine = angles(query_pos)
    source = hidden_in[0].astype(jnp.float32)
    gains_a, gains_m, attn_full = (
        lax.all_gather(gain_attn, "fsdp", axis=0, tiled=True),
        lax.all_gather(gain_mlp, "fsdp", axis=0, tiled=True),
        lax.all_gather(attn_weights, "fsdp", axis=0, tiled=True),
    )
    gains_a = gains_a.astype(jnp.float32)
    gains_m = gains_m.astype(jnp.float32)
    scale_a = lax.rsqrt(jnp.mean(source * source, axis=-1, keepdims=True) + NORM_EPS)
    normed_a = (source * scale_a * gains_a).astype(jnp.bfloat16)
    qkv = jnp.dot(
        normed_a,
        attn_full[:, :3, :].reshape(model_width, 3 * model_width),
        preferred_element_type=jnp.float32,
    )
    queries = rotate(qkv[:, :model_width].reshape(tok_rows, head_count, HEAD), cosine, sine).astype(
        jnp.bfloat16
    )
    keys_own = rotate(
        qkv[:, model_width : 2 * model_width].reshape(tok_rows, head_count, HEAD), cosine, sine
    )
    keys_own = keys_own.reshape(tok_rows, model_width).astype(jnp.bfloat16)
    values_own = qkv[:, 2 * model_width :].astype(jnp.bfloat16)
    keys_all, values_all = (
        lax.all_gather(keys_own, "seq", axis=0, tiled=True),
        lax.all_gather(values_own, "seq", axis=0, tiled=True),
    )
    key_span = min(length, 512)
    key_steps = length // key_span
    key_blocks = keys_all.reshape(key_steps, key_span, head_count, HEAD)
    value_blocks = values_all.reshape(key_steps, key_span, head_count, HEAD)
    pos_blocks = key_pos.reshape(key_steps, key_span)
    doc_blocks = key_doc.reshape(key_steps, key_span)
    block_inputs = (key_blocks, value_blocks, pos_blocks, doc_blocks)

    def scores_of(key_block, pos_block, doc_block):
        raw = (
            jnp.einsum("qhd,khd->hqk", queries, key_block, preferred_element_type=jnp.float32)
            * 0.125
        )
        allowed = (
            (pos_block[None, :] <= query_pos[:, None]) & (doc_block[None, :] == query_doc[:, None])
        )[None]
        return (jnp.where(allowed, raw, MASKED_OUT), allowed)

    def max_step(state_now, block_in):
        row_top, row_total = state_now
        masked, allowed = scores_of(block_in[0], block_in[2], block_in[3])
        new_top = jnp.maximum(row_top, jnp.max(masked, axis=-1))
        kept = jnp.where(allowed, jnp.exp(masked - new_top[..., None]), 0.0)
        row_total = row_total * jnp.exp(row_top - new_top) + jnp.sum(kept, axis=-1)
        return ((new_top, row_total), None)

    start_top = jnp.full((head_count, tok_rows), MASKED_OUT, jnp.float32)
    start_total = jnp.zeros((head_count, tok_rows), jnp.float32)
    (row_top, row_total), _ = lax.scan(max_step, (start_top, start_total), block_inputs)
    log_total = row_top + jnp.log(row_total)

    def probs_of(block_in):
        masked, allowed = scores_of(block_in[0], block_in[2], block_in[3])
        return jnp.where(allowed, jnp.exp(masked - log_total[..., None]), 0.0)

    def out_step(running, block_in):
        attn_prob = probs_of(block_in).astype(jnp.bfloat16)
        return (
            running
            + jnp.einsum(
                "hqk,khd->qhd", attn_prob, block_in[1], preferred_element_type=jnp.float32
            ),
            None,
        )

    attn_mix, _ = lax.scan(
        out_step, jnp.zeros((tok_rows, head_count, HEAD), jnp.float32), block_inputs
    )
    mixed_low = attn_mix.reshape(tok_rows, model_width).astype(jnp.bfloat16)
    middle = source + jnp.dot(mixed_low, attn_full[:, 3, :], preferred_element_type=jnp.float32)
    scale_m = lax.rsqrt(jnp.mean(middle * middle, axis=-1, keepdims=True) + NORM_EPS)
    normed_m = (middle * scale_m * gains_m).astype(jnp.bfloat16)
    grad_out = out_grad[0]
    tok_all = lax.all_gather(normed_m, "fsdp", axis=0, tiled=True)
    gate_up = jnp.einsum(
        "td,ncd->tcn", tok_all, mlp_weights[:, :2], preferred_element_type=jnp.float32
    )
    gate_local = gate_up[:, 0]
    up_local = gate_up[:, 1]
    act_local = (jax.nn.silu(gate_local) * up_local).astype(jnp.bfloat16)
    down_local = mlp_weights[:, 2]
    mlp_out = lax.psum_scatter(
        jnp.dot(act_local, down_local, preferred_element_type=jnp.float32).astype(jnp.bfloat16),
        "fsdp",
        scatter_dimension=0,
        tiled=True,
    ).astype(jnp.float32)
    grad_all = lax.all_gather(grad_out, "fsdp", axis=0, tiled=True)
    grad_act = jnp.einsum("td,nd->tn", grad_all, down_local, preferred_element_type=jnp.float32)
    grad_gu = gate_up_back(grad_act, gate_local, up_local)
    proj_grad = jnp.einsum("tcn,td->ncd", grad_gu, tok_all, preferred_element_type=jnp.float32)
    down_grad = jnp.einsum("tn,td->nd", act_local, grad_all, preferred_element_type=jnp.float32)
    mlp_grad = jnp.concatenate([proj_grad, down_grad[:, None]], 1)
    grad_normed = lax.psum_scatter(
        jnp.einsum(
            "tcn,ncd->td", grad_gu, mlp_weights[:, :2], preferred_element_type=jnp.float32
        ).astype(jnp.bfloat16),
        "fsdp",
        scatter_dimension=0,
        tiled=True,
    ).astype(jnp.float32)
    block_out = (middle + mlp_out).astype(jnp.bfloat16)
    grad_middle = grad_out.astype(jnp.float32) + norm_back(grad_normed, middle, scale_m, gains_m)
    gain_m_term = jnp.sum(grad_normed * middle * scale_m, axis=0)
    grad_branch = grad_middle.astype(jnp.bfloat16)
    grad_mixed = jnp.einsum(
        "td,nd->tn", grad_branch, attn_full[:, 3], preferred_element_type=jnp.float32
    )
    grad_mix3 = grad_mixed.astype(jnp.bfloat16).reshape(tok_rows, head_count, HEAD)

    def delta_step(running, block_in):
        attn_prob = probs_of(block_in)
        grad_prob = jnp.einsum(
            "qhd,khd->hqk", grad_mix3, block_in[1], preferred_element_type=jnp.float32
        )
        return (running + jnp.sum(attn_prob * grad_prob, axis=-1), None)

    row_delta, _ = lax.scan(
        delta_step, jnp.zeros((head_count, tok_rows), jnp.float32), block_inputs
    )

    def grad_step(running, block_in):
        attn_prob = probs_of(block_in)
        grad_prob = jnp.einsum(
            "qhd,khd->hqk", grad_mix3, block_in[1], preferred_element_type=jnp.float32
        )
        grad_score = (attn_prob * (grad_prob - row_delta[..., None])).astype(jnp.bfloat16)
        running = running + jnp.einsum(
            "hqk,khd->qhd", grad_score, block_in[0], preferred_element_type=jnp.float32
        )
        key_term = jnp.einsum(
            "hqk,qhd->khd", grad_score, queries, preferred_element_type=jnp.float32
        )
        value_term = jnp.einsum(
            "hqk,qhd->khd",
            attn_prob.astype(jnp.bfloat16),
            grad_mix3,
            preferred_element_type=jnp.float32,
        )
        return (running, (key_term, value_term))

    grad_query, (key_terms, value_terms) = lax.scan(
        grad_step, jnp.zeros((tok_rows, head_count, HEAD), jnp.float32), block_inputs
    )
    key_terms = key_terms.reshape(length, model_width) * 0.125
    value_terms = value_terms.reshape(length, model_width)
    grad_key, grad_value = (
        lax.psum_scatter(
            key_terms.astype(jnp.bfloat16), "seq", scatter_dimension=0, tiled=True
        ).astype(jnp.float32),
        lax.psum_scatter(
            value_terms.astype(jnp.bfloat16), "seq", scatter_dimension=0, tiled=True
        ).astype(jnp.float32),
    )
    grad_q_pre = (
        rotate(grad_query * 0.125, cosine, -sine)
        .reshape(tok_rows, model_width)
        .astype(jnp.bfloat16)
    )
    grad_k_pre = rotate(grad_key.reshape(tok_rows, head_count, HEAD), cosine, -sine)
    grad_k_pre = grad_k_pre.reshape(tok_rows, model_width).astype(jnp.bfloat16)
    grad_qkv = jnp.stack([grad_q_pre, grad_k_pre, grad_value.astype(jnp.bfloat16)], 1)
    grad_normed_a = jnp.einsum(
        "tcn,dcn->td", grad_qkv, attn_full[:, :3], preferred_element_type=jnp.float32
    )
    grad_in = (grad_middle + norm_back(grad_normed_a, source, scale_a, gains_a)).astype(
        jnp.bfloat16
    )
    gain_a_term = jnp.sum(grad_normed_a * source * scale_a, axis=0)
    proj_grad = jnp.einsum("tn,tcd->ncd", normed_a, grad_qkv, preferred_element_type=jnp.float32)
    out_proj_grad = jnp.einsum(
        "tn,td->nd", mixed_low, grad_branch, preferred_element_type=jnp.float32
    )
    attn_grad = lax.psum_scatter(
        jnp.concatenate([proj_grad, out_proj_grad[:, None]], 1).astype(jnp.bfloat16),
        "fsdp",
        scatter_dimension=0,
        tiled=True,
    ).astype(jnp.float32)
    attn_grad, mlp_grad = (
        lax.psum(attn_grad.astype(jnp.bfloat16), "seq").astype(jnp.float32),
        lax.psum(mlp_grad.astype(jnp.bfloat16), "seq").astype(jnp.float32),
    )
    gain_a_all, gain_m_all = lax.psum((gain_a_term, gain_m_term), ("seq", "fsdp"))
    gain_share = gain_attn.shape[0]
    offset = lax.axis_index("fsdp") * gain_share
    grad_gain_a = lax.dynamic_slice_in_dim(gain_a_all, offset, gain_share, 0)
    grad_gain_m = lax.dynamic_slice_in_dim(gain_m_all, offset, gain_share, 0)
    return (block_out[None], grad_in[None], grad_gain_a, attn_grad, grad_gain_m, mlp_grad)


def solution(mesh):
    return jax.shard_map(
        on_device,
        mesh=mesh,
        in_specs=(
            P("fsdp", "seq", None),
            P("fsdp"),
            P("fsdp", None, None),
            P("fsdp"),
            P("fsdp", None, None),
            P("fsdp", "seq", None),
            P(),
            P("fsdp", None),
        ),
        out_specs=(
            P("fsdp", "seq", None),
            P("fsdp", "seq", None),
            P("fsdp"),
            P("fsdp", None, None),
            P("fsdp"),
            P("fsdp", None, None),
        ),
        check_vma=False,
    )
```

profile of v0, /device:TPU:8, one launch (start us, length us, event | category | flops | bytes accessed | tf_op | source)
XLA Modules:
  0.0 1495.0 jit_solution(13249458120845465604)
XLA Ops:
  7.2 6.5 copy.47
  14.8 9.1 all-gather.1
  24.8 275.9 %all-gather.9.cloned.1.call-done = bf16[2048,4,2048]{2,0,1:T(8,128)(2,1)} async-done(((bf16[256,4,2048]{2,0,1:T(8,128)(2,1)}), bf16[2048,4,2048]{2,0,1:T(8,128)(2,1)}) %all-gather.9.cloned.1.call-update) | async-done | bytes 33554448 | tf_op jit(solution)/shard_map/all_gather | solution.py:64
  300.7 21.0 %slice.76 = bf16[2048,3,2048]{2,0,1:T(8,128)(2,1)} slice(bf16[2048,4,2048]{2,0,1:T(8,128)(2,1)} %all-gather.9.cloned.1.call-done), slice={[0:2048], [0:3], [0:2048]} | slice | bytes 50331648 | tf_op jit(solution)/shard_map/slice | solution.py:72
  321.7 31.8 %copy.48 = bf16[2048,3,2048]{0,2,1:T(8,128)(2,1)} copy(bf16[2048,3,2048]{2,0,1:T(8,128)(2,1)} %slice.76) | data formatting | bytes 50331648 | tf_op jit(solution)/shard_map/slice | solution.py:72
  353.5 13.4 fusion.77
  368.4 2.6 copy.51
  370.9 2.5 copy.52
  373.5 2.5 subtract_convert_fusion.3
  378.4 3.5 gather_fusion
  383.2 12.1 all-gather.2
  395.4 18.0 %all-gather.13.cloned.1.call-done = bf16[512,2048]{0,1:T(8,128)(2,1)} async-done(((bf16[128,2048]{0,1:T(8,128)(2,1)}), bf16[512,2048]{0,1:T(8,128)(2,1)}) %all-gather.13.cloned.1.call-update) | async-done | bytes 2097168 | tf_op jit(solution)/shard_map/all_gather | solution.py:84
  413.4 3.4 fusion.6
  416.8 2.5 select_reduce_fusion
  420.2 31.0 %all-gather.11.cloned.1.call-done = bf16[512,2048]{1,0:T(8,128)(2,1)} async-done(((bf16[128,2048]{1,0:T(8,128)(2,1)}), bf16[512,2048]{1,0:T(8,128)(2,1)}) %all-gather.11.cloned.1.call-update) | async-done | bytes 2097168 | tf_op jit(solution)/shard_map/all_gather | solution.py:85
  451.2 2.9 copy.49
  454.1 6.5 convolution_convert_fusion.2
  460.7 4.9 multiply_reduce_fusion.1
  467.6 44.7 %all-gather.15.cloned.1.call-done = bf16[1024,2048]{1,0:T(8,128)(2,1)} async-done(((bf16[128,2048]{1,0:T(8,128)(2,1)}), bf16[1024,2048]{1,0:T(8,128)(2,1)}) %all-gather.15.cloned.1.call-update) | async-done | bytes 4194320 | tf_op jit(solution)/shard_map/all_gather | solution.py:140
  512.4 14.6 fusion.37
  526.9 32.8 %all-gather.17.cloned.1.call-done = bf16[1,1024,2048]{2,1,0:T(8,128)(2,1)} async-done(((bf16[1,128,2048]{2,1,0:T(8,128)(2,1)}), bf16[1,1024,2048]{2,1,0:T(8,128)(2,1)}) %all-gather.17.cloned.1.call-update) | async-done | bytes 4194320 | tf_op jit(solution)/shard_map/all_gather | solution.py:154
  559.7 11.5 fusion.48
  573.2 12.5 bitcast_convert_fusion
  585.9 11.3 fusion.29
  597.3 35.0 %reduce-scatter.10.cloned.1.call-done = bf16[128,2048]{1,0:T(8,128)(2,1)} async-done(((bf16[1024,2048]{1,0:T(8,128)(2,1)}), bf16[128,2048]{1,0:T(8,128)(2,1)}) %reduce-scatter.10.cloned.1.call-update) | async-done | bytes 524304 | tf_op jit(solution)/shard_map/reduce_scatter | solution.py:160
  633.7 49.1 %reduce-scatter.8.cloned.1.call-done = bf16[128,2048]{1,0:T(8,128)(2,1)} async-done(((bf16[1024,2048]{1,0:T(8,128)(2,1)}), bf16[128,2048]{1,0:T(8,128)(2,1)}) %reduce-scatter.8.cloned.1.call-update) | async-done | bytes 524304 | tf_op jit(solution)/shard_map/reduce_scatter | solution.py:148
  682.8 2.5 fusion.66
  685.3 6.3 fusion.43
  691.9 7.3 multiply_reduce_fusion
  699.2 2.7 multiply_convert_fusion
  706.0 4.0 copy.67
  710.1 7.3 convolution_convert_fusion.1
  717.3 4.0 copy.54
  721.7 5.7 convert_bitcast_fusion.1
  729.0 18.4 %reduce-scatter.16.cloned.1.call-done = bf16[128,2048]{1,0:T(8,128)(2,1)} async-done(((bf16[512,2048]{1,0:T(8,128)(2,1)}), bf16[128,2048]{1,0:T(8,128)(2,1)}) %reduce-scatter.16.cloned.1.call-update) | async-done | bytes 524304
  749.6 36.1 %reduce-scatter.12.cloned.1.call-done = bf16[128,2048]{1,0:T(8,128)(2,1)} async-done(((bf16[512,2048]{1,0:T(8,128)(2,1)}), bf16[128,2048]{1,0:T(8,128)(2,1)}) %reduce-scatter.12.cloned.1.call-update) | async-done | bytes 524304 | tf_op jit(solution)/shard_map/reduce_scatter | solution.py:217
  785.8 13.5 convolution_convert_fusion
  799.3 23.0 %pad_maximum_fusion = bf16[2048,4,2048]{2,0,1:T(8,128)(2,1)} fusion(bf16[2048,1,2048]{2,0,1:T(8,128)(2,1)} %convert_bitcast_fusion.1, bf16[2048,3,2048]{2,0,1:T(8,128)(2,1)} %convolution_convert_fusion), kind=kLoop, calls=%fused_computation.2 | loop fusion | flops 16777216 | bytes 67108864 | tf_op jit(solution)/shard_map/concatenate | solution.py:241
  822.7 9.4 convert_bitcast_fusion.2
  832.2 10.5 convert_bitcast_fusion
  842.7 5.2 pad_maximum_fusion.1
  848.0 297.2 %reduce-scatter.14.cloned.1.call-done = bf16[256,4,2048]{2,0,1:T(8,128)(2,1)} async-done(((bf16[2048,4,2048]{2,0,1:T(8,128)(2,1)}), bf16[256,4,2048]{2,0,1:T(8,128)(2,1)}) %reduce-scatter.14.cloned.1.call-update) | async-done | bytes 4194320 | tf_op jit(solution)/shard_map/reduce_scatter | solution.py:240
  1146.2 13.9 fusion.72
  1160.1 44.1 %all-reduce = (f32[2048]{0:T(1024)S(1)}, f32[2048]{0:T(1024)S(1)}) all-reduce(f32[2048]{0:T(1024)S(1)} %get-tuple-element.130, f32[2048]{0:T(1024)S(1)} %get-tuple-element.128), channel_id=1, replica_groups=mesh['seq'=4,'fsdp'=8] {'seq','fsdp'}, use_global_device_ids=true, to_apply=%region_12.13 | all-reduce | flops 4096 | bytes 32768 | tf_op jit(solution)/shard_map/psum | solution.py:250
  1205.5 2.4 fusion.81
  1207.9 253.1 %all-reduce.4.cloned.1.call-done = (bf16[256,4,2048]{2,0,1:T(8,128)(2,1)}, bf16[1024,3,2048]{0,2,1:T(8,128)(2,1)}) async-done(((bf16[256,4,2048]{2,0,1:T(8,128)(2,1)}, bf16[1024,3,2048]{0,2,1:T(8,128)(2,1)}), (bf16[256,4,2048]{2,0,1:T(8,128)(2,1)}, bf16[1024,3,2048]{0,2,1:T(8,128)(2,1)})) %all-reduce.4.cloned.1.call-update) | async-done | bytes 16777232 | tf_op jit(solution)/shard_map/psum | solution.py:247
  1461.0 8.8 copy.60
  1469.8 18.2 %copy.61 = f32[1024,3,2048]{2,0,1:T(8,128)} copy(bf16[1024,3,2048]{0,2,1:T(8,128)(2,1)} %get-tuple-element.149) | data formatting | bytes 37748736
  (119 shorter events, 24.9 us)
Async XLA Ops:
  7.2 371.2 %copy-start = (s32[1,512]{1,0:T(1,128)S(1)}, s32[1,512]{1,0:T(1,128)}, u32[]{:S(2)}) copy-start(s32[1,512]{1,0:T(1,128)} %param.15) | copy-start | bytes 6148
  7.2 293.5 %all-gather.9.cloned.1.call-start = ((), (), s32[]{:S(2)}) async-start(), calls=%async_computation.5 | async-start | bytes 37748736 | tf_op jit(solution)/shard_map/all_gather | solution.py:64
  13.7 0.7 copy-start.15
  13.7 1.0 copy-start.17
  13.7 10.1 copy-start.5
  13.8 399.7 %all-gather.13.cloned.1.call-start = ((), (), s32[]{:S(2)}) async-start(), calls=%async_computation.7 | async-start | bytes 2621440 | tf_op jit(solution)/shard_map/all_gather | solution.py:84
  370.9 7.4 copy-start.18
  376.8 74.4 %all-gather.11.cloned.1.call-start = ((), (), s32[]{:S(2)}) async-start(), calls=%async_computation.6 | async-start | bytes 2621440 | tf_op jit(solution)/shard_map/all_gather | solution.py:85
  377.8 134.6 %all-gather.15.cloned.1.call-start = ((), (), s32[]{:S(2)}) async-start(), calls=%async_computation.8 | async-start | bytes 4718592 | tf_op jit(solution)/shard_map/all_gather | solution.py:140
  416.8 3.4 copy-start.2
  454.1 6.6 copy-start.10
  454.1 6.6 copy-start.6
  460.6 5.0 copy-start.11
  466.6 93.1 %all-gather.17.cloned.1.call-start = ((), (), s32[]{:S(2)}) async-start(), calls=%async_computation.13 | async-start | bytes 4718592 | tf_op jit(solution)/shard_map/all_gather | solution.py:154
  467.2 165.1 %reduce-scatter.10.cloned.1.call-start = ((), (), s32[]{:S(2)}) async-start(), calls=%async_computation.10 | async-start | bytes 4718592 | tf_op jit(solution)/shard_map/reduce_scatter | solution.py:160
  571.2 1.3 copy-start.19
  571.2 2.0 copy-start.21
  585.7 97.1 %reduce-scatter.8.cloned.1.call-start = ((), (), s32[]{:S(2)}) async-start(), calls=%async_computation.9 | async-start | bytes 4718592 | tf_op jit(solution)/shard_map/reduce_scatter | solution.py:148
  597.2 85.6 %copy-start.9 = (bf16[1,128,2048]{2,1,0:T(8,128)(2,1)S(1)}, bf16[1,128,2048]{2,1,0:T(8,128)(2,1)}, u32[]{:S(2)}) copy-start(bf16[1,128,2048]{2,1,0:T(8,128)(2,1)} %param.13) | copy-start | bytes 1572868
  597.2 150.1 %reduce-scatter.16.cloned.1.call-start = ((), (), s32[]{:S(2)}) async-start(), calls=%async_computation.14 | async-start | bytes 2621440
  691.8 7.3 slice-start
  691.9 7.3 slice-start.1
  699.2 4.8 copy-start.8
  702.0 2.0 copy-start.3
  710.0 75.8 %reduce-scatter.12.cloned.1.call-start = ((), (), s32[]{:S(2)}) async-start(), calls=%async_computation.11 | async-start | bytes 2621440 | tf_op jit(solution)/shard_map/reduce_scatter | solution.py:217
  717.3 4.3 copy-start.12
  721.4 423.8 %reduce-scatter.14.cloned.1.call-start = ((), (), s32[]{:S(2)}) async-start(), calls=%async_computation.12 | async-start | bytes 37748736 | tf_op jit(solution)/shard_map/reduce_scatter | solution.py:240
  721.7 5.8 copy-start.4
  721.7 5.7 copy-start.7
  727.4 21.3 %copy-start.14 = (f32[128,32]{0,1:T(8,128)S(1)}, f32[128,32]{0,1:T(8,128)}, u32[]{:S(2)}) copy-start(f32[128,32]{0,1:T(8,128)} %get-tuple-element.182) | copy-start | bytes 49156
  822.4 638.6 %all-reduce.4.cloned.1.call-start = ((), (), s32[]{:S(2)}) async-start(), calls=%async_computation.15 | async-start | bytes 33554432 | tf_op jit(solution)/shard_map/psum | solution.py:247
  822.7 9.5 copy-start.16
  822.7 9.5 copy-start.20
  822.7 9.5 copy-start.22
  1145.2 1.0 copy-start.13
  1469.8 18.2 %copy-start.1 = (s32[1,512]{1,0:T(1,128)S(1)}, s32[1,512]{1,0:T(1,128)}, u32[]{:S(2)}) copy-start(s32[1,512]{1,0:T(1,128)} %param.15) | copy-start | bytes 6148
Sparse Core Ops, SparseCore 0:
  13.9 286.7 all-gather.8
  377.0 36.4 all-gather.12
  415.8 35.3 all-gather.10
  466.7 45.5 all-gather.14
  513.8 45.8 all-gather.16
  585.8 46.4 reduce-scatter.9
  634.6 48.1 reduce-scatter.7
  710.1 37.1 reduce-scatter.15
  750.6 35.1 reduce-scatter.11
  822.5 322.6 reduce-scatter.13
  1150.0 310.8 all-reduce.3
where the time goes:
time: 1510 us; the launch traced here: 1490 us
  waiting for transfers between devices  1090 us (72%)
  matrix products  156 us (10%)
  local copies, waits for them, and re-layouts  120 us (8%)
  blocking collectives  65.3 us (4%)
  other arithmetic  46.1 us (3%)
    reduce_scatter x1, waiting for transfers between devices, on_device(): lax.psum_scatter(jnp.concatenate([proj_grad, out_proj_grad[:, None]], 1)....  297 us
    all_gather x1, waiting for transfers between devices, on_device(): lax.all_gather(attn_weights, 'fsdp', axis=0, tiled=True)  276 us
    psum x1, waiting for transfers between devices, on_device(): lax.psum(attn_grad.astype(jnp.bfloat16), 'seq').astype(jnp.float32)  253 us
    slice x2, local copies, waits for them, and re-layouts, on_device(): attn_full[:, :3, :].reshape(model_width, 3 * model_width)  52.8 us
    reduce_scatter x1, waiting for transfers between devices, on_device(): lax.psum_scatter(jnp.dot(act_local, down_local, preferred_element_type=jn...  49.1 us
    unnamed x57, local copies, waits for them, and re-layouts  45.3 us
    all_gather x1, waiting for transfers between devices, on_device(): tok_all = lax.all_gather(normed_m, 'fsdp', axis=0, tiled=True)  44.7 us
    psum x1, blocking collectives, on_device(): lax.psum((gain_a_term, gain_m_term), ('seq', 'fsdp'))  44.1 us
  transfers between devices with their start and end apart: 11, of which 11 were waited for; matrix products, arithmetic and copies ran while one was open for 7% of the time, Pallas kernels for 0%

commit v1 on v0

v1 whole, which is shorter than its diff:
```python
import functools

import jax
import jax.numpy as jnp
from jax import lax
from jax.experimental import pallas as pl
from jax.experimental.pallas import tpu as pltpu
from jax.sharding import PartitionSpec as P

HEAD = 64


NORM_EPS = 1e-05
ROPE_BASE = 130000.0
MASKED_OUT = -1e30
F32 = jnp.float32
BF16 = jnp.bfloat16
MESH = pl.DeviceIdType.MESH
DMA = pltpu.SemaphoreType.DMA
ANY = pl.BlockSpec(memory_space=pl.ANY)
VMEM = pl.BlockSpec(memory_space=pltpu.VMEM)


def send(src, dst, send_sem, recv_sem, device):
    return pltpu.make_async_remote_copy(
        src_ref=src,
        dst_ref=dst,
        send_sem=send_sem,
        recv_sem=recv_sem,
        device_id=device,
        device_id_type=MESH,
    )


class Place:
    def __init__(self, n_seq, n_fsdp):
        self.n_seq, self.line = n_seq, n_fsdp // 2
        self.s = lax.axis_index("seq")
        self.f = lax.axis_index("fsdp")
        self.r = lax.div(self.f, 2)
        self.c = lax.rem(self.f, 2)
        self.up = (self.s, self.f + 2)
        self.down = (self.s, self.f - 2)
        self.sister = (self.s, 2 * self.r + 1 - self.c)

    def peer(self, d):
        return (jnp.bitwise_xor(self.s, d), self.f)

    def greet(self):
        barrier = pltpu.get_barrier_semaphore()
        wrap = 2 * self.line
        partners = [
            (self.s, lax.rem(self.f + 2, wrap)),
            (self.s, lax.rem(self.f + wrap - 2, wrap)),
            self.sister,
        ]
        partners += [self.peer(d) for d in range(1, self.n_seq)]
        for partner in partners:
            pl.semaphore_signal(barrier, inc=1, device_id=partner, device_id_type=MESH)
        pl.semaphore_wait(barrier, len(partners))


class GatherLine:
    def __init__(self, x, n_seq, n_fsdp, parts=1):
        line = n_fsdp // 2
        self.args, self.in_specs = [x], [ANY]
        self.outs = [jax.ShapeDtypeStruct((n_fsdp,) + x.shape, x.dtype)]
        self.out_specs = [ANY]
        self.scratch = [DMA((line, parts)) for _ in range(5)] + [DMA((1,))]
        self.parts = parts

    def steps(self, at, refs):
        x, o, line_r, sis_r, up_s, down_s, sis_s, own_s = refs
        parts, line, r, c = self.parts, at.line, at.r, at.c
        rows = x.shape[0] // parts

        def cut(ref, k):
            return ref.at[pl.ds(k * rows, rows)]

        def go_up(src, b, k):
            return send(src, cut(o.at[2 * b + c], k), up_s.at[b, k], line_r.at[b, k], at.up)

        def go_down(src, b, k):
            return send(src, cut(o.at[2 * b + c], k), down_s.at[b, k], line_r.at[b, k], at.down)

        def go_sister(src, b, k):
            return send(src, cut(o.at[2 * b + c], k), sis_s.at[b, k], sis_r.at[b, k], at.sister)

        own = pltpu.make_async_copy(x, o.at[at.f], own_s.at[0])
        own.start()
        for k in range(parts):
            src = cut(x, k)
            pl.when(r < line - 1)(lambda: go_up(src, r, k).start())
            pl.when(r > 0)(lambda: go_down(src, r, k).start())
            go_sister(src, r, k).start()
        yield
        for t in range(1, line):
            for k in range(parts):
                low, high = r - t, r + t

                @pl.when(low >= 0)
                def _():
                    src = cut(o.at[2 * low + c], k)
                    go_up(src, low, k).wait_recv()
                    pl.when(r < line - 1)(lambda: go_up(src, low, k).start())
                    go_sister(src, low, k).start()

                @pl.when(high < line)
                def _():
                    src = cut(o.at[2 * high + c], k)
                    go_down(src, high, k).wait_recv()
                    pl.when(r > 0)(lambda: go_down(src, high, k).start())
                    go_sister(src, high, k).start()

            yield
        for b in range(line):
            for k in range(parts):
                src = cut(o.at[2 * b + 1 - c], k)
                send(src, src, sis_s.at[b, k], sis_r.at[b, k], at.sister).wait_recv()
                src = cut(x, k)
                go_sister(src, b, k).wait_send()
                pl.when((b <= r) & (r < line - 1))(lambda: go_up(src, b, k).wait_send())
                pl.when((b >= r) & (r > 0))(lambda: go_down(src, b, k).wait_send())
        own.wait()


class ScatterLine:
    def __init__(self, part, n_seq, n_fsdp, parts=1, out_dtype=F32):
        line = n_fsdp // 2
        block = part.shape[1:]
        self.args, self.in_specs = [part], [VMEM]
        self.outs = [jax.ShapeDtypeStruct(block, out_dtype)]
        self.out_specs = [VMEM]
        self.scratch = [
            pltpu.VMEM((line,) + block, part.dtype),
            pltpu.VMEM((line + 1,) + block, part.dtype),
        ]
        self.scratch += [DMA((line, parts)), DMA((line, parts)), DMA((line, parts))]
        self.scratch += [DMA((line + 1, parts))]
        self.parts = parts

    def steps(self, at, refs):
        part, o, sis, come, sis_s, sis_r, line_s, line_r = refs
        parts, line, r, c = self.parts, at.line, at.r, at.c
        rows = part.shape[1] // parts
        tile = 16 if rows % 16 == 0 else rows

        def cut(ref, k):
            return ref.at[pl.ds(k * rows, rows)]

        def to_sister(b, k):
            return send(
                cut(part.at[2 * b + 1 - c], k),
                cut(sis.at[b], k),
                sis_s.at[b, k],
                sis_r.at[b, k],
                at.sister,
            )

        def slot(b, own):
            return jnp.where(b == own, line, b)

        def go_up(b, k):
            return send(cut(sis.at[b], k), cut(come.at[b], k), line_s.at[b, k], line_r.at[b, k], at.up)

        def go_down(b, k, own):
            i = slot(b, own)
            return send(
                cut(sis.at[b], k), cut(come.at[i], k), line_s.at[b, k], line_r.at[i, k], at.down
            )

        def add(b, k, came, out=None):
            def body(i, carry):
                at_rows = pl.ds(k * rows + i * tile, tile)
                total = part[2 * b + c, at_rows].astype(F32) + sis[b, at_rows].astype(F32)
                for j in came:
                    total = total + come[j, at_rows].astype(F32)
                if out is None:
                    sis[b, at_rows] = total.astype(sis.dtype)
                else:
                    out[at_rows] = total.astype(out.dtype)
                return carry

            lax.fori_loop(0, rows // tile, body, 0)

        order = []
        for j in range(line):
            order += [b for b in (line - 1 - j, j) if b not in order]
        for b in order:
            for k in range(parts):
                to_sister(b, k).start()
        yield
        for j in range(line - 1):
            for k in range(parts):
                b = line - 1 - j

                @pl.when(b > r)
                def _():
                    to_sister(b, k).wait_recv()

                    @pl.when(r > 0)
                    def _():
                        go_up(b, k).wait_recv()
                        add(b, k, [b])

                    pl.when(r == 0)(lambda: add(b, k, []))
                    go_up(b, k).start()

                @pl.when(j < r)
                def _():
                    to_sister(j, k).wait_recv()

                    @pl.when(r < line - 1)
                    def _():
                        go_down(j, k, -1).wait_recv()
                        add(j, k, [j])

                    pl.when(r == line - 1)(lambda: add(j, k, []))
                    go_down(j, k, r - 1).start()

            yield
        for k in range(parts):
            to_sister(r, k).wait_recv()
            pl.when(r > 0)(lambda: go_up(r, k).wait_recv())
            pl.when(r < line - 1)(lambda: go_down(r, k, r).wait_recv())
            pl.when(r == 0)(lambda: add(r, k, [line], o))
            pl.when(r == line - 1)(lambda: add(r, k, [r], o))
            pl.when((r > 0) & (r < line - 1))(lambda: add(r, k, [r, line], o))
        yield
        for b in range(line):
            for k in range(parts):
                to_sister(b, k).wait_send()
                pl.when(b != r)(lambda: go_up(b, k).wait_send())


class GatherSeq:
    def __init__(self, x, n_seq, n_fsdp):
        self.args, self.in_specs = [x], [ANY]
        self.outs = [jax.ShapeDtypeStruct((n_seq,) + x.shape, x.dtype)]
        self.out_specs = [ANY]
        self.scratch = [DMA((n_seq,)), DMA((n_seq,))]

    def steps(self, at, refs):
        x, o, s_sem, r_sem = refs

        def go(d):
            return send(x, o.at[at.s], s_sem.at[d], r_sem.at[d], at.peer(d))

        for d in reversed(range(1, at.n_seq)):
            go(d).start()
        own = pltpu.make_async_copy(x, o.at[at.s], s_sem.at[0])
        own.start()
        yield
        own.wait()
        for d in range(1, at.n_seq):
            go(d).wait()


class SwapSeq:
    def __init__(self, x, n_seq, n_fsdp):
        self.args, self.in_specs = [x], [ANY]
        self.outs = [jax.ShapeDtypeStruct(x.shape, x.dtype)]
        self.out_specs = [ANY]
        self.scratch = [DMA((n_seq,)), DMA((n_seq,))]

    def steps(self, at, refs):
        x, o, s_sem, r_sem = refs

        def go(d):
            peer = at.peer(d)
            return send(x.at[peer[0]], o.at[at.s], s_sem.at[d], r_sem.at[d], peer)

        for d in reversed(range(1, at.n_seq)):
            go(d).start()
        own = pltpu.make_async_copy(x.at[at.s], o.at[at.s], s_sem.at[0])
        own.start()
        yield
        own.wait()
        for d in range(1, at.n_seq):
            go(d).wait()


class ScatterSeq:
    def __init__(self, part, n_seq, n_fsdp, out_dtype=F32):
        block = part.shape[1:]
        self.args, self.in_specs = [part], [VMEM]
        self.outs = [jax.ShapeDtypeStruct(block, out_dtype)]
        self.out_specs = [VMEM]
        self.scratch = [pltpu.VMEM((n_seq,) + block, part.dtype), DMA((n_seq,)), DMA((n_seq,))]

    def steps(self, at, refs):
        part, o, land, s_sem, r_sem = refs
        rows = part.shape[1]
        tile = 16 if rows % 16 == 0 else rows

        def go(d):
            peer = at.peer(d)
            return send(part.at[peer[0]], land.at[d], s_sem.at[d], r_sem.at[d], peer)

        for d in reversed(range(1, at.n_seq)):
            go(d).start()
        yield
        for d in range(1, at.n_seq):
            go(d).wait()

        def body(i, carry):
            at_rows = pl.ds(i * tile, tile)
            total = part[at.s, at_rows].astype(F32)
            for d in range(1, at.n_seq):
                total = total + land[d, at_rows].astype(F32)
            o[at_rows] = total.astype(o.dtype)
            return carry

        lax.fori_loop(0, rows // tile, body, 0)


def transfer(name, collective_id, n_seq, n_fsdp, *ops):
    n_in = [len(op.args) for op in ops]
    n_out = [len(op.outs) for op in ops]
    n_scratch = [len(op.scratch) for op in ops]

    def kernel(*refs):
        at = Place(n_seq, n_fsdp)
        at.greet()
        first_out = sum(n_in)
        first_scratch = first_out + sum(n_out)
        running = []
        for i, op in enumerate(ops):
            mine = []
            for base, count in ((0, n_in), (first_out, n_out), (first_scratch, n_scratch)):
                start = base + sum(count[:i])
                mine += refs[start : start + count[i]]
            running.append(op.steps(at, mine))
        while running:
            for one in list(running):
                if next(one, "end") == "end":
                    running.remove(one)

    return pl.pallas_call(
        kernel,
        out_shape=[o for op in ops for o in op.outs],
        in_specs=[s for op in ops for s in op.in_specs],
        out_specs=[s for op in ops for s in op.out_specs],
        scratch_shapes=[s for op in ops for s in op.scratch],
        compiler_params=pltpu.CompilerParams(
            collective_id=collective_id, has_side_effects=True, vmem_limit_bytes=48 * 2**20
        ),
        name=name,
    )(*[a for op in ops for a in op.args])


def angles(positions):
    freqs = ROPE_BASE ** (-jnp.arange(0, HEAD, 2).astype(jnp.float32) / HEAD)
    turn = positions.astype(jnp.float32)[:, None] * freqs[None, :]
    return (jnp.cos(turn)[:, None, :], jnp.sin(turn)[:, None, :])


def rotate(field, cosine, sine):
    half = field.shape[-1] // 2
    front = field[..., :half]
    back_half = field[..., half:]
    return jnp.concatenate(
        [front * cosine - back_half * sine, back_half * cosine + front * sine], -1
    )


def norm_back(grad_normed, value, scale, gain):
    weighted = grad_normed * gain
    inner_mean = jnp.mean(weighted * value, axis=-1, keepdims=True)
    return scale * (weighted - value * scale * scale * inner_mean)


def scale_of(value):
    return lax.rsqrt(jnp.mean(value * value, axis=-1, keepdims=True) + NORM_EPS)


def dot(a, b, dims):
    return lax.dot_general(a, b, (dims, ((), ())), preferred_element_type=F32)


def on_device(
    n_seq, n_fsdp,
    hidden_in, gain_attn, attn_weights, gain_mlp, mlp_weights, out_grad, block_slots, doc_ids,
):
    tok_rows = hidden_in.shape[1]
    model = hidden_in.shape[2]
    length = doc_ids.shape[1]
    share = model // n_seq
    heads = share // HEAD
    block_rows = tok_rows // 2
    seq_index = lax.axis_index("seq")
    within = jnp.arange(block_rows, dtype=jnp.int32)
    pos = (block_slots.reshape(-1)[:, None] * block_rows + within[None, :]).reshape(-1)
    doc = doc_ids[0][pos]
    cosine, sine = angles(pos)
    move = functools.partial

    def run(name, cid, *ops):
        return transfer(name, cid, n_seq, n_fsdp, *[op(n_seq=n_seq, n_fsdp=n_fsdp) for op in ops])

    w_share = lax.dynamic_slice_in_dim(attn_weights, seq_index * share, share, 2)
    own_gains = jnp.concatenate(
        [
            jnp.broadcast_to(gain_attn[None], (16,) + gain_attn.shape),
            jnp.broadcast_to(gain_mlp[None], (16,) + gain_mlp.shape),
        ],
        0,
    )
    w, x_all, gains = run(
        "gather_in",
        1,
        move(GatherLine, w_share.reshape(-1, 4 * share), parts=2),
        move(GatherSeq, hidden_in[0]),
        move(GatherLine, own_gains),
    )
    w = w.reshape(model, 4 * share)
    w_qkv, w_out = w[:, : 3 * share], w[:, 3 * share :]
    x_all = x_all.reshape(length, model)
    gains = gains.astype(F32)
    gain_a, gain_m = gains[:, 0].reshape(model), gains[:, 16].reshape(model)
    late_grad, x_all = lax.optimization_barrier((out_grad[0], x_all))
    grad_all = lax.all_gather(late_grad, "fsdp", axis=0, tiled=True)

    x_wide = x_all.astype(F32)
    n1 = (x_wide * scale_of(x_wide) * gain_a).astype(BF16)
    qkv = dot(n1, w_qkv, ((1,), (0,)))

    def turn(field, s):
        return rotate(field.reshape(length, heads, HEAD), cosine, s).astype(BF16)

    q = turn(qkv[:, :share], sine)
    k = turn(qkv[:, share : 2 * share], sine)
    v = qkv[:, 2 * share :].astype(BF16).reshape(length, heads, HEAD)
    allowed = ((pos[None, :] <= pos[:, None]) & (doc[None, :] == doc[:, None]))[None]
    z = jnp.einsum("qhd,khd->hqk", q, k, preferred_element_type=F32) * 0.125
    z = jnp.where(allowed, z, MASKED_OUT)
    top = jnp.max(z, axis=-1, keepdims=True)
    e = jnp.where(allowed, jnp.exp(z - top), 0.0)
    p = e / jnp.sum(e, axis=-1, keepdims=True)
    p_low = p.astype(BF16)
    o = jnp.einsum("hqk,khd->qhd", p_low, v, preferred_element_type=F32)
    o = o.reshape(length, share).astype(BF16)
    (o_all,) = run("gather_o", 2, move(GatherSeq, o))
    o_all = o_all.transpose(1, 0, 2).reshape(length, model)
    y = dot(o_all, w_out, ((1,), (0,))).astype(BF16)
    (y,) = run("swap_y", 3, move(SwapSeq, y.reshape(n_seq, tok_rows, share)))
    y = y.transpose(1, 0, 2).reshape(tok_rows, model)

    source = hidden_in[0].astype(F32)
    middle = source + y.astype(F32)
    scale_m = scale_of(middle)
    n2 = (middle * scale_m * gain_m).astype(BF16)
    (n2_all,) = run("gather_n2", 4, move(GatherLine, n2, parts=2))
    n2_all = n2_all.reshape(-1, model)
    w_gate, w_up, w_down = mlp_weights[:, 0], mlp_weights[:, 1], mlp_weights[:, 2]
    gate = dot(n2_all, w_gate, ((1,), (1,)))
    up = dot(n2_all, w_up, ((1,), (1,)))
    grad_act = dot(grad_all, w_down, ((1,), (1,)))
    sigma = jax.nn.sigmoid(gate)
    hid = (gate * sigma * up).astype(BF16)
    dg = (grad_act * up * sigma * (1.0 + gate * (1.0 - sigma))).astype(BF16)
    du = (grad_act * gate * sigma).astype(BF16)
    mlp_grad = jnp.stack(
        [
            dot(dg, n2_all, ((0,), (0,))).astype(BF16),
            dot(du, n2_all, ((0,), (0,))).astype(BF16),
            dot(hid, grad_all, ((0,), (0,))).astype(BF16),
        ],
        1,
    )
    mlp_grad = lax.psum(mlp_grad, "seq").astype(F32)

    dn2_part = (dot(dg, w_gate, ((1,), (0,))) + dot(du, w_up, ((1,), (0,)))).astype(BF16)
    (dn2,) = run(
        "scatter_dn2", 5, move(ScatterLine, dn2_part.reshape(n_fsdp, tok_rows, model), parts=2)
    )
    out_part = dot(hid, w_down, ((1,), (0,))).astype(BF16)

    dh1 = out_grad[0].astype(F32) + norm_back(dn2, middle, scale_m, gain_m)
    gain_m_term = jnp.sum(dn2 * middle * scale_m, axis=0)
    da = dh1.astype(BF16)
    (da_cols,) = run(
        "swap_da", 6, move(SwapSeq, da.reshape(tok_rows, n_seq, share).transpose(1, 0, 2))
    )
    da_cols = da_cols.reshape(length, share)
    do_part = dot(da_cols, w_out, ((1,), (1,))).astype(BF16)
    do, mlp_out = run(
        "scatter_do",
        7,
        move(ScatterSeq, do_part.reshape(length, n_seq, share).transpose(1, 0, 2), out_dtype=BF16),
        move(ScatterLine, out_part.reshape(n_fsdp, tok_rows, model), parts=2),
    )
    block_out = (middle + mlp_out).astype(BF16)
    do = do.reshape(length, heads, HEAD)
    dp = jnp.einsum("qhd,khd->hqk", do, v, preferred_element_type=F32)
    delta = jnp.sum(p * dp, axis=-1, keepdims=True)
    dz = (p * (dp - delta)).astype(BF16)
    dq = jnp.einsum("hqk,khd->qhd", dz, k, preferred_element_type=F32) * 0.125
    dk = jnp.einsum("hqk,qhd->khd", dz, q, preferred_element_type=F32) * 0.125
    dv = jnp.einsum("hqk,qhd->khd", p_low, do, preferred_element_type=F32)
    dqkv = jnp.concatenate(
        [
            turn(dq, -sine).reshape(length, share),
            turn(dk, -sine).reshape(length, share),
            dv.reshape(length, share).astype(BF16),
        ],
        1,
    )
    dn1_part = dot(dqkv, w_qkv, ((1,), (1,))).astype(BF16)
    dw_qkv = dot(n1, dqkv, ((0,), (0,))).astype(BF16)
    dw_o = dot(o_all, da_cols, ((0,), (0,))).astype(BF16)
    dw = jnp.concatenate([dw_qkv, dw_o], 1)
    dn1, dw = run(
        "scatter_dw",
        8,
        move(ScatterSeq, dn1_part.reshape(n_seq, tok_rows, model)),
        move(ScatterLine, dw.reshape(n_fsdp, -1, 4 * share), parts=2, out_dtype=BF16),
    )
    scale_a = scale_of(source)
    grad_in = (dh1 + norm_back(dn1, source, scale_a, gain_a)).astype(BF16)
    gain_a_term = jnp.sum(dn1 * source * scale_a, axis=0)
    gain_terms = jnp.stack([gain_a_term, gain_m_term], 0).reshape(2, n_fsdp, -1)
    gain_terms = jnp.pad(gain_terms.transpose(1, 0, 2), ((0, 0), (0, 6), (0, 0)))
    dw, gain_terms = run(
        "gather_dw", 9, move(GatherSeq, dw), move(ScatterLine, gain_terms)
    )
    attn_grad = dw.reshape(n_seq, -1, 4, share).transpose(1, 2, 0, 3).reshape(-1, 4, model)
    attn_grad = attn_grad.astype(F32)
    (gain_terms,) = run("gather_gain", 10, move(GatherSeq, gain_terms))
    gain_terms = jnp.sum(gain_terms, axis=0)
    return (block_out[None], grad_in[None], gain_terms[0], attn_grad, gain_terms[1], mlp_grad)


def solution(mesh):
    return jax.shard_map(
        functools.partial(on_device, mesh.shape["seq"], mesh.shape["fsdp"]),
        mesh=mesh,
        in_specs=(
            P("fsdp", "seq", None),
            P("fsdp"),
            P("fsdp", None, None),
            P("fsdp"),
            P("fsdp", None, None),
            P("fsdp", "seq", None),
            P(),
            P("fsdp", None),
        ),
        out_specs=(
            P("fsdp", "seq", None),
            P("fsdp", "seq", None),
            P("fsdp"),
            P("fsdp", None, None),
            P("fsdp"),
            P("fsdp", None, None),
        ),
        check_vma=False,
    )
```

time: 1510 us -> 738 us (0.49)
  waiting for transfers between devices: 1090 us -> 0.04 us
  Pallas kernels: 0 us -> 483 us
  blocking collectives: 65.3 us -> 0 us
  local copies, waits for them, and re-layouts: 120 us -> 69.1 us
  matrix products: 156 us -> 120 us
    pallas_call x0 -> x10, Pallas kernels: none -> 483 us  [transfer(): pl.pallas_call(kernel, out_shape=[o for op in ops for o in op.outs], in_s...]
    reduce_scatter x4 -> x0, waiting for transfers between devices: 417 us -> none  [the longest x1 297 us: on_device(): lax.psum_scatter(jnp.concatenate([proj_grad, out_proj_grad[:, None]], 1)....]
    all_gather x5 -> x1, waiting for transfers between devices: 402 us -> 0.01 us  [on_device(): grad_all = lax.all_gather(late_grad, 'fsdp', axis=0, tiled=True)]
    psum x1, waiting for transfers between devices: 253 us -> 0.01 us  [on_device(): mlp_grad = lax.psum(mlp_grad, 'seq').astype(F32)]
    slice x6 -> x7, local copies, waits for them, and re-layouts: 60.2 us -> 8.43 us  [the longest x2 3.36 us: on_device(): q = turn(qkv[:, :share], sine)]
    psum x1 -> x0, blocking collectives: 44.1 us -> none  [on_device(): lax.psum((gain_a_term, gain_m_term), ('seq', 'fsdp'))]
    dot_general x18 -> x20, matrix products: 156 us -> 112 us  [the longest x15 99 us: dot(): return lax.dot_general(a, b, (dims, ((), ())), preferred_element_type=F32)]
    unnamed x57 -> x111, local copies, waits for them, and re-layouts: 45.3 us -> 12 us
  transfers between devices with their start and end apart: 11 -> 2, of which waited for: 11 -> 0; matrix products, arithmetic and copies ran while one was open for 7% -> 21% of each run, Pallas kernels for 0% -> 57%
where the time goes in v1:
time: 738 us; the launch traced here: 725 us
  Pallas kernels  483 us (65%)
  matrix products  120 us (16%)
  local copies, waits for them, and re-layouts  69.1 us (9%)
  other arithmetic  38 us (5%)
  between operations  15.4 us (2%)
    pallas_call x10, Pallas kernels, transfer(): pl.pallas_call(kernel, out_shape=[o for op in ops for o in op.outs], in_s...  483 us
    dot_general x15, matrix products, dot(): return lax.dot_general(a, b, (dims, ((), ())), preferred_element_type=F32)  99 us
    convert_element_type x2, local copies, waits for them, and re-layouts, on_device(): attn_grad = attn_grad.astype(F32)  20.2 us
  transfers between devices with their start and end apart: 2, of which 0 were waited for; matrix products, arithmetic and copies ran while one was open for 21% of the time, Pallas kernels for 57%

profile of v1, /device:TPU:8, one launch (start us, length us, event | category | flops | bytes accessed | tf_op | source)
XLA Modules:
  0.0 725.4 jit_solution(8599659863217587245)
XLA Ops:
  7.3 1.6 constant_dynamic-slice_fusion
  9.3 71.6 %gather_in.1 = (bf16[8,256,2048]{2,1,0:T(8,128)(2,1)}, bf16[4,128,2048]{2,1,0:T(8,128)(2,1)S(1)}, bf16[8,32,256]{2,1,0:T(8,128)(2,1)S(1)}) custom-call(bf16[256,2048]{1,0:T(8,128)(2,1)S(1)} %bitcast.130, bf16[128,2048]{1,0:T(8,128)(2,1)S(1)} %bitcast.123, bf16[32,256]{1,0:T(8,128)(2,1)S(1)} %pad_maximum_fusion.21.refs_2_), custom_call_target="tpu_custom_call" | custom-call | tf_op jit(solution)/shard_map/gather_in/pallas_call | solution.py:339
  81.9 5.6 fusion.4
  87.5 1.7 copy-done.19
  90.0 2.1 copy.32
  92.1 3.0 fusion.85
  95.5 1.6 copy.35
  97.1 3.5 gather_fusion
  103.0 8.3 %fusion.88 = (f32[8,512]{1,0:T(8,128)S(1)}, f32[8,512,512]{1,2,0:T(8,128)}) fusion(pred[512,512]{0,1:T(8,128)(4,1)} %compare_and_fusion, bf16[512,8,32]{0,2,1:T(8,128)(2,1)} %get-tuple-element.54, bf16[512,8,32]{0,2,1:T(8,128)(2,1)} %get-tuple-element.55, bf16[512,8,32]{0,2,1:T(8,128)(2,1)S(1)} %get-tuple-element.44, ...), kind=kOutput, calls=%fused_computation.137 | convolution fusion | flops 281018880 | bytes 9715712 | tf_op jit(solution)/shard_map/sub | solution.py:438
  111.4 4.3 fusion.50
  117.8 28.0 %gather_o.1 = bf16[4,512,512]{2,1,0:T(8,128)(2,1)S(1)} custom-call(bf16[512,512]{1,0:T(8,128)(2,1)S(1)} %copy-done.7), custom_call_target="tpu_custom_call" | custom-call | tf_op jit(solution)/shard_map/gather_o/pallas_call | solution.py:339
  145.8 2.4 copy.38
  148.2 3.5 fusion.47
  151.7 10.5 %swap_y.1 = bf16[4,128,512]{2,1,0:T(8,128)(2,1)S(1)} custom-call(bf16[4,128,512]{2,1,0:T(8,128)(2,1)S(1)} %bitcast.138), custom_call_target="tpu_custom_call" | custom-call | tf_op jit(solution)/shard_map/swap_y/pallas_call | solution.py:339
  163.5 35.7 %gather_n2.1 = bf16[8,128,2048]{2,1,0:T(8,128)(2,1)S(1)} custom-call(bf16[128,2048]{1,0:T(8,128)(2,1)S(1)} %multiply_convert_fusion.4.refs_0_), custom_call_target="tpu_custom_call" | custom-call | tf_op jit(solution)/shard_map/gather_n2/pallas_call | solution.py:339
  199.2 2.0 copy-done.5
  201.3 8.5 %fusion.11 = f32[1024,1024]{1,0:T(8,128)} fusion(bf16[1024,2048]{1,0:T(8,128)(2,1)S(1)} %bitcast.126, bf16[1024,3,2048]{2,0,1:T(8,128)(2,1)} %param.12), kind=kOutput, calls=%fused_computation.22 | convolution fusion | flops 4294967296 | bytes 12582912 | tf_op jit(solution)/shard_map/dot_general | solution.py:378
  209.8 7.7 %fusion.19 = f32[1024,1024]{1,0:T(8,128)S(1)} fusion(bf16[1024,2048]{1,0:T(8,128)(2,1)} %all-gather.2.cloned.1.call-done, bf16[1024,3,2048]{2,0,1:T(8,128)(2,1)} %param.12), kind=kOutput, calls=%fused_computation.30 | convolution fusion | flops 4294967296 | bytes 12582912 | tf_op jit(solution)/shard_map/dot_general | solution.py:378
  217.5 8.0 %multiply_convert_fusion.1 = (bf16[1024,1024]{1,0:T(8,128)(2,1)S(1)}, bf16[1024,1024]{1,0:T(8,128)(2,1)S(1)}, bf16[1024,1024]{1,0:T(8,128)(2,1)S(1)}) fusion(f32[1024,1024]{1,0:T(8,128)S(1)} %copy-done.52, f32[1024,1024]{1,0:T(8,128)S(1)} %fusion.19, bf16[1024,2048]{1,0:T(8,128)(2,1)S(1)} %bitcast.127, bf16[1024,3,2048]{2,0,1:T(8,128)(2,1)} %param.12), kind=kOutput, calls=%fused_computation.35 | convolution fusion | flops 4311744512 | bytes 23068672 | tf_op jit(solution)/shard_map/dot_general | solution.py:378
  225.5 4.8 convert_bitcast_fusion.1
  230.4 4.8 convert_bitcast_fusion.2
  235.2 15.7 %convert_bitcast_fusion = bf16[1024,1,2048]{2,0,1:T(8,128)(2,1)S(1)} fusion(bf16[1024,1024]{1,0:T(8,128)(2,1)S(1)} %get-tuple-element.34, bf16[1024,2048]{1,0:T(8,128)(2,1)S(1)} %copy-done.45), kind=kOutput, calls=%fused_computation.32 | convolution fusion | flops 4297064448 | bytes 10485760 | tf_op jit(solution)/shard_map/dot_general | solution.py:378
  250.9 5.4 pad_maximum_fusion
  256.3 7.1 fusion.9
  263.4 7.7 %add_convert_fusion = bf16[1024,2048]{1,0:T(8,128)(2,1)S(1)} fusion(f32[1024,2048]{1,0:T(8,128)S(1)} %fusion.9, bf16[1024,1024]{1,0:T(8,128)(2,1)S(1)} %copy-done.50, bf16[1024,3,2048]{2,0,1:T(8,128)(2,1)} %param.12), kind=kOutput, calls=%fused_computation.6 | convolution fusion | flops 4299161600 | bytes 18874368 | tf_op jit(solution)/shard_map/dot_general | solution.py:378
  271.1 51.6 %scatter_dn2.1 = f32[128,2048]{1,0:T(8,128)S(1)} custom-call(bf16[8,128,2048]{2,1,0:T(8,128)(2,1)S(1)} %bitcast.125), custom_call_target="tpu_custom_call" | custom-call | tf_op jit(solution)/shard_map/scatter_dn2/pallas_call | solution.py:339
  324.1 14.7 %swap_da.1 = bf16[4,128,512]{2,1,0:T(8,128)(2,1)S(1)} custom-call(bf16[4,128,512]{2,1,0:T(8,128)(2,1)S(1)} %bitcast.135), custom_call_target="tpu_custom_call" | custom-call | tf_op jit(solution)/shard_map/swap_da/pallas_call | solution.py:339
  339.6 3.0 convolution_convert_fusion.2
  342.5 2.5 copy.41
  345.1 2.9 copy.42
  348.0 9.3 %fusion.24 = bf16[1024,2048]{1,0:T(8,128)(2,1)} fusion(bf16[1024,1024]{1,0:T(8,128)(2,1)} %copy-done.48, bf16[1024,3,2048]{2,0,1:T(8,128)(2,1)} %param.12), kind=kOutput, calls=%fused_computation.43 | convolution fusion | flops 4297064448 | bytes 10485760 | tf_op jit(solution)/shard_map/dot_general | solution.py:378
  357.4 87.5 %scatter_do.1 = (bf16[512,512]{1,0:T(8,128)(2,1)S(1)}, f32[128,2048]{1,0:T(8,128)S(1)}) custom-call(bf16[4,512,512]{2,1,0:T(8,128)(2,1)S(1)} %bitcast.122, bf16[8,128,2048]{2,1,0:T(8,128)(2,1)} %bitcast.149), custom_call_target="tpu_custom_call" | custom-call | tf_op jit(solution)/shard_map/scatter_do/pallas_call | solution.py:339
  448.0 4.9 multiply_reduce_fusion
  454.1 2.7 multiply_convert_fusion
  457.9 1.4 fusion.45
  461.2 1.4 fusion.53
  463.4 5.7 convolution_convert_fusion
  469.1 7.8 %pad_maximum_fusion.1 = bf16[2048,2048]{0,1:T(8,128)(2,1)} fusion(bf16[2048,512]{0,1:T(8,128)(2,1)S(1)} %convolution_convert_fusion.1, bf16[2048,1536]{0,1:T(8,128)(2,1)} %convolution_convert_fusion), kind=kLoop, calls=%fused_computation.3 | loop fusion | flops 16777216 | bytes 16777216 | tf_op jit(solution)/shard_map/concatenate | solution.py:512
  476.9 12.6 %copy.47 = bf16[2048,2048]{1,0:T(8,128)(2,1)} copy(bf16[2048,2048]{0,1:T(8,128)(2,1)} %pad_maximum_fusion.1) | data formatting | bytes 16777216 | tf_op jit(solution)/shard_map/concatenate | solution.py:512
  489.5 6.3 fusion.35
  495.9 120.7 %scatter_dw.1 = (f32[128,2048]{1,0:T(8,128)S(1)}, bf16[256,2048]{1,0:T(8,128)(2,1)S(1)}) custom-call(bf16[4,128,2048]{2,1,0:T(8,128)(2,1)S(1)} %bitcast.131, bf16[8,256,2048]{2,1,0:T(8,128)(2,1)} %bitcast.139), custom_call_target="tpu_custom_call" | custom-call | tf_op jit(solution)/shard_map/scatter_dw/pallas_call | solution.py:339
  617.0 56.9 %gather_dw.1 = (bf16[4,256,2048]{2,1,0:T(8,128)(2,1)S(1)}, f32[8,256]{1,0:T(8,128)S(1)}) custom-call(bf16[256,2048]{1,0:T(8,128)(2,1)S(1)} %get-tuple-element.25.refs_0_, f32[8,8,256]{2,1,0:T(8,128)S(1)} %pad.4.refs_1_), custom_call_target="tpu_custom_call" | custom-call | tf_op jit(solution)/shard_map/gather_dw/pallas_call | solution.py:339
  673.9 2.0 copy-done.4
  675.9 5.3 gather_gain.1
  681.3 10.6 %reshape.349 = f32[4,256,4,512]{3,2,1,0:T(4,128)} reshape(bf16[4,256,2048]{2,1,0:T(8,128)(2,1)} %copy-done.4) | data formatting | bytes 12582912 | tf_op jit(solution)/shard_map/convert_element_type | solution.py:528
  691.9 9.6 %copy.55 = f32[4,256,1,4,512]{4,3,0,2,1:T(4,128)} copy(f32[4,256,1,4,512]{4,3,2,1,0:T(4,128)} %bitcast.140) | data formatting | bytes 16777216 | tf_op jit(solution)/shard_map/convert_element_type | solution.py:528
  702.1 1.6 fusion.71
  703.8 14.4 %convert_element_type.182 = f32[1024,3,2048]{2,0,1:T(8,128)} convert(bf16[1024,3,2048]{2,0,1:T(8,128)(2,1)} %all-reduce.3.cloned.1.call-done) | non-fusion elementwise | flops 6291456 | bytes 37748736 | tf_op jit(solution)/shard_map/convert_element_type | solution.py:471
  (158 shorter events, 19.2 us)
Async XLA Ops:
  7.2 89.9 %copy-start = (s32[1,512]{1,0:T(1,128)S(1)}, s32[1,512]{1,0:T(1,128)}, u32[]{:S(2)}) copy-start(s32[1,512]{1,0:T(1,128)} %param.15) | copy-start | bytes 6148
  7.2 2.0 copy-start.43
  7.2 2.0 copy-start.44
  7.2 2.1 copy-start.2
  7.2 202.5 %all-gather.2.cloned.1.call-start = ((), (), s32[]{:S(2)}) async-start(), calls=%async_computation | async-start | bytes 4718592 | tf_op jit(solution)/shard_map/all_gather | solution.py:422
  7.3 74.1 %copy-start.42 = (s32[4,2]{0,1:T(2,128)S(1)}, s32[4,2]{0,1:T(2,128)}, u32[]{:S(2)}) copy-start(s32[4,2]{0,1:T(2,128)} %param.14) | copy-start | bytes 100
  80.8 6.6 copy-start.8
  80.9 622.9 %all-reduce.3.cloned.1.call-start = ((), (), s32[]{:S(2)}) async-start(), calls=%async_computation.1 | async-start | bytes 25165824 | tf_op jit(solution)/shard_map/psum | solution.py:471
  81.8 5.7 copy-start.40
  103.0 8.4 %copy-start.21 = (bf16[512,8,32]{0,2,1:T(8,128)(2,1)}, bf16[512,8,32]{0,2,1:T(8,128)(2,1)S(1)}, u32[]{:S(2)}) copy-start(bf16[512,8,32]{0,2,1:T(8,128)(2,1)S(1)} %get-tuple-element.44) | copy-start | bytes 786436
  103.0 8.4 %copy-start.25 = (bf16[512,512]{0,1:T(8,128)(2,1)S(1)}, bf16[512,512]{0,1:T(8,128)(2,1)}, u32[]{:S(2)}) copy-start(bf16[512,512]{0,1:T(8,128)(2,1)} %copy.32) | copy-start | bytes 1572868
  111.4 4.3 copy-start.33
  162.8 160.9 %copy-start.15 = (f32[128,2048]{1,0:T(8,128)}, f32[128,2048]{1,0:T(8,128)S(1)}, u32[]{:S(2)}) copy-start(f32[128,2048]{1,0:T(8,128)S(1)} %get-tuple-element.33) | copy-start | bytes 3145732
  163.3 160.3 %copy-start.35 = (f32[128]{0:T(128)}, f32[128]{0:T(128)S(1)}, u32[]{:S(2)}) copy-start(f32[128]{0:T(128)S(1)} %get-tuple-element.66) | copy-start | bytes 1540
  199.2 2.0 copy-start.5
  209.7 7.7 %copy-start.6 = (bf16[8,128,2048]{2,1,0:T(8,128)(2,1)S(1)}, bf16[8,128,2048]{2,1,0:T(8,128)(2,1)}, u32[]{:S(2)}) copy-start(bf16[8,128,2048]{2,1,0:T(8,128)(2,1)} %copy-done.5) | copy-start | bytes 12582916
  209.8 7.8 %copy-start.52 = (f32[1024,1024]{1,0:T(8,128)S(1)}, f32[1024,1024]{1,0:T(8,128)}, u32[]{:S(2)}) copy-start(f32[1024,1024]{1,0:T(8,128)} %fusion.11) | copy-start | bytes 12582916
  225.5 4.8 copy-start.49
  225.5 4.8 copy-start.51
  225.5 9.7 %copy-start.48 = (bf16[1024,1024]{1,0:T(8,128)(2,1)}, bf16[1024,1024]{1,0:T(8,128)(2,1)S(1)}, u32[]{:S(2)}) copy-start(bf16[1024,1024]{1,0:T(8,128)(2,1)S(1)} %get-tuple-element.34) | copy-start | bytes 6291460
  230.4 4.8 copy-start.45
  256.3 7.1 copy-start.50
  271.1 52.5 %copy-start.17 = (bf16[1,128,2048]{2,1,0:T(8,128)(2,1)S(1)}, bf16[1,128,2048]{2,1,0:T(8,128)(2,1)}, u32[]{:S(2)}) copy-start(bf16[1,128,2048]{2,1,0:T(8,128)(2,1)} %param.13) | copy-start | bytes 1572868
  323.7 15.1 %copy-start.38 = (f32[128]{0:T(128)}, f32[128]{0:T(128)S(1)}, u32[]{:S(2)}) copy-start(f32[128]{0:T(128)S(1)} %broadcast_multiply_fusion.2) | copy-start | bytes 1540
  447.9 5.0 copy-start.26
  447.9 5.0 slice-start
  447.9 6.2 slice-start.1
  447.9 6.2 copy-start.34
  454.1 2.7 copy-start.23
  454.1 2.7 copy-start.24
  457.9 2.0 copy-start.20
  459.7 2.9 copy-start.28
  459.8 2.8 copy-start.30
  461.2 2.2 copy-start.9
  461.2 2.2 copy-start.41
  476.9 12.6 %copy-start.29 = (bf16[512,8,64]{0,2,1:T(8,128)(2,1)S(1)}, bf16[512,8,64]{0,2,1:T(8,128)(2,1)}, u32[]{:S(2)}) copy-start(bf16[512,8,64]{0,2,1:T(8,128)(2,1)} %copy-done.28) | copy-start | bytes 1572868
  476.9 12.6 %copy-start.31 = (bf16[512,8,64]{0,2,1:T(8,128)(2,1)S(1)}, bf16[512,8,64]{0,2,1:T(8,128)(2,1)}, u32[]{:S(2)}) copy-start(bf16[512,8,64]{0,2,1:T(8,128)(2,1)} %copy-done.30) | copy-start | bytes 1572868
  476.9 12.6 %copy-start.47 = (bf16[8,64,512]{2,1,0:T(8,128)(2,1)S(1)}, bf16[8,64,512]{2,1,0:T(8,128)(2,1)}, u32[]{:S(2)}) copy-start(bf16[8,64,512]{2,1,0:T(8,128)(2,1)} %copy-done.46) | copy-start | bytes 1572868
  495.9 120.7 %copy-start.3 = (bf16[1,128,2048]{2,1,0:T(8,128)(2,1)S(1)}, bf16[1,128,2048]{2,1,0:T(8,128)(2,1)}, u32[]{:S(2)}) copy-start(bf16[1,128,2048]{2,1,0:T(8,128)(2,1)} %param.8) | copy-start | bytes 1572868
  495.9 120.7 %copy-start.37 = (f32[128]{0:T(128)S(1)}, f32[128]{0:T(128)}, u32[]{:S(2)}) copy-start(f32[128]{0:T(128)} %get-tuple-element.65) | copy-start | bytes 1540
  495.9 121.0 %copy-start.32 = (f32[2048]{0:T(1024)S(1)}, f32[2048]{0:T(1024)}, u32[]{:S(2)}) copy-start(f32[2048]{0:T(1024)} %get-tuple-element.28) | copy-start | bytes 24580
  673.9 2.0 copy-start.4
  691.9 10.2 %copy-start.11 = (f32[128,2048]{1,0:T(8,128)S(1)}, f32[128,2048]{1,0:T(8,128)}, u32[]{:S(2)}) copy-start(f32[128,2048]{1,0:T(8,128)} %copy-done.10) | copy-start | bytes 3145732
  691.9 10.2 %copy-start.16 = (f32[128,2048]{1,0:T(8,128)S(1)}, f32[128,2048]{1,0:T(8,128)}, u32[]{:S(2)}) copy-start(f32[128,2048]{1,0:T(8,128)} %copy-done.15) | copy-start | bytes 3145732
  691.9 10.2 %copy-start.18 = (bf16[1,128,2048]{2,1,0:T(8,128)(2,1)S(1)}, bf16[1,128,2048]{2,1,0:T(8,128)(2,1)}, u32[]{:S(2)}) copy-start(bf16[1,128,2048]{2,1,0:T(8,128)(2,1)} %param.13) | copy-start | bytes 1572868
  691.9 10.2 %copy-start.36 = (f32[128]{0:T(128)S(1)}, f32[128]{0:T(128)}, u32[]{:S(2)}) copy-start(f32[128]{0:T(128)} %copy-done.35) | copy-start | bytes 1540
  691.9 10.2 %copy-start.39 = (f32[128]{0:T(128)S(1)}, f32[128]{0:T(128)}, u32[]{:S(2)}) copy-start(f32[128]{0:T(128)} %copy-done.38) | copy-start | bytes 1540
  703.8 14.4 %copy-start.1 = (s32[1,512]{1,0:T(1,128)S(1)}, s32[1,512]{1,0:T(1,128)}, u32[]{:S(2)}) copy-start(s32[1,512]{1,0:T(1,128)} %param.15) | copy-start | bytes 6148
  (9 other events, 10.3 us)
Sparse Core Ops, SparseCore 0:
  81.0 48.6 all-gather.1
  256.4 291.7 all-reduce.2

commit v2 on v1

v2 whole, which is shorter than its diff:
```python
import functools
import types

import jax
import jax.numpy as jnp
from jax import lax
from jax.experimental import pallas as pl
from jax.experimental.pallas import tpu as pltpu
from jax.sharding import PartitionSpec as P

HEAD = 64


NORM_EPS = 1e-05
ROPE_BASE = 130000.0
MASKED_OUT = -1e30
F32 = jnp.float32
BF16 = jnp.bfloat16
MESH = pl.DeviceIdType.MESH
DMA = pltpu.SemaphoreType.DMA
ANY = pl.BlockSpec(memory_space=pl.ANY)
VMEM = pl.BlockSpec(memory_space=pltpu.VMEM)


def send(src, dst, send_sem, recv_sem, device):
    return pltpu.make_async_remote_copy(
        src_ref=src,
        dst_ref=dst,
        send_sem=send_sem,
        recv_sem=recv_sem,
        device_id=device,
        device_id_type=MESH,
    )


class Place:
    def __init__(self, n_seq, n_fsdp):
        self.n_seq, self.line = n_seq, n_fsdp // 2
        self.s = lax.axis_index("seq")
        self.f = lax.axis_index("fsdp")
        self.r = lax.div(self.f, 2)
        self.c = lax.rem(self.f, 2)
        self.up = (self.s, self.f + 2)
        self.down = (self.s, self.f - 2)
        self.sister = (self.s, 2 * self.r + 1 - self.c)

    def peer(self, d):
        return (jnp.bitwise_xor(self.s, d), self.f)

    def greet(self):
        barrier = pltpu.get_barrier_semaphore()
        wrap = 2 * self.line
        partners = [
            (self.s, lax.rem(self.f + 2, wrap)),
            (self.s, lax.rem(self.f + wrap - 2, wrap)),
            self.sister,
        ]
        partners += [self.peer(d) for d in range(1, self.n_seq)]
        for partner in partners:
            pl.semaphore_signal(barrier, inc=1, device_id=partner, device_id_type=MESH)
        pl.semaphore_wait(barrier, len(partners))


class GatherLine:
    def __init__(self, n_fsdp, parts=1):
        line = n_fsdp // 2
        self.scratch = [DMA((line, parts)) for _ in range(5)] + [DMA((1,))]
        self.parts = parts

    def steps(self, at, x, o, refs, use=None):
        line_r, sis_r, up_s, down_s, sis_s, own_s = refs
        parts, line, r, c = self.parts, at.line, at.r, at.c
        rows = o.shape[1] // parts

        def cut(ref, k):
            return ref.at[pl.ds(k * rows, rows)]

        def go_up(src, b, k):
            return send(src, cut(o.at[2 * b + c], k), up_s.at[b, k], line_r.at[b, k], at.up)

        def go_down(src, b, k):
            return send(src, cut(o.at[2 * b + c], k), down_s.at[b, k], line_r.at[b, k], at.down)

        def go_sister(src, b, k):
            return send(src, cut(o.at[2 * b + c], k), sis_s.at[b, k], sis_r.at[b, k], at.sister)

        def complete(b):
            for k in range(parts):
                src = cut(o.at[2 * b + 1 - c], k)
                send(src, src, sis_s.at[b, k], sis_r.at[b, k], at.sister).wait_recv()
            if use is not None:
                use(b)

        own = pltpu.make_async_copy(x, o.at[at.f], own_s.at[0])
        own.start()
        for k in range(parts):
            src = cut(x, k)
            pl.when(r < line - 1)(lambda: go_up(src, r, k).start())
            pl.when(r > 0)(lambda: go_down(src, r, k).start())
            go_sister(src, r, k).start()
        yield
        for t in range(1, line):
            for k in range(parts):
                low, high = r - t, r + t

                @pl.when(low >= 0)
                def _():
                    src = cut(o.at[2 * low + c], k)
                    go_up(src, low, k).wait_recv()
                    pl.when(r < line - 1)(lambda: go_up(src, low, k).start())
                    go_sister(src, low, k).start()

                @pl.when(high < line)
                def _():
                    src = cut(o.at[2 * high + c], k)
                    go_down(src, high, k).wait_recv()
                    pl.when(r > 0)(lambda: go_down(src, high, k).start())
                    go_sister(src, high, k).start()

            yield
            if t == 1:
                own.wait()
                complete(r)
            else:
                pl.when(r - t + 1 >= 0)(lambda: complete(r - t + 1))
                pl.when(r + t - 1 < line)(lambda: complete(r + t - 1))
        pl.when(r - line + 1 >= 0)(lambda: complete(r - line + 1))
        pl.when(r + line - 1 < line)(lambda: complete(r + line - 1))
        yield
        for b in range(line):
            for k in range(parts):
                src = cut(x, k)
                go_sister(src, b, k).wait_send()
                pl.when((b <= r) & (r < line - 1))(lambda: go_up(src, b, k).wait_send())
                pl.when((b >= r) & (r > 0))(lambda: go_down(src, b, k).wait_send())


class ScatterLine:
    def __init__(self, part, n_fsdp, parts=1, far=False):
        line = n_fsdp // 2
        block = part.shape[1:]
        self.scratch = [
            pltpu.VMEM((line,) + block, part.dtype),
            pltpu.VMEM((line + 1,) + block, part.dtype),
        ]
        self.scratch += [DMA((line, parts)), DMA((line, parts)), DMA((line, parts))]
        self.scratch += [DMA((line + 1, parts))]
        if far:
            self.scratch += [pltpu.VMEM((line,) + block, part.dtype), DMA((line,))]
        self.parts, self.far = parts, far

    def steps(self, at, refs):
        part, o, sis, come, sis_s, sis_r, line_s, line_r = refs[:8]
        near, near_s = refs[8:] if self.far else (None, None)
        parts, line, r, c = self.parts, at.line, at.r, at.c
        rows = part.shape[1] // parts
        tile = 16 if rows % 16 == 0 else rows

        def cut(ref, k):
            return ref.at[pl.ds(k * rows, rows)]

        def to_sister(b, k):
            return send(
                cut(part.at[2 * b + 1 - c], k),
                cut(sis.at[b], k),
                sis_s.at[b, k],
                sis_r.at[b, k],
                at.sister,
            )

        def slot(b, own):
            return jnp.where(b == own, line, b)

        def go_up(b, k):
            return send(cut(sis.at[b], k), cut(come.at[b], k), line_s.at[b, k], line_r.at[b, k], at.up)

        def go_down(b, k, own):
            i = slot(b, own)
            return send(
                cut(sis.at[b], k), cut(come.at[i], k), line_s.at[b, k], line_r.at[i, k], at.down
            )

        def add(b, k, came, out=None):
            def body(i, carry):
                at_rows = pl.ds(k * rows + i * tile, tile)
                own = near[b, at_rows] if self.far else part[2 * b + c, at_rows]
                total = own.astype(F32) + sis[b, at_rows].astype(F32)
                for j in came:
                    total = total + come[j, at_rows].astype(F32)
                if out is None:
                    sis[b, at_rows] = total.astype(sis.dtype)
                else:
                    out[at_rows] = total.astype(out.dtype)
                return carry

            lax.fori_loop(0, rows // tile, body, 0)

        order = []
        for j in range(line):
            order += [b for b in (line - 1 - j, j) if b not in order]
        for b in order:
            for k in range(parts):
                to_sister(b, k).start()
        if self.far:
            loads = [
                pltpu.make_async_copy(part.at[2 * b + c], near.at[b], near_s.at[b])
                for b in range(line)
            ]
            for one in loads:
                one.start()
            for one in loads:
                one.wait()
        yield
        for j in range(line - 1):
            for k in range(parts):
                b = line - 1 - j

                @pl.when(b > r)
                def _():
                    to_sister(b, k).wait_recv()

                    @pl.when(r > 0)
                    def _():
                        go_up(b, k).wait_recv()
                        add(b, k, [b])

                    pl.when(r == 0)(lambda: add(b, k, []))
                    go_up(b, k).start()

                @pl.when(j < r)
                def _():
                    to_sister(j, k).wait_recv()

                    @pl.when(r < line - 1)
                    def _():
                        go_down(j, k, -1).wait_recv()
                        add(j, k, [j])

                    pl.when(r == line - 1)(lambda: add(j, k, []))
                    go_down(j, k, r - 1).start()

            yield
        for k in range(parts):
            to_sister(r, k).wait_recv()
            pl.when(r > 0)(lambda: go_up(r, k).wait_recv())
            pl.when(r < line - 1)(lambda: go_down(r, k, r).wait_recv())
            pl.when(r == 0)(lambda: add(r, k, [line], o))
            pl.when(r == line - 1)(lambda: add(r, k, [r], o))
            pl.when((r > 0) & (r < line - 1))(lambda: add(r, k, [r, line], o))
        yield
        for b in range(line):
            for k in range(parts):
                to_sister(b, k).wait_send()
                pl.when(b != r)(lambda: go_up(b, k).wait_send())


class GatherSeq:
    def __init__(self, n_seq):
        self.scratch = [DMA((n_seq,)), DMA((n_seq,))]

    def steps(self, at, refs):
        x, o, s_sem, r_sem = refs

        def go(d):
            return send(x, o.at[at.s], s_sem.at[d], r_sem.at[d], at.peer(d))

        for d in reversed(range(1, at.n_seq)):
            go(d).start()
        own = pltpu.make_async_copy(x, o.at[at.s], s_sem.at[0])
        own.start()
        yield
        own.wait()
        for d in range(1, at.n_seq):
            go(d).wait()


class ScatterSeq:
    def __init__(self, part):
        self.scratch = [pltpu.VMEM(part.shape, part.dtype), DMA(part.shape[:1]), DMA(part.shape[:1])]

    def steps(self, at, refs):
        part, o, land, s_sem, r_sem = refs
        rows = part.shape[1]
        tile = 16 if rows % 16 == 0 else rows

        def go(d):
            peer = at.peer(d)
            return send(part.at[peer[0]], land.at[d], s_sem.at[d], r_sem.at[d], peer)

        for d in reversed(range(1, at.n_seq)):
            go(d).start()
        yield
        for d in range(1, at.n_seq):
            go(d).wait()

        def body(i, carry):
            at_rows = pl.ds(i * tile, tile)
            total = part[at.s, at_rows].astype(F32)
            for d in range(1, at.n_seq):
                total = total + land[d, at_rows].astype(F32)
            o[at_rows] = total.astype(o.dtype)
            return carry

        lax.fori_loop(0, rows // tile, body, 0)


class ReduceSeq:
    def __init__(self, shape, dtype, n_seq):
        rows, cols = shape
        self.bits = n_seq.bit_length() - 1
        self.rows = rows // 2
        self.room = self.rows - (self.rows >> self.bits)
        self.scratch = [
            pltpu.VMEM(shape, dtype),
            pltpu.VMEM((2 * self.room, cols), dtype),
            DMA((2,)),
            DMA((2, self.bits)),
            DMA((2, self.bits)),
            DMA((2, n_seq)),
            DMA((2, n_seq)),
            DMA((2,)),
        ]

    def steps(self, at, refs):
        g_in, o, g, land, load_s, rs_s, rs_r, ag_s, ag_r, own_s = refs
        bits = self.bits
        orders = [[(i + p) % bits for i in range(bits)] for p in range(2)]
        mult = self.rows >> bits

        def bit(t, b):
            return jnp.bitwise_and(lax.shift_right_logical(t, b), 1)

        def base(p, t, n):
            low = p * self.rows
            for i in range(n):
                low = low + bit(t, orders[p][i]) * (self.rows >> (i + 1))
            return pl.multiple_of(low, mult)

        def load(p):
            part = pl.ds(p * self.rows, self.rows)
            return pltpu.make_async_copy(g_in.at[part], g.at[part], load_s.at[p])

        def slot(p, i):
            return p * self.room + sum(self.rows >> (j + 1) for j in range(i))

        def halve(p, i):
            size = self.rows >> (i + 1)
            other = jnp.bitwise_xor(at.s, 1 << orders[p][i])
            return send(
                g.at[pl.ds(base(p, other, i + 1), size)],
                land.at[pl.ds(slot(p, i), size)],
                rs_s.at[p, i],
                rs_r.at[p, i],
                (other, at.f),
            )

        def add(p, i):
            size = self.rows >> (i + 1)
            low, first = base(p, at.s, i + 1), slot(p, i)

            def body(j, carry):
                mine = pl.ds(pl.multiple_of(low + j * 16, 16), 16)
                came = pl.ds(pl.multiple_of(first + j * 16, 16), 16)
                total = g[mine].astype(F32) + land[came].astype(F32)
                g[mine] = total.astype(g.dtype)
                return carry

            lax.fori_loop(0, size // 16, body, 0)

        def masks(p, j):
            out = [0]
            for i in range(j):
                out += [m | (1 << orders[p][bits - 1 - i]) for m in out]
            return out

        def double(p, j, mask):
            b = orders[p][bits - 1 - j]
            piece = pl.ds(base(p, jnp.bitwise_xor(at.s, mask), bits), mult)
            src = g.at[piece] if mask == 0 else o.at[piece]
            i = (1 << b) | mask
            return send(
                src, o.at[piece], ag_s.at[p, i], ag_r.at[p, i], (jnp.bitwise_xor(at.s, 1 << b), at.f)
            )

        def arrive(p, j, mask):
            b = orders[p][bits - 1 - j]
            piece = pl.ds(base(p, jnp.bitwise_xor(at.s, (1 << b) | mask), bits), mult)
            i = (1 << b) | mask
            return send(
                o.at[piece], o.at[piece], ag_s.at[p, i], ag_r.at[p, i],
                (jnp.bitwise_xor(at.s, 1 << b), at.f),
            )

        def own(p):
            piece = pl.ds(base(p, at.s, bits), mult)
            return pltpu.make_async_copy(g.at[piece], o.at[piece], own_s.at[p])

        for p in range(2):
            load(p).start()
        for p in range(2):
            load(p).wait()
            halve(p, 0).start()
        yield
        for i in range(bits):
            for p in range(2):
                halve(p, i).wait_recv()
                add(p, i)
                if i + 1 < bits:
                    halve(p, i + 1).start()
                else:
                    for j in range(bits):
                        double(p, j, 0).start()
                    own(p).start()
                yield
        for j in range(bits):
            for p in range(2):
                for mask in masks(p, j):
                    arrive(p, j, mask).wait_recv()
                    came = (1 << orders[p][bits - 1 - j]) | mask
                    for later in range(j + 1, bits):
                        double(p, later, came).start()
                yield
        for p in range(2):
            own(p).wait()
            for i in range(bits):
                halve(p, i).wait_send()
            for j in range(bits):
                for mask in masks(p, j):
                    double(p, j, mask).wait_send()


class SpreadSeq:
    def __init__(self, n_seq):
        self.bits = n_seq.bit_length() - 1
        self.scratch = [DMA((2, n_seq)), DMA((2, n_seq)), DMA((1,))]

    def steps(self, at, refs):
        x, o, s_sem, r_sem, own_s = refs
        bits, half = self.bits, x.shape[0] // 2
        orders = [[(i + p) % bits for i in range(bits)] for p in range(2)]

        def known(p, j):
            out = [0]
            for i in range(j):
                out += [m | (1 << orders[p][i]) for m in out]
            return out

        def piece(p, mask):
            return o.at[jnp.bitwise_xor(at.s, mask), pl.ds(p * half, half)]

        def go(p, j, mask):
            b = 1 << orders[p][j]
            src = x.at[pl.ds(p * half, half)] if mask == 0 else piece(p, mask)
            i = b | mask
            return send(src, piece(p, mask), s_sem.at[p, i], r_sem.at[p, i], at.peer(b))

        def arrive(p, j, mask):
            b = 1 << orders[p][j]
            i = b | mask
            here = piece(p, i)
            return send(here, here, s_sem.at[p, i], r_sem.at[p, i], at.peer(b))

        for p in range(2):
            for j in range(bits):
                go(p, j, 0).start()
        own = pltpu.make_async_copy(x, o.at[at.s], own_s.at[0])
        own.start()
        yield
        for j in range(bits):
            for p in range(2):
                for mask in known(p, j):
                    arrive(p, j, mask).wait_recv()
                    for later in range(j + 1, bits):
                        go(p, later, (1 << orders[p][j]) | mask).start()
            yield
        own.wait()
        for j in range(bits):
            for p in range(2):
                for mask in known(p, j):
                    go(p, j, mask).wait_send()


def interleave(order, running):
    for name in order:
        if name in running and next(running[name], END) is END:
            del running[name]
    while running:
        for name in list(running):
            if next(running[name], END) is END:
                del running[name]


END = object()


class Rooms:
    def __init__(self):
        self.args, self.in_specs, self.outs, self.out_specs, self.scratch = [], [], [], [], []
        self.names = ([], [], [])

    def note(self, group, name, x):
        many = isinstance(x, (list, tuple))
        self.names[group].append((name, len(x) if many else None))
        return list(x) if many else [x]

    def take(self, spec, **arrays):
        for name, x in arrays.items():
            new = self.note(0, name, x)
            self.args += new
            self.in_specs += [spec] * len(new)

    def give(self, spec, **shapes):
        for name, x in shapes.items():
            new = self.note(1, name, x)
            self.outs += new
            self.out_specs += [spec] * len(new)

    def keep(self, **kinds):
        for name, x in kinds.items():
            self.scratch += self.note(2, name, x)

    def bind(self, refs, groups):
        table, refs = types.SimpleNamespace(), list(refs)
        for group in groups:
            for name, many in self.names[group]:
                count = 1 if many is None else many
                mine, refs = refs[:count], refs[count:]
                setattr(table, name, mine[0] if many is None else mine)
        return table

    def run(self, body, name, collective_id, n_seq, n_fsdp):
        def kernel(*refs):
            at = Place(n_seq, n_fsdp)
            at.greet()
            body(at, self.bind(refs, (0, 1, 2)))

        out = pl.pallas_call(
            kernel,
            out_shape=self.outs,
            in_specs=self.in_specs,
            out_specs=self.out_specs,
            scratch_shapes=self.scratch,
            compiler_params=pltpu.CompilerParams(
                collective_id=collective_id, has_side_effects=True, vmem_limit_bytes=62 * 2**20
            ),
            name=name,
        )(*self.args)
        return self.bind(out, (1,))


def like(shape, dtype=BF16):
    return jax.ShapeDtypeStruct(tuple(shape), dtype)


def room(*shape, dtype=BF16):
    return pltpu.VMEM(shape, dtype)


def dot(a, b, dims):
    return lax.dot_general(a, b, (dims, ((), ())), preferred_element_type=F32)


NN = ((1,), (0,))
NT = ((1,), (1,))
TN = ((0,), (0,))


def turned(x, cos, sin):
    lane = lax.broadcasted_iota(jnp.int32, x.shape, 1)
    other = jnp.where(lane % HEAD < HEAD // 2, pltpu.roll(x, 96, 1), pltpu.roll(x, 32, 1))
    return x * cos + other * sin


def head_masks():
    lane = lax.broadcasted_iota(jnp.int32, (1, 128), 1)
    first = (lane < HEAD).astype(F32)
    return first, 1.0 - first


def back_pair(pair, do, q, k, v, lse, cos, sin, dqkv, masking, dk, dv):
    pos_col, pos_row, doc_col, doc_row = masking
    length, share = q.shape
    span = 256
    masks = head_masks()
    lane = lax.broadcasted_iota(jnp.int32, (span, 128), 1)
    lanes = slice(pair * 128, pair * 128 + 128)
    dk[...] = jnp.zeros_like(dk)
    dv[...] = jnp.zeros_like(dv)

    def one_span(i, carry):
        rows = pl.ds(pl.multiple_of(i * span, span), span)
        allowed = (pos_row[...] <= pos_col[rows]) & (doc_row[...] == doc_col[rows])
        bias = jnp.where(allowed, 0.0, MASKED_OUT)
        dq = jnp.zeros((span, 128), F32)
        for h in range(2):
            mask = masks[h].astype(BF16)
            field, grad = q[rows, lanes] * mask, do[rows, lanes] * mask
            log_total = jnp.sum(
                jnp.where(lane == 2 * pair + h, lse[rows], 0.0), axis=-1, keepdims=True
            )
            z = dot(field, k[:, lanes], NT) * 0.125 + bias
            prob = jnp.exp(z - log_total)
            dp = dot(grad, v[:, lanes], NT)
            delta = jnp.sum(prob * dp, axis=-1, keepdims=True)
            dz = (prob * (dp - delta)).astype(BF16)
            dq = dq + dot(dz, k[:, lanes], NN) * masks[h]
            dk[...] += dot(dz, field, TN)
            dv[...] += dot(prob.astype(BF16), grad, TN)
        dqkv[rows, lanes] = turned(dq * 0.125, cos[rows], -sin[rows]).astype(BF16)
        return carry

    lax.fori_loop(0, length // span, one_span, 0)
    at = share + pair * 128
    dqkv[:, at : at + 128] = turned(dk[...] * 0.125, cos[...], -sin[...]).astype(BF16)
    at = 2 * share + pair * 128
    dqkv[:, at : at + 128] = dv[...].astype(BF16)


def norm_back(grad_normed, value, scale, gain):
    weighted = grad_normed * gain
    inner_mean = jnp.mean(weighted * value, axis=-1, keepdims=True)
    return scale * (weighted - value * scale * scale * inner_mean)


def scale_of(value):
    return lax.rsqrt(jnp.mean(value * value, axis=-1, keepdims=True) + NORM_EPS)


def front(n_seq, n_fsdp, w_own, hidden, gains, out_grad, mlp_w, tables):
    cos, sin, pos_col, pos_row, doc_col, doc_row = tables
    tok, model = hidden.shape
    length, share = n_seq * tok, w_own.shape[1] // 4
    line, rows_f, units = n_fsdp // 2, w_own.shape[0], mlp_w.shape[1]
    qkv_shape, o_shape = (n_fsdp, rows_f, 3 * share), (n_fsdp, rows_f, share)
    per = n_fsdp // n_seq
    n_pairs = share // 128
    span = 256
    get_w, get_o = GatherLine(n_fsdp, 2), GatherLine(n_fsdp)
    get_gain, get_grad, get_n2 = GatherLine(n_fsdp), GatherLine(n_fsdp, 2), GatherLine(n_fsdp, 2)
    get_x = GatherSeq(n_seq)
    rooms = Rooms()
    rooms.take(
        VMEM, hidden=hidden, gains=gains, cos=cos, sin=sin,
        pos_col=pos_col, pos_row=pos_row, doc_col=doc_col, doc_row=doc_row,
    )
    rooms.take(ANY, w_own=w_own, out_grad=out_grad, mlp_w=mlp_w)
    rooms.give(
        ANY,
        w_qkv_out=like(qkv_shape),
        w_o_out=like(o_shape),
        n1_out=like((n_seq, length, share)),
        o_out=like((n_seq, length, share)),
        n2_out=like((n_fsdp, tok, model)),
        grad_out=like((n_fsdp, tok, model)),
        hid=like((n_fsdp * tok, units)),
        dg=like((n_fsdp * tok, units)),
        du=like((n_fsdp * tok, units)),
    )
    rooms.give(
        VMEM,
        q=like((length, share)),
        k=like((length, share)),
        v=like((length, share)),
        lse=like((length, 128), F32),
        middle=like((tok, model), F32),
        gain_a=like((1, model), F32),
        gain_m=like((1, model), F32),
    )
    rooms.keep(
        get_w=get_w.scratch, get_o=get_o.scratch, get_gain=get_gain.scratch,
        get_grad=get_grad.scratch, get_n2=get_n2.scratch, get_x=get_x.scratch,
        w_qkv_all=room(*qkv_shape),
        w_o_all=room(*o_shape),
        gains_all=room(n_fsdp, *gains.shape),
        x_all=room(n_seq, tok, model),
        n1=room(n_fsdp, length, rows_f),
        o_all=room(n_seq, length, share),
        y_total=room(length, share, dtype=F32),
        y=room(n_seq, tok, share),
        y_land=room(n_seq, tok, share),
        n2=room(tok, model),
        n2_all=room(n_fsdp, tok, model),
        grad_all=room(n_fsdp, tok, model),
        w_gate=room(units, model),
        w_up=room(units, model),
        w_down=room(units, model),
        act=room(n_fsdp * tok, units, dtype=F32),
        stage=room(line, 3, 2 * tok, units),
        load=DMA((3,)),
        save=DMA((6 + n_fsdp,)),
        stage_s=DMA((line, 3)),
        o_s=DMA((n_pairs, n_seq)),
        o_r=DMA((n_pairs, n_seq)),
        y_s=DMA((n_seq,)),
        y_r=DMA((n_seq,)),
    )

    def body(at, r):
        loads = [
            pltpu.make_async_copy(r.mlp_w.at[i], w, r.load.at[i])
            for i, w in enumerate((r.w_gate, r.w_up, r.w_down))
        ]
        saves = []
        w_qkv, w_o = r.w_own.at[:, pl.ds(0, 3 * share)], r.w_own.at[:, pl.ds(3 * share, share)]

        def save(src, dst):
            saves.append(pltpu.make_async_copy(src, dst, r.save.at[len(saves)]))
            saves[-1].start()

        def total(c, rows, cols):
            low, left = (c // 2) * length, (c % 2) * share
            return (
                slice(low + rows.start, low + rows.stop), slice(left + cols.start, left + cols.stop)
            )

        def project(b):
            for f in (2 * b, 2 * b + 1):
                for c in range(3):
                    weights = r.w_qkv_all[f, :, c * share : (c + 1) * share]
                    for i in range(0, length, span):
                        part = dot(r.n1[f, i : i + span], weights, NN)
                        r.act[total(c, slice(i, i + span), slice(0, share))] += part

        def grad_of(b):
            rows = pl.ds(pl.multiple_of(2 * tok * b, 2 * tok), 2 * tok)
            grad = r.grad_all[pl.ds(2 * b, 2)].reshape(2 * tok, model)
            r.act[rows] = dot(grad, r.w_down[...], NT)

        def stored(b, k):
            rows = pl.ds(pl.multiple_of(2 * tok * b, 2 * tok), 2 * tok)
            return pltpu.make_async_copy(
                r.stage.at[b, k], (r.hid, r.dg, r.du)[k].at[rows], r.stage_s.at[b, k]
            )

        def activate(b):
            rows = pl.ds(pl.multiple_of(2 * tok * b, 2 * tok), 2 * tok)
            n2 = r.n2_all[pl.ds(2 * b, 2)].reshape(2 * tok, model)
            gate = dot(n2, r.w_gate[...], NT)
            up = dot(n2, r.w_up[...], NT)
            grad = r.act[rows]
            sigma = jax.nn.sigmoid(gate)
            silu = gate * sigma
            r.stage[b, 0] = (silu * up).astype(BF16)
            r.stage[b, 1] = (grad * up * sigma * (1.0 + gate * (1.0 - sigma))).astype(BF16)
            r.stage[b, 2] = (grad * silu).astype(BF16)
            for k in range(3):
                stored(b, k).start()

        def attend(pair):
            lanes = slice(pair * 128, pair * 128 + 128)
            masks = head_masks()
            lane = lax.broadcasted_iota(jnp.int32, (span, 128), 1)

            def one_span(i, carry):
                rows = pl.ds(pl.multiple_of(i * span, span), span)
                allowed = (r.pos_row[...] <= r.pos_col[rows]) & (r.doc_row[...] == r.doc_col[rows])
                bias = jnp.where(allowed, 0.0, MASKED_OUT)
                parts = []
                for h in range(2):
                    field = r.q[rows, lanes] * masks[h].astype(BF16)
                    z = dot(field, r.k[:, lanes], NT) * 0.125 + bias
                    top = jnp.max(z, axis=-1, keepdims=True)
                    e = jnp.exp(z - top)
                    sum_e = jnp.sum(e, axis=-1, keepdims=True)
                    prob = (e * (1.0 / sum_e)).astype(BF16)
                    parts.append(dot(prob, r.v[:, lanes], NN) * masks[h])
                    here = lane == 2 * pair + h
                    r.lse[rows] = jnp.where(here, top + jnp.log(sum_e), r.lse[rows])
                r.o_all[at.s, rows, lanes] = (parts[0] + parts[1]).astype(BF16)
                return carry

            lax.fori_loop(0, length // span, one_span, 0)

        def go_o(pair, d, owner):
            here = r.o_all.at[owner, :, pl.ds(pair * 128, 128)]
            return send(here, here, r.o_s.at[pair, d], r.o_r.at[pair, d], at.peer(d))

        def go_y(d):
            peer = at.peer(d)
            return send(r.y.at[peer[0]], r.y_land.at[d], r.y_s.at[d], r.y_r.at[d], peer)

        def chain():
            weights = get_w.steps(at, w_qkv, r.w_qkv_all, r.get_w, project)
            next(weights)
            rows_in = get_x.steps(at, [r.hidden, r.x_all] + r.get_x)
            next(rows_in)
            for one in loads:
                one.start()
            r.act[...] = jnp.zeros_like(r.act)
            for _ in get_gain.steps(at, r.gains, r.gains_all, r.get_gain):
                pass
            for f in range(n_fsdp):
                cols = slice(f * rows_f, (f + 1) * rows_f)
                r.gain_a[:, cols] = r.gains_all[f, 0:1].astype(F32)
                r.gain_m[:, cols] = r.gains_all[f, 16:17].astype(F32)
            next(weights)
            for _ in rows_in:
                pass
            r.lse[...] = jnp.zeros_like(r.lse)

            def norm(i, carry):
                j, k = i // (tok // 16), i % (tok // 16)
                x = r.x_all[j, pl.ds(pl.multiple_of(k * 16, 16), 16)].astype(F32)
                normed = (x * scale_of(x) * r.gain_a[...]).astype(BF16)
                rows = pl.ds(pl.multiple_of(i * 16, 16), 16)
                for f in range(n_fsdp):
                    r.n1[f, rows] = normed[:, f * rows_f : (f + 1) * rows_f]
                return carry

            lax.fori_loop(0, length // 16, norm, 0)
            for f in range(n_fsdp):
                save(r.n1.at[f], r.n1_out.at[f // per, :, pl.ds((f % per) * rows_f, rows_f)])
            yield
            for _ in weights:
                yield
            save(r.w_qkv_all, r.w_qkv_out)
            for c, out in enumerate((r.q, r.k)):
                for j in range(0, share, 128):
                    field = r.act[total(c, slice(0, length), slice(j, j + 128))]
                    out[:, j : j + 128] = turned(field, r.cos[...], r.sin[...]).astype(BF16)
            r.v[...] = r.act[total(2, slice(0, length), slice(0, share))].astype(BF16)
            projected.append(True)
            yield
            for pair in range(n_pairs):
                attend(pair)
                for d in reversed(range(1, n_seq)):
                    go_o(pair, d, at.s).start()
                yield
            for _ in out_weights:
                pass
            for d in range(n_seq):
                owner = at.peer(d)[0]
                if d:
                    for pair in range(n_pairs):
                        go_o(pair, d, owner).wait_recv()
                for h in range(per):
                    part = dot(
                        r.o_all[owner, :, h * rows_f : (h + 1) * rows_f],
                        r.w_o_all[owner * per + h],
                        NN,
                    )
                    if d == 0 and h == 0:
                        r.y_total[...] = part
                    else:
                        r.y_total[...] += part
                yield
            for j in range(n_seq):
                r.y[j] = r.y_total[j * tok : (j + 1) * tok].astype(BF16)
            for d in reversed(range(1, n_seq)):
                go_y(d).start()
            save(r.o_all, r.o_out)
            save(r.w_o_all, r.w_o_out)
            r.y_land[0] = r.y[at.s]
            yield
            for d in range(1, n_seq):
                go_y(d).wait()

            def middle(i, carry):
                rows = pl.ds(pl.multiple_of(i * 16, 16), 16)
                for j in range(n_seq):
                    cols = slice(j * share, (j + 1) * share)
                    branch = r.y_land[jnp.bitwise_xor(at.s, j), rows].astype(F32)
                    r.middle[rows, cols] = r.hidden[rows, cols].astype(F32) + branch
                h = r.middle[rows]
                r.n2[rows] = (h * scale_of(h) * r.gain_m[...]).astype(BF16)
                return carry

            lax.fori_loop(0, tok // 16, middle, 0)
            yield
            tokens = get_n2.steps(at, r.n2, r.n2_all, r.get_n2, activate)
            next(tokens)
            yield
            next(tokens)
            for _ in grads:
                pass
            for one in loads[:2]:
                one.wait()
            for _ in tokens:
                yield

        def cotangents():
            while not projected:
                yield
            loads[2].wait()
            yield from get_grad.steps(at, r.out_grad, r.grad_all, r.get_grad, grad_of)
            save(r.grad_all, r.grad_out)

        projected = []
        out_weights = get_o.steps(at, w_o, r.w_o_all, r.get_o)
        grads = cotangents()
        order = [0, 0, 0, 1, 0, 0, 1, 0, 1, 0, 1, 0, 1, 1, 2, 0, 0, 2, 0, 0, 0, 0, 2, 0, 2, 0]
        interleave(order, {0: chain(), 1: out_weights, 2: grads})
        for pair in range(n_pairs):
            for d in range(1, n_seq):
                go_o(pair, d, at.s).wait_send()
        save(r.n2_all, r.n2_out)
        for b in range(line):
            for k in range(3):
                stored(b, k).wait()
        for one in saves:
            one.wait()

    return rooms.run(body, "front", 1, n_seq, n_fsdp)


BACK_ONE_ORDER = [2, 0, 0, 0, 3]


def back_one(n_seq, n_fsdp, dn2_part, middle, out_grad, gain_m, w_qkv, w_o, o_all, n1, saved, grads):
    q, k, v, lse, cos, sin, pos_col, pos_row, doc_col, doc_row = saved
    tok, model = middle.shape
    length, share = q.shape
    rooms = Rooms()
    rooms.take(
        VMEM, middle=middle, out_grad=out_grad, gain_m=gain_m, q=q, k=k, v=v, lse=lse,
        cos=cos, sin=sin, pos_col=pos_col, pos_row=pos_row, doc_col=doc_col, doc_row=doc_row,
    )
    rooms.take(ANY, dn2_part=dn2_part, w_qkv=w_qkv, w_o=w_o, o_all=o_all, n1=n1, g_in=grads)
    rooms.give(ANY, g_out=[like(g.shape) for g in grads], dw_qkv=like((model, 3 * share)))
    rooms.give(
        VMEM,
        dh1=like((tok, model), F32),
        gain=like((8, model), F32),
        dn1_part=like((n_seq, tok, model)),
        dw_o=like((model // n_fsdp, share)),
    )
    line = ScatterLine(dn2_part, n_fsdp, 2, far=True)
    o_block = like((n_fsdp, model // n_fsdp, share))
    line_o = ScatterLine(o_block, n_fsdp)
    reduces = [ReduceSeq(g.shape, g.dtype, n_seq) for g in grads]
    rooms.keep(
        line=line.scratch,
        line_o=line_o.scratch,
        reduce_0=reduces[0].scratch,
        reduce_1=reduces[1].scratch,
        dw_o_part=room(*o_block.shape),
        dn2=room(tok, model, dtype=F32),
        da=room(tok, model),
        da_cols=room(length, share),
        w_qkv_here=room(*w_qkv.shape),
        w_o_here=room(*w_o.shape),
        o_here=room(*o_all.shape),
        do_part=room(n_seq, length, share),
        do_land=room(n_seq, length, share),
        do=room(length, share),
        dqkv=room(length, 3 * share),
        dk=room(length, 128, dtype=F32),
        dv=room(length, 128, dtype=F32),
        dw_stage=room(2, share, 3 * share),
        load=DMA((4,)),
        stage=DMA((2,)),
        swap=[DMA((n_seq,)), DMA((n_seq,))],
        do_sem=[DMA((n_seq,)), DMA((n_seq,))],
    )

    def body(at, r):
        def chain():
            loads = [
                pltpu.make_async_copy(a, b, r.load.at[i])
                for i, (a, b) in enumerate(
                    ((r.w_qkv, r.w_qkv_here), (r.w_o, r.w_o_here), (r.o_all, r.o_here), (r.n1, r.o_here))
                )
            ]
            for one in loads[:3]:
                one.start()
            yield from line.steps(at, [r.dn2_part, r.dn2] + r.line)
            middle, out_grad, gain_m = r.middle, r.out_grad, r.gain_m
            dn2, dh1, da, gain = r.dn2, r.dh1, r.da, r.gain
            gain[...] = jnp.zeros_like(gain)

            def norm(i, carry):
                rows = pl.ds(i * 16, 16)
                h, grad = middle[rows], dn2[rows]
                scale = lax.rsqrt(jnp.mean(h * h, axis=-1, keepdims=True) + NORM_EPS)
                wide = out_grad[rows].astype(F32) + norm_back(grad, h, scale, gain_m[...])
                dh1[rows] = wide
                da[rows] = wide.astype(BF16)
                term = grad * h * scale
                gain[...] += term[:8] + term[8:]
                return carry

            lax.fori_loop(0, tok // 16, norm, 0)
            da_cols = r.da_cols
            swap_s, swap_r = r.swap

            def swap(d):
                peer = at.peer(d)
                cols = pl.ds(pl.multiple_of(peer[0] * share, 128), share)
                rows = pl.ds(pl.multiple_of(at.s * tok, tok), tok)
                return send(da.at[:, cols], da_cols.at[rows], swap_s.at[d], swap_r.at[d], peer)

            for d in reversed(range(1, n_seq)):
                swap(d).start()
            cols = pl.ds(pl.multiple_of(at.s * share, 128), share)
            rows = pl.ds(pl.multiple_of(at.s * tok, tok), tok)
            da_cols[rows] = da[:, cols]
            for one in loads[:3]:
                one.wait()
            yield
            for d in range(1, n_seq):
                swap(d).wait()
            w_qkv_here, w_o_here, o_here = r.w_qkv_here, r.w_o_here, r.o_here
            do_part, do_land = r.do_part, r.do_land
            do_s, do_r = r.do_sem

            def go(d):
                return send(
                    do_part.at[d], do_land.at[d], do_s.at[d], do_r.at[d], at.peer(d)
                )

            for d in reversed(range(n_seq)):
                rows = pl.ds(pl.multiple_of(at.peer(d)[0] * share, share), share)
                do_part[d] = dot(da_cols[...], w_o_here[rows], NT).astype(BF16)
                if d:
                    go(d).start()
            yield
            dw_o = r.dw_o_part
            per = n_fsdp // n_seq
            for j in range(n_seq):
                field = dot(o_here[j], da_cols[...], TN).astype(BF16)
                dw_o[j * per : (j + 1) * per] = field.reshape((per,) + dw_o.shape[1:])
            loads[3].start()
            running[1] = line_o.steps(at, [dw_o, r.dw_o] + r.line_o)
            yield
            for d in range(1, n_seq):
                go(d).wait()
            do = r.do

            def sum_do(i, carry):
                rows = pl.ds(i * 16, 16)
                total = do_part[0, rows].astype(F32)
                for d in range(1, n_seq):
                    total = total + do_land[d, rows].astype(F32)
                do[rows] = total.astype(BF16)
                return carry

            lax.fori_loop(0, length // 16, sum_do, 0)
            yield
            dqkv = r.dqkv
            masking = [r.pos_col, r.pos_row, r.doc_col, r.doc_row]
            for pair in range(share // 128):
                back_pair(
                    pair, do, r.q, r.k, r.v, r.lse, r.cos, r.sin,
                    dqkv, masking, r.dk, r.dv,
                )
                yield
            loads[3].wait()
            dw_qkv, stage, stage_s = r.dw_qkv, r.dw_stage, r.stage

            def put(j):
                return pltpu.make_async_copy(
                    stage.at[j % 2], dw_qkv.at[pl.ds(j * share, share)], stage_s.at[j % 2]
                )

            for j in range(n_seq):
                if j >= 2:
                    put(j - 2).wait()
                stage[j % 2] = dot(o_here[j], dqkv[...], TN).astype(BF16)
                put(j).start()
                yield
            dn1_part = r.dn1_part
            for j in range(n_seq):
                rows = slice(j * share, (j + 1) * share)
                field = dot(dqkv[...], w_qkv_here[rows], NT).astype(BF16)
                dn1_part[:, :, rows] = field.reshape(n_seq, tok, share)
                yield
            put(n_seq - 2).wait()
            put(n_seq - 1).wait()

        running = {
            0: chain(),
            2: reduces[0].steps(at, [r.g_in[0], r.g_out[0]] + r.reduce_0),
            3: reduces[1].steps(at, [r.g_in[1], r.g_out[1]] + r.reduce_1),
        }
        interleave(BACK_ONE_ORDER, running)

    return rooms.run(body, "back_one", 2, n_seq, n_fsdp)


BACK_TWO_ORDER = [0, 2, 1, 3, 0, 2, 0, 1, 0]


def back_two(
    n_seq, n_fsdp, dn1_part, dw_qkv, dw_o, out_part, middle, source, dh1, gain_a, gain_m_term, grad
):
    tok, model = middle.shape
    rooms = Rooms()
    line = ScatterLine(dw_qkv, n_fsdp, 2, far=True)
    line_out = ScatterLine(out_part, n_fsdp, 2, far=True)
    gain_block = like((n_fsdp, 8, model // n_fsdp), F32)
    line_gain = ScatterLine(gain_block, n_fsdp)
    scatter = ScatterSeq(dn1_part)
    reduce = ReduceSeq(grad.shape, grad.dtype, n_seq)
    spread, spread_o = SpreadSeq(n_seq), SpreadSeq(n_seq)
    gather = GatherSeq(n_seq)
    rooms.take(
        VMEM, dn1_part=dn1_part, middle=middle, source=source, dh1=dh1,
        gain_a=gain_a, gain_m_term=gain_m_term,
    )
    rooms.take(ANY, dw_qkv=dw_qkv, out_part=out_part, dw_o=dw_o, g_in=grad)
    rooms.give(
        ANY,
        g_out=like(grad.shape),
        dw_qkv_all=like((n_seq,) + dw_qkv.shape[1:]),
        dw_o_all=like((n_seq,) + dw_o.shape),
    )
    rooms.give(
        VMEM,
        block_out=like((tok, model)),
        grad_in=like((tok, model)),
        gains=like(gain_block.shape[1:], F32),
    )
    rooms.keep(
        line=line.scratch,
        line_out=line_out.scratch,
        line_gain=line_gain.scratch,
        scatter=scatter.scratch,
        reduce=reduce.scratch,
        spread=spread.scratch,
        spread_o=spread_o.scratch,
        gather=gather.scratch,
        dw_own=room(*dw_qkv.shape[1:]),
        mlp_out=room(tok, model, dtype=F32),
        dn1=room(tok, model, dtype=F32),
        gain_part=room(*gain_block.shape, dtype=F32),
        gain_own=room(*gain_block.shape[1:], dtype=F32),
        gain_all=room(n_seq, *gain_block.shape[1:], dtype=F32),
        gain_sum=room(8, model, dtype=F32),
    )

    def body(at, r):
        def weights():
            yield from line.steps(at, [r.dw_qkv, r.dw_own] + r.line)
            yield from spread.steps(at, [r.dw_own, r.dw_qkv_all] + r.spread)

        def rows_out():
            yield from line_out.steps(at, [r.out_part, r.mlp_out] + r.line_out)
            middle, mlp_out, block_out = r.middle, r.mlp_out, r.block_out

            def add(i, carry):
                rows = pl.ds(i * 16, 16)
                block_out[rows] = (middle[rows] + mlp_out[rows]).astype(BF16)
                return carry

            lax.fori_loop(0, tok // 16, add, 0)

        def rows_in():
            yield from scatter.steps(at, [r.dn1_part, r.dn1] + r.scatter)
            source, dh1, dn1 = r.source, r.dh1, r.dn1
            gain_a, grad_in, gain_sum = r.gain_a, r.grad_in, r.gain_sum
            gain_sum[...] = jnp.zeros_like(gain_sum)

            def norm(i, carry):
                rows = pl.ds(i * 16, 16)
                x, grad = source[rows].astype(F32), dn1[rows]
                scale = lax.rsqrt(jnp.mean(x * x, axis=-1, keepdims=True) + NORM_EPS)
                wide = dh1[rows] + norm_back(grad, x, scale, gain_a[...])
                grad_in[rows] = wide.astype(BF16)
                term = grad * x * scale
                gain_sum[...] += term[:8] + term[8:]
                return carry

            lax.fori_loop(0, tok // 16, norm, 0)
            first = jnp.sum(gain_sum[...], axis=0, keepdims=True)
            second = jnp.sum(r.gain_m_term[...], axis=0, keepdims=True)
            row = lax.broadcasted_iota(jnp.int32, gain_sum.shape, 0)
            both = jnp.where(row == 0, first, jnp.where(row == 1, second, 0.0))
            part, width = r.gain_part, model // n_fsdp
            for f in range(n_fsdp):
                part[f] = both[:, f * width : (f + 1) * width]
            yield
            yield from line_gain.steps(at, [part, r.gain_own] + r.line_gain)
            yield from gather.steps(at, [r.gain_own, r.gain_all] + r.gather)
            total = r.gain_all[0]
            for j in range(1, n_seq):
                total = total + r.gain_all[j]
            r.gains[...] = total

        running = {
            0: weights(),
            1: reduce.steps(at, [r.g_in, r.g_out] + r.reduce),
            2: rows_in(),
            3: spread_o.steps(at, [r.dw_o, r.dw_o_all] + r.spread_o),
            4: rows_out(),
        }
        interleave(BACK_TWO_ORDER, running)

    return rooms.run(body, "back_two", 3, n_seq, n_fsdp)


def widen_mlp_kernel(gate, up, down, out):
    for c, ref in enumerate((gate, up, down)):
        out[c] = ref[...].astype(F32)


def widen_attn_kernel(qkv, o, out):
    n_seq, rows, share = o.shape
    for s in range(n_seq):
        at = pl.ds(s * share, share)
        for c in range(3):
            out[:, c, at] = qkv[s, :, c * share : (c + 1) * share].astype(F32)
        out[:, 3, at] = o[s].astype(F32)


def grid_call(kernel, name, grid, args, in_specs, outs, out_specs, scratch=(), aliases=None):
    return pl.pallas_call(
        kernel,
        grid=grid,
        out_shape=outs,
        in_specs=in_specs,
        out_specs=out_specs,
        scratch_shapes=list(scratch),
        input_output_aliases=aliases or {},
        compiler_params=pltpu.CompilerParams(vmem_limit_bytes=48 * 2**20),
        name=name,
    )(*args)


def angles(positions):
    freqs = ROPE_BASE ** (-jnp.arange(0, HEAD, 2).astype(jnp.float32) / HEAD)
    turn = positions.astype(jnp.float32)[:, None] * freqs[None, :]
    cosine, sine = jnp.cos(turn), jnp.sin(turn)
    return jnp.concatenate([cosine] * 4, 1), jnp.concatenate([-sine, sine] * 2, 1)


def on_device(
    n_seq, n_fsdp,
    hidden_in, gain_attn, attn_weights, gain_mlp, mlp_weights, out_grad, block_slots, doc_ids,
):
    tok, model = hidden_in.shape[1:]
    share = model // n_seq
    block_rows = tok // 2
    within = jnp.arange(block_rows, dtype=jnp.int32)
    slot = block_slots.reshape(-1)
    pos = (slot[:, None] * block_rows + within[None, :]).reshape(-1)
    pick = slot[:, None] == jnp.arange(slot.shape[0], dtype=jnp.int32)[None, :]
    doc = doc_ids[0].reshape(1, -1, block_rows)
    doc = jnp.sum(jnp.where(pick[:, :, None], doc, 0), axis=1).reshape(-1)
    tables = (*angles(pos), pos[:, None], pos[None, :], doc[:, None], doc[None, :])
    start = lax.axis_index("seq") * share
    w_own = lax.dynamic_slice_in_dim(attn_weights, start, share, 2).reshape(-1, 4 * share)
    gains = jnp.concatenate(
        [
            jnp.broadcast_to(gain_attn[None], (16,) + gain_attn.shape),
            jnp.broadcast_to(gain_mlp[None], (16,) + gain_mlp.shape),
        ],
        0,
    )
    mlp_w = mlp_weights.transpose(1, 0, 2)
    a = front(n_seq, n_fsdp, w_own, hidden_in[0], gains, out_grad[0], mlp_w, tables)
    n2_all, grad_all = a.n2_out.reshape(-1, model), a.grad_out.reshape(-1, model)
    w_qkv, w_o = a.w_qkv_out.reshape(model, -1), a.w_o_out.reshape(model, -1)
    grad_down = dot(a.hid, grad_all, TN).astype(BF16)
    grad_gate = dot(a.dg, n2_all, TN).astype(BF16)
    grad_up = dot(a.du, n2_all, TN).astype(BF16)
    dn2_part = (dot(a.dg, mlp_w[0], NN) + dot(a.du, mlp_w[1], NN)).astype(BF16)
    out_part = dot(a.hid, mlp_w[2], NN).astype(BF16)
    b = back_one(
        n_seq, n_fsdp, dn2_part.reshape(n_fsdp, tok, model), a.middle, out_grad[0], a.gain_m,
        w_qkv, w_o, a.o_out, a.n1_out, (a.q, a.k, a.v, a.lse, *tables), (grad_down, grad_gate),
    )
    grad_down, grad_gate = b.g_out
    c = back_two(
        n_seq, n_fsdp, b.dn1_part, b.dw_qkv.reshape(n_fsdp, -1, 3 * share), b.dw_o,
        out_part.reshape(n_fsdp, tok, model), a.middle, hidden_in[0], b.dh1, a.gain_a, b.gain,
        grad_up,
    )
    own_rows, units = b.dw_o.shape[0], grad_up.shape[0]
    step = min(own_rows, 64)
    attn_grad = grid_call(
        widen_attn_kernel,
        "widen_attn",
        (own_rows // step,),
        (c.dw_qkv_all, c.dw_o_all),
        [
            pl.BlockSpec((n_seq, step, 3 * share), lambda i: (0, i, 0)),
            pl.BlockSpec((n_seq, step, share), lambda i: (0, i, 0)),
        ],
        like((own_rows, 4, model), F32),
        pl.BlockSpec((step, 4, model), lambda i: (i, 0, 0)),
    )
    step = min(units, 128)
    mlp_grad = grid_call(
        widen_mlp_kernel,
        "widen_mlp",
        (units // step,),
        (grad_gate, c.g_out, grad_down),
        [pl.BlockSpec((step, model), lambda i: (i, 0))] * 3,
        like((3, units, model), F32),
        pl.BlockSpec((3, step, model), lambda i: (0, i, 0)),
    )
    mlp_grad = mlp_grad.transpose(1, 0, 2)
    return (c.block_out[None], c.grad_in[None], c.gains[0], attn_grad, c.gains[1], mlp_grad)


def solution(mesh):
    return jax.shard_map(
        functools.partial(on_device, mesh.shape["seq"], mesh.shape["fsdp"]),
        mesh=mesh,
        in_specs=(
            P("fsdp", "seq", None),
            P("fsdp"),
            P("fsdp", None, None),
            P("fsdp"),
            P("fsdp", None, None),
            P("fsdp", "seq", None),
            P(),
            P("fsdp", None),
        ),
        out_specs=(
            P("fsdp", "seq", None),
            P("fsdp", "seq", None),
            P("fsdp"),
            P("fsdp", None, None),
            P("fsdp"),
            P("fsdp", None, None),
        ),
        check_vma=False,
    )
```

time: 738 us -> 597 us (0.81)
  matrix products: 120 us -> 41.3 us
  local copies, waits for them, and re-layouts: 69.1 us -> 14.8 us
  Pallas kernels: 483 us -> 528 us
  other arithmetic: 38 us -> 4.46 us
  between operations: 15.4 us -> 1.19 us
    dot_general x15 -> x6, matrix products: 99 us -> 41.3 us  [dot(): return lax.dot_general(a, b, (dims, ((), ())), preferred_element_type=F32)]
    pallas_call x10 -> x5, Pallas kernels: 483 us -> 528 us  [the longest x3 511 us: run(): pl.pallas_call(kernel, out_shape=self.outs, in_specs=self.in_specs, out_s...]
    convert_element_type x5 -> x1, local copies, waits for them, and re-layouts: 23.9 us -> 0.08 us  [angles(): turn = positions.astype(jnp.float32)[:, None] * freqs[None, :]]
    convert_element_type x5 -> x0, other arithmetic: 17.6 us -> none  [the longest x1 14.4 us: on_device(): mlp_grad = lax.psum(mlp_grad, 'seq').astype(F32)]
    dot_general x5 -> x0, matrix products: 12.8 us -> none  [the longest x1 4.95 us: on_device(): dp = jnp.einsum('qhd,khd->hqk', do, v, preferred_element_type=F32)]
    concatenate x1 -> x0, local copies, waits for them, and re-layouts: 12.6 us -> none  [on_device(): dw = jnp.concatenate([dw_qkv, dw_o], 1)]
    sub x1 -> x0, matrix products: 8.35 us -> none  [on_device(): e = jnp.where(allowed, jnp.exp(z - top), 0.0)]
  transfers between devices with their start and end apart: 2 -> 0, of which waited for: 0 -> 0; matrix products, arithmetic and copies ran while one was open for 21% -> 0% of each run, Pallas kernels for 57% -> 0%
where the time goes in v2:
time: 597 us; the launch traced here: 590 us
  Pallas kernels  528 us (88%)
  matrix products  41.3 us (7%)
  local copies, waits for them, and re-layouts  14.8 us (2%)
    pallas_call x3, Pallas kernels, run(): pl.pallas_call(kernel, out_shape=self.outs, in_specs=self.in_specs, out_s...  511 us
    dot_general x6, matrix products, dot(): return lax.dot_general(a, b, (dims, ((), ())), preferred_element_type=F32)  41.3 us
    pallas_call x2, Pallas kernels, grid_call(): pl.pallas_call(kernel, grid=grid, out_shape=outs, in_specs=in_specs, out_...  17.1 us

profile of v2, /device:TPU:8, one launch (start us, length us, event | category | flops | bytes accessed | tf_op | source)
XLA Modules:
  0.0 589.6 jit_solution(9493726302276993107)
XLA Ops:
  0.6 0.5 broadcast.51
  1.2 1.3 reduce.3
  2.5 0.1 broadcast_in_dim.48
  2.6 0.8 copy.25
  3.4 0.1 broadcast_in_dim_reshape.12
  3.4 0.1 iota_compare_fusion
  3.5 0.1 select_reduce_fusion
  3.6 0.7 broadcast_in_dim_reshape.14.refs_7_.refs_12_
  4.3 0.1 iota_add_fusion
  4.3 0.1 convert_element_type.33
  4.4 0.6 add.48.refs_5_.refs_10_
  5.0 0.7 broadcast_in_dim.45
  5.7 0.7 broadcast_in_dim.46
  6.3 0.6 pad_maximum_fusion.2.refs_1_
  7.0 0.9 add.51.refs_4_.refs_9_
  7.9 0.9 broadcast_in_dim_reshape.15.refs_6_.refs_11_
  8.7 1.0 fusion.4
  9.7 1.3 pad_maximum_fusion
  11.0 1.6 constant_dynamic-slice_fusion
  12.6 1.2 copy.31
  13.8 153.2 %front.1 = (bf16[8,256,1536]{2,1,0:T(8,128)(2,1)}, bf16[8,256,512]{2,1,0:T(8,128)(2,1)}, bf16[4,512,512]{2,1,0:T(8,128)(2,1)}, bf16[4,512,512]{2,1,0:T(8,128)(2,...) custom-call(bf16[128,2048]{1,0:T(8,128)(2,1)} %bitcast.55, ...), custom_call_target="tpu_custom_call" | custom-call | tf_op jit(solution)/shard_map/front/pallas_call | solution.py:537
  167.1 0.0 copy-start.8
  167.1 9.6 %convolution_convert_fusion.2.refs_18_ = bf16[1024,2048]{1,0:T(8,128)(2,1)} fusion(bf16[1024,1024]{1,0:T(8,128)(2,1)} %get-tuple-element.47, bf16[1024,2048]{1,0:T(8,128)(2,1)} %bitcast.63), kind=kOutput, calls=%fused_computation.10 | convolution fusion | flops 4297064448 | bytes 10485760 | tf_op jit(solution)/shard_map/dot_general | solution.py:560
  176.7 0.0 copy-done.8
  176.7 8.5 %fusion.3 = bf16[1024,2048]{1,0:T(8,128)(2,1)} fusion(bf16[1024,1024]{1,0:T(8,128)(2,1)S(1)} %copy-done.8, bf16[3,1024,2048]{2,1,0:T(8,128)(2,1)} %bitcast.41), kind=kOutput, calls=%fused_computation.7 | convolution fusion | flops 4297064448 | bytes 10485760 | tf_op jit(solution)/shard_map/dot_general | solution.py:560
  185.2 0.0 copy-done.5
  185.2 0.0 copy-done.7
  185.2 0.0 slice-start
  185.2 0.0 slice-start.1
  185.2 6.3 %convolution_convert_fusion.refs_9_ = bf16[1024,2048]{1,0:T(8,128)(2,1)} fusion(bf16[1024,1024]{1,0:T(8,128)(2,1)S(1)} %copy-done.7, bf16[1024,2048]{1,0:T(8,128)(2,1)S(1)} %bitcast.61), kind=kOutput, calls=%fused_computation.8 | convolution fusion | flops 4297064448 | bytes 10485760 | tf_op jit(solution)/shard_map/dot_general | solution.py:560
  191.5 0.0 copy-done.6
  191.5 6.3 %convolution_convert_fusion.1.refs_19_ = bf16[1024,2048]{1,0:T(8,128)(2,1)} fusion(bf16[1024,1024]{1,0:T(8,128)(2,1)S(1)} %copy-done.6, bf16[1024,2048]{1,0:T(8,128)(2,1)S(1)} %bitcast.62), kind=kOutput, calls=%fused_computation.9 | convolution fusion | flops 4297064448 | bytes 10485760 | tf_op jit(solution)/shard_map/dot_general | solution.py:560
  197.8 0.0 slice-done
  197.8 0.0 slice-done.1
  197.8 0.0 slice-done.2
  197.9 4.5 fusion.1
  202.4 6.0 %add_convert_fusion = bf16[1024,2048]{1,0:T(8,128)(2,1)} fusion(f32[1024,2048]{1,0:T(8,128)S(1)} %fusion.1, bf16[1024,1024]{1,0:T(8,128)(2,1)S(1)} %copy-done.6, bf16[3,1024,2048]{2,1,0:T(8,128)(2,1)S(1)} %bitcast.45), kind=kOutput, calls=%fused_computation | convolution fusion | flops 4299161600 | bytes 18874368 | tf_op jit(solution)/shard_map/dot_general | solution.py:560
  208.4 219.1 %back_one.1 = (bf16[1024,2048]{1,0:T(8,128)(2,1)}, bf16[1024,2048]{1,0:T(8,128)(2,1)}, bf16[2048,1536]{1,0:T(8,128)(2,1)}, f32[128,2048]{1,0:T(8,128)}, f32[8,20...) custom-call(f32[128,2048]{1,0:T(8,128)} %get-tuple-element.35.refs_0_.refs_1_, ...), custom_call_target="tpu_custom_call" | custom-call | tf_op jit(solution)/shard_map/back_one/pallas_call | solution.py:537
  427.5 138.5 %back_two.1 = (bf16[1024,2048]{1,0:T(8,128)(2,1)}, bf16[4,256,1536]{2,1,0:T(8,128)(2,1)}, bf16[4,256,512]{2,1,0:T(8,128)(2,1)}, bf16[128,2048]{1,0:T(8,128)(2,1)...) custom-call(bf16[4,128,2048]{2,1,0:T(8,128)(2,1)} %get-tuple-element.50.refs_0_, ...), custom_call_target="tpu_custom_call" | custom-call | tf_op jit(solution)/shard_map/back_two/pallas_call | solution.py:537
  566.0 1.3 fusion.6
  567.3 1.9 copy-done.1
  569.2 1.2 copy-done.2
  570.4 4.7 widen_attn.1
  575.2 0.0 copy-done
  575.2 12.4 %widen_mlp.1 = f32[3,1024,2048]{2,1,0:T(8,128)} custom-call(bf16[1024,2048]{1,0:T(8,128)(2,1)S(1)} %copy-done, bf16[1024,2048]{1,0:T(8,128)(2,1)} %get-tuple-element.62.up, bf16[1024,2048]{1,0:T(8,128)(2,1)} %get-tuple-element.63.down), custom_call_target="tpu_custom_call" | custom-call | tf_op jit(solution)/shard_map/widen_mlp/pallas_call | solution.py:1206
  587.6 0.8 copy.34
  588.4 0.0 copy-done.3
  588.4 0.8 copy.35
  (13 shorter events, 0.0 us)
Async XLA Ops:
  167.1 9.6 %copy-start.8 = (bf16[1024,1024]{1,0:T(8,128)(2,1)S(1)}, bf16[1024,1024]{1,0:T(8,128)(2,1)}, u32[]{:S(2)}) copy-start(bf16[1024,1024]{1,0:T(8,128)(2,1)} %get-tuple-element.47) | copy-start | bytes 6291460
  176.7 8.5 %copy-start.5 = (bf16[8,128,2048]{2,1,0:T(8,128)(2,1)S(1)}, bf16[8,128,2048]{2,1,0:T(8,128)(2,1)}, u32[]{:S(2)}) copy-start(bf16[8,128,2048]{2,1,0:T(8,128)(2,1)} %get-tuple-element.49) | copy-start | bytes 12582916
  176.7 8.5 %copy-start.7 = (bf16[1024,1024]{1,0:T(8,128)(2,1)S(1)}, bf16[1024,1024]{1,0:T(8,128)(2,1)}, u32[]{:S(2)}) copy-start(bf16[1024,1024]{1,0:T(8,128)(2,1)} %get-tuple-element.42) | copy-start | bytes 6291460
  185.2 6.3 %copy-start.6 = (bf16[1024,1024]{1,0:T(8,128)(2,1)S(1)}, bf16[1024,1024]{1,0:T(8,128)(2,1)}, u32[]{:S(2)}) copy-start(bf16[1024,1024]{1,0:T(8,128)(2,1)} %get-tuple-element.41) | copy-start | bytes 6291460
  185.2 12.6 %slice-start = ((s8[12582912]{0:T(1024)(128)(4,1)}), s8[4194304]{0:T(1024)(128)(4,1)S(1)}, s32[]{:S(2)}) async-start(s8[12582912]{0:T(1024)(128)(4,1)} %bitcast.42), calls=%async_computation | async-start | bytes 8388608
  185.2 12.6 %slice-start.1 = ((s8[12582912]{0:T(1024)(128)(4,1)}), s8[4194304]{0:T(1024)(128)(4,1)S(1)}, s32[]{:S(2)}) async-start(s8[12582912]{0:T(1024)(128)(4,1)} %bitcast.42), calls=%async_computation.1 | async-start | bytes 8388608
  191.5 6.3 %slice-start.2 = ((s8[12582912]{0:T(1024)(128)(4,1)}), s8[4194304]{0:T(1024)(128)(4,1)S(1)}, s32[]{:S(2)}) async-start(s8[12582912]{0:T(1024)(128)(4,1)} %bitcast.42), calls=%async_computation.2 | async-start | bytes 8388608
  567.3 1.9 copy-start.1
  569.2 1.2 copy-start.2
  570.4 4.7 copy-start
  575.2 12.4 %copy-start.4 = (bf16[128,2048]{1,0:T(8,128)(2,1)S(1)}, bf16[128,2048]{1,0:T(8,128)(2,1)}, u32[]{:S(2)}) copy-start(bf16[128,2048]{1,0:T(8,128)(2,1)} %get-tuple-element.56) | copy-start | bytes 1572868
  575.2 13.2 %copy-start.3 = (bf16[128,2048]{1,0:T(8,128)(2,1)S(1)}, bf16[128,2048]{1,0:T(8,128)(2,1)}, u32[]{:S(2)}) copy-start(bf16[128,2048]{1,0:T(8,128)(2,1)} %get-tuple-element.57) | copy-start | bytes 1572868

commit v3 on v2

--- a/solution.py
+++ b/solution.py
@@ -1,4 +1,5 @@
 import functools
+import math
 import types
 
 import jax
@@ -274,57 +275,93 @@
             go(d).wait()
 
 
-class ScatterSeq:
-    def __init__(self, part):
-        self.scratch = [pltpu.VMEM(part.shape, part.dtype), DMA(part.shape[:1]), DMA(part.shape[:1])]
-
-    def steps(self, at, refs):
-        part, o, land, s_sem, r_sem = refs
-        rows = part.shape[1]
-        tile = 16 if rows % 16 == 0 else rows
-
-        def go(d):
-            peer = at.peer(d)
-            return send(part.at[peer[0]], land.at[d], s_sem.at[d], r_sem.at[d], peer)
-
-        for d in reversed(range(1, at.n_seq)):
-            go(d).start()
+class HalveSeq:
+    def __init__(self, shape, dtype, n_seq):
+        n, rows, cols = shape
+        bits = n_seq.bit_length() - 1
+        self.half = rows // 2
+        self.orders = [[(i + p) % bits for i in range(bits)] for p in range(2)]
+        self.scratch = [
+            pltpu.VMEM((2, n - 1, self.half, cols), dtype), DMA((2, n - 1)), DMA((2, n - 1))
+        ]
+
+    def masks(self, p, i):
+        out = [0]
+        for b in self.orders[p][i + 1 :]:
+            out += [m | (1 << b) for m in out]
+        return out
+
+    def slot(self, p, i, u):
+        return sum(len(self.masks(p, j)) for j in range(i)) + self.masks(p, i).index(u)
+
+    def steps(self, at, part, o, refs):
+        land, s_sem, r_sem = refs
+        half, bits = self.half, len(self.orders[0])
+        tile = 16 if half % 16 == 0 else half
+
+        def go(p, i, u):
+            b = 1 << self.orders[p][i]
+            if i == 0:
+                src = part.at[b | u, pl.ds(p * half, half)]
+            else:
+                src = land.at[p, self.slot(p, 0, b | u)]
+            n = self.slot(p, i, u)
+            return send(src, land.at[p, n], s_sem.at[p, n], r_sem.at[p, n], at.peer(b))
+
+        def add(p, u, upto, out, first):
+            def body(k, carry):
+                rows = pl.ds(pl.multiple_of(k * tile, tile), tile)
+                total = part[u, pl.ds(pl.multiple_of(p * half + k * tile, tile), tile)].astype(F32)
+                for i in range(upto):
+                    total = total + land[p, self.slot(p, i, u), rows].astype(F32)
+                out[pl.ds(pl.multiple_of(first + k * tile, tile), tile)] = total.astype(out.dtype)
+                return carry
+
+            lax.fori_loop(0, half // tile, body, 0)
+
+        for p in range(2):
+            for u in self.masks(p, 0):
+                go(p, 0, u).start()
         yield
-        for d in range(1, at.n_seq):
-            go(d).wait()
-
-        def body(i, carry):
-            at_rows = pl.ds(i * tile, tile)
-            total = part[at.s, at_rows].astype(F32)
-            for d in range(1, at.n_seq):
-                total = total + land[d, at_rows].astype(F32)
-            o[at_rows] = total.astype(o.dtype)
-            return carry
-
-        lax.fori_loop(0, rows // tile, body, 0)
+        for i in range(bits):
+            for p in range(2):
+                for u in self.masks(p, i):
+                    go(p, i, u).wait_recv()
+                if i + 1 < bits:
+                    b = 1 << self.orders[p][i + 1]
+                    for u in self.masks(p, i + 1):
+                        add(p, b | u, i + 1, land.at[p, self.slot(p, 0, b | u)], 0)
+                        go(p, i + 1, u).start()
+                else:
+                    add(p, 0, bits, o, p * half)
+            yield
+        for p in range(2):
+            for i in range(bits):
+                for u in self.masks(p, i):
+                    go(p, i, u).wait_send()
 
 
 class ReduceSeq:
-    def __init__(self, shape, dtype, n_seq):
+    def __init__(self, shape, dtype, n_seq, parts=4):
         rows, cols = shape
-        self.bits = n_seq.bit_length() - 1
-        self.rows = rows // 2
+        self.bits, self.parts = n_seq.bit_length() - 1, parts
+        self.rows = rows // parts
         self.room = self.rows - (self.rows >> self.bits)
         self.scratch = [
             pltpu.VMEM(shape, dtype),
-            pltpu.VMEM((2 * self.room, cols), dtype),
-            DMA((2,)),
-            DMA((2, self.bits)),
-            DMA((2, self.bits)),
-            DMA((2, n_seq)),
-            DMA((2, n_seq)),
-            DMA((2,)),
+            pltpu.VMEM((parts * self.room, cols), dtype),
+            DMA((parts,)),
+            DMA((parts, self.bits)),
+            DMA((parts, self.bits)),
+            DMA((parts, n_seq)),
+            DMA((parts, n_seq)),
+            DMA((parts,)),
         ]
 
-    def steps(self, at, refs):
+    def steps(self, at, refs, fill=None):
         g_in, o, g, land, load_s, rs_s, rs_r, ag_s, ag_r, own_s = refs
-        bits = self.bits
-        orders = [[(i + p) % bits for i in range(bits)] for p in range(2)]
+        bits, parts = self.bits, range(self.parts)
+        orders = [[(i + p) % bits for i in range(bits)] for p in parts]
         mult = self.rows >> bits
 
         def bit(t, b):
@@ -395,14 +432,18 @@
             piece = pl.ds(base(p, at.s, bits), mult)
             return pltpu.make_async_copy(g.at[piece], o.at[piece], own_s.at[p])
 
-        for p in range(2):
-            load(p).start()
-        for p in range(2):
-            load(p).wait()
+        if g_in is not None:
+            for p in parts:
+                load(p).start()
+        for p in parts:
+            if g_in is not None:
+                load(p).wait()
+            if fill is not None:
+                fill(p * self.rows, self.rows)
             halve(p, 0).start()
         yield
         for i in range(bits):
-            for p in range(2):
+            for p in parts:
                 halve(p, i).wait_recv()
                 add(p, i)
                 if i + 1 < bits:
@@ -413,14 +454,14 @@
                     own(p).start()
                 yield
         for j in range(bits):
-            for p in range(2):
+            for p in parts:
                 for mask in masks(p, j):
                     arrive(p, j, mask).wait_recv()
                     came = (1 << orders[p][bits - 1 - j]) | mask
                     for later in range(j + 1, bits):
                         double(p, later, came).start()
                 yield
-        for p in range(2):
+        for p in parts:
             own(p).wait()
             for i in range(bits):
                 halve(p, i).wait_send()
@@ -626,8 +667,46 @@
     return lax.rsqrt(jnp.mean(value * value, axis=-1, keepdims=True) + NORM_EPS)
 
 
-def front(n_seq, n_fsdp, w_own, hidden, gains, out_grad, mlp_w, tables):
-    cos, sin, pos_col, pos_row, doc_col, doc_row = tables
+def fill_tables(slots, docs, r):
+    length = docs.shape[1]
+    block = length // (2 * slots.shape[0])
+
+    def place(shape, axis):
+        i = lax.broadcasted_iota(jnp.int32, shape, axis)
+        slot = jnp.zeros(shape, jnp.int32)
+        for j in range(2 * slots.shape[0]):
+            slot = jnp.where(i // block == j, slots[j // 2, j % 2], slot)
+        return slot * block + i % block
+
+    r.pos_col[...] = place((length, 1), 0)
+    r.pos_row[...] = place((1, length), 1)
+    lane = lax.broadcasted_iota(jnp.int32, (1, 128), 1)
+    half = HEAD // 2
+    steps = (lane % half).astype(F32) / half
+    freqs = jnp.exp(steps * -math.log(ROPE_BASE))
+    sign = jnp.where(lane % HEAD < half, -1.0, 1.0)
+    r.doc_row[...] = jnp.zeros((1, length), jnp.int32)
+
+    def body(i, carry):
+        rows = pl.ds(pl.multiple_of(i * 128, 128), 128)
+        pos = r.pos_col[rows]
+        turn = pos.astype(F32) * freqs
+        r.cos[rows] = jnp.cos(turn)
+        r.sin[rows] = jnp.sin(turn) * sign
+        at = lax.broadcasted_iota(jnp.int32, (128, length), 1)
+        own = jnp.sum(jnp.where(at == pos, docs[...], 0), axis=1, keepdims=True)
+        r.doc_col[rows] = own
+        here = lax.broadcasted_iota(jnp.int32, (128, length), 0) + i * 128
+        r.doc_row[...] += jnp.sum(jnp.where(at == here, own, 0), axis=0, keepdims=True)
+        return carry
+
+    lax.fori_loop(0, length // 128, body, 0)
+
+
+FRONT_ORDER = [0, 0, 0, 1, 0, 0, 1, 0, 1, 0, 1, 0, 1, 1, 2, 0, 0, 2, 0, 0, 0, 0, 2, 0, 2, 0]
+
+
+def front(n_seq, n_fsdp, w_own, hidden, own_gains, out_grad, mlp_w, slots, docs):
     tok, model = hidden.shape
     length, share = n_seq * tok, w_own.shape[1] // 4
     line, rows_f, units = n_fsdp // 2, w_own.shape[0], mlp_w.shape[1]
@@ -639,10 +718,8 @@
     get_gain, get_grad, get_n2 = GatherLine(n_fsdp), GatherLine(n_fsdp, 2), GatherLine(n_fsdp, 2)
     get_x = GatherSeq(n_seq)
     rooms = Rooms()
-    rooms.take(
-        VMEM, hidden=hidden, gains=gains, cos=cos, sin=sin,
-        pos_col=pos_col, pos_row=pos_row, doc_col=doc_col, doc_row=doc_row,
-    )
+    rooms.take(VMEM, hidden=hidden, own_gains=own_gains, docs=docs)
+    rooms.take(pl.BlockSpec(memory_space=pltpu.SMEM), slots=slots)
     rooms.take(ANY, w_own=w_own, out_grad=out_grad, mlp_w=mlp_w)
     rooms.give(
         ANY,
@@ -665,13 +742,20 @@
         middle=like((tok, model), F32),
         gain_a=like((1, model), F32),
         gain_m=like((1, model), F32),
+        cos=like((length, 128), F32),
+        sin=like((length, 128), F32),
+        pos_col=like((length, 1), jnp.int32),
+        pos_row=like((1, length), jnp.int32),
+        doc_col=like((length, 1), jnp.int32),
+        doc_row=like((1, length), jnp.int32),
     )
     rooms.keep(
+        gains=room(32, rows_f),
         get_w=get_w.scratch, get_o=get_o.scratch, get_gain=get_gain.scratch,
         get_grad=get_grad.scratch, get_n2=get_n2.scratch, get_x=get_x.scratch,
         w_qkv_all=room(*qkv_shape),
         w_o_all=room(*o_shape),
-        gains_all=room(n_fsdp, *gains.shape),
+        gains_all=room(n_fsdp, 32, rows_f),
         x_all=room(n_seq, tok, model),
         n1=room(n_fsdp, length, rows_f),
         o_all=room(n_seq, length, share),
@@ -787,7 +871,12 @@
             for one in loads:
                 one.start()
             r.act[...] = jnp.zeros_like(r.act)
-            for _ in get_gain.steps(at, r.gains, r.gains_all, r.get_gain):
+            for i, gain in enumerate(r.own_gains):
+                r.gains[16 * i : 16 * i + 16] = jnp.broadcast_to(gain[...], (16, rows_f))
+            gain_steps = get_gain.steps(at, r.gains, r.gains_all, r.get_gain)
+            next(gain_steps)
+            fill_tables(r.slots, r.docs, r)
+            for _ in gain_steps:
                 pass
             for f in range(n_fsdp):
                 cols = slice(f * rows_f, (f + 1) * rows_f)
@@ -879,17 +968,22 @@
                 yield
 
         def cotangents():
+            blocks = get_grad.steps(at, r.out_grad, r.grad_all, r.get_grad, grad_of)
+            next(blocks)
+            yield
+            next(blocks)
+            yield
             while not projected:
                 yield
             loads[2].wait()
-            yield from get_grad.steps(at, r.out_grad, r.grad_all, r.get_grad, grad_of)
+            for _ in blocks:
+                yield
             save(r.grad_all, r.grad_out)
 
         projected = []
         out_weights = get_o.steps(at, w_o, r.w_o_all, r.get_o)
         grads = cotangents()
-        order = [0, 0, 0, 1, 0, 0, 1, 0, 1, 0, 1, 0, 1, 1, 2, 0, 0, 2, 0, 0, 0, 0, 2, 0, 2, 0]
-        interleave(order, {0: chain(), 1: out_weights, 2: grads})
+        interleave(FRONT_ORDER, {0: chain(), 1: out_weights, 2: grads})
         for pair in range(n_pairs):
             for d in range(1, n_seq):
                 go_o(pair, d, at.s).wait_send()
@@ -903,45 +997,176 @@
     return rooms.run(body, "front", 1, n_seq, n_fsdp)
 
 
-BACK_ONE_ORDER = [2, 0, 0, 0, 3]
-
-
-def back_one(n_seq, n_fsdp, dn2_part, middle, out_grad, gain_m, w_qkv, w_o, o_all, n1, saved, grads):
+MIDDLE_ORDER = [0, 0, 1, 1, 2, 2, 2, 2, 0, 1, 1, 2, 2, 0, 1, 1, 2, 2, 0, 1, 1, 0, 1, 1]
+
+
+def middle(n_seq, n_fsdp, hid, dg, du, n2_all, grad_all, mlp_w, h1, out_grad, gain_m):
+    tok, model = h1.shape
+    tokens, units = hid.shape
+    share, length, line = model // n_seq, n_seq * tok, n_fsdp // 2
+    step = min(256, units)
+    rooms = Rooms()
+    rooms.take(VMEM, h1=h1, out_grad=out_grad, gain_m=gain_m)
+    rooms.take(ANY, far=[hid, grad_all, dg, du, n2_all], mlp_w=mlp_w)
+    rooms.give(
+        ANY,
+        grad_down=like((units, model)),
+        grads=[like((units, model))] * 2,
+        out_part=like((n_fsdp, tok, model)),
+    )
+    rooms.give(
+        VMEM, dh1=like((tok, model), F32), gain=like((8, model), F32), da_cols=like((length, share))
+    )
+    scatter = ScatterLine(like((n_fsdp, tok, model)), n_fsdp, 2)
+    reduce = ReduceSeq((units, model), BF16, n_seq)
+    rooms.keep(
+        scatter=scatter.scratch,
+        reduce=reduce.scratch,
+        near=[room(*x.shape) for x in (hid, grad_all, dg, du, n2_all)],
+        weights=[room(units, model)] * 3,
+        dn2_part=room(n_fsdp, tok, model),
+        dn2=room(tok, model, dtype=F32),
+        da=room(tok, model),
+        stage=room(2, 2 * tok, model),
+        load=DMA((8,)),
+        stage_s=DMA((2,)),
+        swap=[DMA((n_seq,)), DMA((n_seq,))],
+    )
+
+    def body(at, r):
+        hid, grad_all, dg, du, n2_all = r.near
+        gate_w, up_w, down_w = r.weights
+        loads = [
+            pltpu.make_async_copy(a, b, r.load.at[i])
+            for i, (a, b) in enumerate(
+                list(zip(r.far, r.near)) + [(r.mlp_w.at[i], w) for i, w in enumerate(r.weights)]
+            )
+        ]
+
+        def ready(*which):
+            for i in which:
+                loads[i].wait()
+
+        def to_grad(act, rows_in, i):
+            return dot(act[:, i : i + step], rows_in[...].reshape(tokens, model), TN).astype(BF16)
+
+        def chain():
+            for i in (0, 1, 2, 3, 5, 6, 4, 7):
+                loads[i].start()
+            ready(0, 1)
+            next(down)
+            yield
+            ready(2, 3, 5, 6)
+            for b in range(line):
+                rows = slice(2 * tok * b, 2 * tok * (b + 1))
+                part = dot(dg[rows], gate_w[...], NN) + dot(du[rows], up_w[...], NN)
+                r.dn2_part[2 * b : 2 * b + 2] = part.astype(BF16).reshape(2, tok, model)
+            yield from scatter.steps(at, [r.dn2_part, r.dn2] + r.scatter)
+            h1, out_grad, gain_m = r.h1, r.out_grad, r.gain_m
+            dn2, dh1, da, gain = r.dn2, r.dh1, r.da, r.gain
+            gain[...] = jnp.zeros_like(gain)
+
+            def norm(i, carry):
+                rows = pl.ds(i * 16, 16)
+                h, grad = h1[rows], dn2[rows]
+                scale = lax.rsqrt(jnp.mean(h * h, axis=-1, keepdims=True) + NORM_EPS)
+                wide = out_grad[rows].astype(F32) + norm_back(grad, h, scale, gain_m[...])
+                dh1[rows] = wide
+                da[rows] = wide.astype(BF16)
+                term = grad * h * scale
+                gain[...] += term[:8] + term[8:]
+                return carry
+
+            lax.fori_loop(0, tok // 16, norm, 0)
+            da_cols = r.da_cols
+            swap_s, swap_r = r.swap
+
+            def swap(d):
+                peer = at.peer(d)
+                cols = pl.ds(pl.multiple_of(peer[0] * share, 128), share)
+                rows = pl.ds(pl.multiple_of(at.s * tok, tok), tok)
+                return send(da.at[:, cols], da_cols.at[rows], swap_s.at[d], swap_r.at[d], peer)
+
+            for d in reversed(range(1, n_seq)):
+                swap(d).start()
+            cols = pl.ds(pl.multiple_of(at.s * share, 128), share)
+            rows = pl.ds(pl.multiple_of(at.s * tok, tok), tok)
+            da_cols[rows] = da[:, cols]
+            yield
+            for d in range(1, n_seq):
+                swap(d).wait()
+
+        def products():
+            ready(4, 7)
+            jobs = [(r.grads[0], dg, n2_all, i) for i in range(0, units, step)]
+            jobs += [(r.grads[1], du, n2_all, i) for i in range(0, units, step)]
+            jobs += [(None, None, None, b) for b in range(line)]
+            waiting = [None, None]
+            for n, (out, act, rows_in, i) in enumerate(jobs):
+                if waiting[n % 2] is not None:
+                    waiting[n % 2].wait()
+                if out is None:
+                    rows = slice(2 * tok * i, 2 * tok * (i + 1))
+                    r.stage[n % 2] = dot(hid[rows], down_w[...], NN).astype(BF16)
+                    src = r.stage.at[n % 2].reshape(2, tok, model)
+                    dst = r.out_part.at[pl.ds(2 * i, 2)]
+                else:
+                    r.stage[n % 2, :step] = to_grad(act, rows_in, i)
+                    src, dst = r.stage.at[n % 2, pl.ds(0, step)], out.at[pl.ds(i, step)]
+                waiting[n % 2] = pltpu.make_async_copy(src, dst, r.stage_s.at[n % 2])
+                waiting[n % 2].start()
+                yield
+            for one in waiting:
+                one.wait()
+
+        def fill(low, rows):
+            part = hid[:, low : low + rows]
+            rows_in = grad_all[...].reshape(tokens, model)
+            r.reduce[0][low : low + rows] = dot(part, rows_in, TN).astype(BF16)
+
+        down = reduce.steps(at, [None, r.grad_down] + r.reduce, fill)
+        interleave(MIDDLE_ORDER, {0: chain(), 1: down, 2: products()})
+
+    return rooms.run(body, "middle", 4, n_seq, n_fsdp)
+
+
+BACK_ONE_ORDER = [2, 0, 3, 0, 1, 2, 2, 3, 2, 2, 1, 0, 2, 2, 3, 2, 0, 2, 1, 0, 2, 0, 2, 3, 0, 2, 0, 2]
+BACK_ONE_ORDER += [0, 1, 2, 0, 2, 3, 0, 2, 0, 2, 0]
+
+
+def back_one(n_seq, n_fsdp, da_cols, w_qkv, w_o, o_all, n1, saved, out_part, h1, grad):
     q, k, v, lse, cos, sin, pos_col, pos_row, doc_col, doc_row = saved
-    tok, model = middle.shape
-    length, share = q.shape
+    (length, share), model = q.shape, w_qkv.shape[0]
+    tok = length // n_seq
     rooms = Rooms()
     rooms.take(
-        VMEM, middle=middle, out_grad=out_grad, gain_m=gain_m, q=q, k=k, v=v, lse=lse,
+        VMEM, da_cols=da_cols, h1=h1, q=q, k=k, v=v, lse=lse,
         cos=cos, sin=sin, pos_col=pos_col, pos_row=pos_row, doc_col=doc_col, doc_row=doc_row,
     )
-    rooms.take(ANY, dn2_part=dn2_part, w_qkv=w_qkv, w_o=w_o, o_all=o_all, n1=n1, g_in=grads)
-    rooms.give(ANY, g_out=[like(g.shape) for g in grads], dw_qkv=like((model, 3 * share)))
+    rooms.take(ANY, w_qkv=w_qkv, w_o=w_o, o_all=o_all, n1=n1, out_part=out_part, g_in=grad)
+    rooms.give(ANY, g_out=like(grad.shape), dw_qkv=like((model, 3 * share)))
     rooms.give(
         VMEM,
-        dh1=like((tok, model), F32),
-        gain=like((8, model), F32),
         dn1_part=like((n_seq, tok, model)),
         dw_o=like((model // n_fsdp, share)),
-    )
-    line = ScatterLine(dn2_part, n_fsdp, 2, far=True)
+        block_out=like((tok, model)),
+    )
     o_block = like((n_fsdp, model // n_fsdp, share))
     line_o = ScatterLine(o_block, n_fsdp)
-    reduces = [ReduceSeq(g.shape, g.dtype, n_seq) for g in grads]
+    halve = HalveSeq((n_seq, length, share), BF16, n_seq)
+    line_out = ScatterLine(out_part, n_fsdp, 2, far=True)
+    reduce = ReduceSeq(grad.shape, grad.dtype, n_seq)
     rooms.keep(
-        line=line.scratch,
         line_o=line_o.scratch,
-        reduce_0=reduces[0].scratch,
-        reduce_1=reduces[1].scratch,
+        line_out=line_out.scratch,
+        mlp_out=room(tok, model, dtype=F32),
+        reduce=reduce.scratch,
         dw_o_part=room(*o_block.shape),
-        dn2=room(tok, model, dtype=F32),
-        da=room(tok, model),
-        da_cols=room(length, share),
         w_qkv_here=room(*w_qkv.shape),
         w_o_here=room(*w_o.shape),
         o_here=room(*o_all.shape),
         do_part=room(n_seq, length, share),
-        do_land=room(n_seq, length, share),
+        halve=halve.scratch,
         do=room(length, share),
         dqkv=room(length, 3 * share),
         dk=room(length, 128, dtype=F32),
@@ -949,8 +1174,6 @@
         dw_stage=room(2, share, 3 * share),
         load=DMA((4,)),
         stage=DMA((2,)),
-        swap=[DMA((n_seq,)), DMA((n_seq,))],
-        do_sem=[DMA((n_seq,)), DMA((n_seq,))],
     )
 
     def body(at, r):
@@ -961,59 +1184,19 @@
                     ((r.w_qkv, r.w_qkv_here), (r.w_o, r.w_o_here), (r.o_all, r.o_here), (r.n1, r.o_here))
                 )
             ]
-            for one in loads[:3]:
-                one.start()
-            yield from line.steps(at, [r.dn2_part, r.dn2] + r.line)
-            middle, out_grad, gain_m = r.middle, r.out_grad, r.gain_m
-            dn2, dh1, da, gain = r.dn2, r.dh1, r.da, r.gain
-            gain[...] = jnp.zeros_like(gain)
-
-            def norm(i, carry):
-                rows = pl.ds(i * 16, 16)
-                h, grad = middle[rows], dn2[rows]
-                scale = lax.rsqrt(jnp.mean(h * h, axis=-1, keepdims=True) + NORM_EPS)
-                wide = out_grad[rows].astype(F32) + norm_back(grad, h, scale, gain_m[...])
-                dh1[rows] = wide
-                da[rows] = wide.astype(BF16)
-                term = grad * h * scale
-                gain[...] += term[:8] + term[8:]
-                return carry
-
-            lax.fori_loop(0, tok // 16, norm, 0)
+            for i in (1, 2, 0):
+                loads[i].start()
+            loads[1].wait()
             da_cols = r.da_cols
-            swap_s, swap_r = r.swap
-
-            def swap(d):
-                peer = at.peer(d)
-                cols = pl.ds(pl.multiple_of(peer[0] * share, 128), share)
-                rows = pl.ds(pl.multiple_of(at.s * tok, tok), tok)
-                return send(da.at[:, cols], da_cols.at[rows], swap_s.at[d], swap_r.at[d], peer)
-
-            for d in reversed(range(1, n_seq)):
-                swap(d).start()
-            cols = pl.ds(pl.multiple_of(at.s * share, 128), share)
-            rows = pl.ds(pl.multiple_of(at.s * tok, tok), tok)
-            da_cols[rows] = da[:, cols]
-            for one in loads[:3]:
-                one.wait()
-            yield
-            for d in range(1, n_seq):
-                swap(d).wait()
             w_qkv_here, w_o_here, o_here = r.w_qkv_here, r.w_o_here, r.o_here
-            do_part, do_land = r.do_part, r.do_land
-            do_s, do_r = r.do_sem
-
-            def go(d):
-                return send(
-                    do_part.at[d], do_land.at[d], do_s.at[d], do_r.at[d], at.peer(d)
-                )
-
+            do_part = r.do_part
             for d in reversed(range(n_seq)):
                 rows = pl.ds(pl.multiple_of(at.peer(d)[0] * share, share), share)
                 do_part[d] = dot(da_cols[...], w_o_here[rows], NT).astype(BF16)
-                if d:
-                    go(d).start()
-            yield
+            exchange = halve.steps(at, do_part, r.do, r.halve)
+            next(exchange)
+            yield
+            loads[2].wait()
             dw_o = r.dw_o_part
             per = n_fsdp // n_seq
             for j in range(n_seq):
@@ -1022,20 +1205,9 @@
             loads[3].start()
             running[1] = line_o.steps(at, [dw_o, r.dw_o] + r.line_o)
             yield
-            for d in range(1, n_seq):
-                go(d).wait()
+            for _ in exchange:
+                yield
             do = r.do
-
-            def sum_do(i, carry):
-                rows = pl.ds(i * 16, 16)
-                total = do_part[0, rows].astype(F32)
-                for d in range(1, n_seq):
-                    total = total + do_land[d, rows].astype(F32)
-                do[rows] = total.astype(BF16)
-                return carry
-
-            lax.fori_loop(0, length // 16, sum_do, 0)
-            yield
             dqkv = r.dqkv
             masking = [r.pos_col, r.pos_row, r.doc_col, r.doc_row]
             for pair in range(share // 128):
@@ -1058,46 +1230,59 @@
                 stage[j % 2] = dot(o_here[j], dqkv[...], TN).astype(BF16)
                 put(j).start()
                 yield
+            loads[0].wait()
             dn1_part = r.dn1_part
             for j in range(n_seq):
                 rows = slice(j * share, (j + 1) * share)
                 field = dot(dqkv[...], w_qkv_here[rows], NT).astype(BF16)
-                dn1_part[:, :, rows] = field.reshape(n_seq, tok, share)
+                for i in range(n_seq):
+                    dn1_part[jnp.bitwise_xor(at.s, i), :, rows] = field[i * tok : (i + 1) * tok]
                 yield
             put(n_seq - 2).wait()
             put(n_seq - 1).wait()
 
+        def rows_out():
+            yield from line_out.steps(at, [r.out_part, r.mlp_out] + r.line_out)
+            h1, mlp_out, block_out = r.h1, r.mlp_out, r.block_out
+
+            def add(i, carry):
+                rows = pl.ds(i * 16, 16)
+                block_out[rows] = (h1[rows] + mlp_out[rows]).astype(BF16)
+                return carry
+
+            lax.fori_loop(0, tok // 16, add, 0)
+
         running = {
             0: chain(),
-            2: reduces[0].steps(at, [r.g_in[0], r.g_out[0]] + r.reduce_0),
-            3: reduces[1].steps(at, [r.g_in[1], r.g_out[1]] + r.reduce_1),
+            3: rows_out(),
+            2: reduce.steps(at, [r.g_in, r.g_out] + r.reduce),
         }
         interleave(BACK_ONE_ORDER, running)
 
     return rooms.run(body, "back_one", 2, n_seq, n_fsdp)
 
 
-BACK_TWO_ORDER = [0, 2, 1, 3, 0, 2, 0, 1, 0]
+BACK_TWO_ORDER = [0, 2, 1, 3, 0, 2, 1, 1, 3, 2, 1, 1, 0, 2, 2, 1, 1, 2, 1, 1, 2, 0, 2, 1, 1, 0, 0, 2, 2]
+BACK_TWO_ORDER += [1, 1, 1, 1, 3, 3, 0, 1, 1, 0]
 
 
 def back_two(
-    n_seq, n_fsdp, dn1_part, dw_qkv, dw_o, out_part, middle, source, dh1, gain_a, gain_m_term, grad
+    n_seq, n_fsdp, dn1_part, dw_qkv, dw_o, source, dh1, gain_a, gain_m_term, grad
 ):
-    tok, model = middle.shape
+    tok, model = source.shape
     rooms = Rooms()
     line = ScatterLine(dw_qkv, n_fsdp, 2, far=True)
-    line_out = ScatterLine(out_part, n_fsdp, 2, far=True)
     gain_block = like((n_fsdp, 8, model // n_fsdp), F32)
     line_gain = ScatterLine(gain_block, n_fsdp)
-    scatter = ScatterSeq(dn1_part)
+    scatter = HalveSeq(dn1_part.shape, BF16, n_seq)
     reduce = ReduceSeq(grad.shape, grad.dtype, n_seq)
     spread, spread_o = SpreadSeq(n_seq), SpreadSeq(n_seq)
     gather = GatherSeq(n_seq)
     rooms.take(
-        VMEM, dn1_part=dn1_part, middle=middle, source=source, dh1=dh1,
+        VMEM, dn1_part=dn1_part, source=source, dh1=dh1,
         gain_a=gain_a, gain_m_term=gain_m_term,
     )
-    rooms.take(ANY, dw_qkv=dw_qkv, out_part=out_part, dw_o=dw_o, g_in=grad)
+    rooms.take(ANY, dw_qkv=dw_qkv, dw_o=dw_o, g_in=grad)
     rooms.give(
         ANY,
         g_out=like(grad.shape),
@@ -1106,13 +1291,11 @@
     )
     rooms.give(
         VMEM,
-        block_out=like((tok, model)),
         grad_in=like((tok, model)),
         gains=like(gain_block.shape[1:], F32),
     )
     rooms.keep(
         line=line.scratch,
-        line_out=line_out.scratch,
         line_gain=line_gain.scratch,
         scatter=scatter.scratch,
         reduce=reduce.scratch,
@@ -1120,7 +1303,6 @@
         spread_o=spread_o.scratch,
         gather=gather.scratch,
         dw_own=room(*dw_qkv.shape[1:]),
-        mlp_out=room(tok, model, dtype=F32),
         dn1=room(tok, model, dtype=F32),
         gain_part=room(*gain_block.shape, dtype=F32),
         gain_own=room(*gain_block.shape[1:], dtype=F32),
@@ -1133,19 +1315,8 @@
             yield from line.steps(at, [r.dw_qkv, r.dw_own] + r.line)
             yield from spread.steps(at, [r.dw_own, r.dw_qkv_all] + r.spread)
 
-        def rows_out():
-            yield from line_out.steps(at, [r.out_part, r.mlp_out] + r.line_out)
-            middle, mlp_out, block_out = r.middle, r.mlp_out, r.block_out
-
-            def add(i, carry):
-                rows = pl.ds(i * 16, 16)
-                block_out[rows] = (middle[rows] + mlp_out[rows]).astype(BF16)
-                return carry
-
-            lax.fori_loop(0, tok // 16, add, 0)
-
         def rows_in():
-            yield from scatter.steps(at, [r.dn1_part, r.dn1] + r.scatter)
+            yield from scatter.steps(at, r.dn1_part, r.dn1, r.scatter)
             source, dh1, dn1 = r.source, r.dh1, r.dn1
             gain_a, grad_in, gain_sum = r.gain_a, r.grad_in, r.gain_sum
             gain_sum[...] = jnp.zeros_like(gain_sum)
@@ -1181,25 +1352,24 @@
             1: reduce.steps(at, [r.g_in, r.g_out] + r.reduce),
             2: rows_in(),
             3: spread_o.steps(at, [r.dw_o, r.dw_o_all] + r.spread_o),
-            4: rows_out(),
         }
         interleave(BACK_TWO_ORDER, running)
 
     return rooms.run(body, "back_two", 3, n_seq, n_fsdp)
 
 
-def widen_mlp_kernel(gate, up, down, out):
+def finish_kernel(gate, up, down, qkv, o, rows_out, rows_in, gains, mlp, attn, out, back, gain):
     for c, ref in enumerate((gate, up, down)):
-        out[c] = ref[...].astype(F32)
-
-
-def widen_attn_kernel(qkv, o, out):
+        mlp[c] = ref[...].astype(F32)
     n_seq, rows, share = o.shape
     for s in range(n_seq):
         at = pl.ds(s * share, share)
         for c in range(3):
-            out[:, c, at] = qkv[s, :, c * share : (c + 1) * share].astype(F32)
-        out[:, 3, at] = o[s].astype(F32)
+            attn[:, c, at] = qkv[s, :, c * share : (c + 1) * share].astype(F32)
+        attn[:, 3, at] = o[s].astype(F32)
+    out[...] = rows_out[...]
+    back[...] = rows_in[...]
+    gain[...] = gains[...]
 
 
 def grid_call(kernel, name, grid, args, in_specs, outs, out_specs, scratch=(), aliases=None):
@@ -1216,81 +1386,63 @@
     )(*args)
 
 
-def angles(positions):
-    freqs = ROPE_BASE ** (-jnp.arange(0, HEAD, 2).astype(jnp.float32) / HEAD)
-    turn = positions.astype(jnp.float32)[:, None] * freqs[None, :]
-    cosine, sine = jnp.cos(turn), jnp.sin(turn)
-    return jnp.concatenate([cosine] * 4, 1), jnp.concatenate([-sine, sine] * 2, 1)
-
-
 def on_device(
     n_seq, n_fsdp,
     hidden_in, gain_attn, attn_weights, gain_mlp, mlp_weights, out_grad, block_slots, doc_ids,
 ):
     tok, model = hidden_in.shape[1:]
     share = model // n_seq
-    block_rows = tok // 2
-    within = jnp.arange(block_rows, dtype=jnp.int32)
-    slot = block_slots.reshape(-1)
-    pos = (slot[:, None] * block_rows + within[None, :]).reshape(-1)
-    pick = slot[:, None] == jnp.arange(slot.shape[0], dtype=jnp.int32)[None, :]
-    doc = doc_ids[0].reshape(1, -1, block_rows)
-    doc = jnp.sum(jnp.where(pick[:, :, None], doc, 0), axis=1).reshape(-1)
-    tables = (*angles(pos), pos[:, None], pos[None, :], doc[:, None], doc[None, :])
     start = lax.axis_index("seq") * share
     w_own = lax.dynamic_slice_in_dim(attn_weights, start, share, 2).reshape(-1, 4 * share)
-    gains = jnp.concatenate(
-        [
-            jnp.broadcast_to(gain_attn[None], (16,) + gain_attn.shape),
-            jnp.broadcast_to(gain_mlp[None], (16,) + gain_mlp.shape),
-        ],
-        0,
-    )
     mlp_w = mlp_weights.transpose(1, 0, 2)
-    a = front(n_seq, n_fsdp, w_own, hidden_in[0], gains, out_grad[0], mlp_w, tables)
-    n2_all, grad_all = a.n2_out.reshape(-1, model), a.grad_out.reshape(-1, model)
+    a = front(
+        n_seq, n_fsdp, w_own, hidden_in[0], [gain_attn[None], gain_mlp[None]], out_grad[0], mlp_w,
+        block_slots, doc_ids,
+    )
+    tables = (a.cos, a.sin, a.pos_col, a.pos_row, a.doc_col, a.doc_row)
     w_qkv, w_o = a.w_qkv_out.reshape(model, -1), a.w_o_out.reshape(model, -1)
-    grad_down = dot(a.hid, grad_all, TN).astype(BF16)
-    grad_gate = dot(a.dg, n2_all, TN).astype(BF16)
-    grad_up = dot(a.du, n2_all, TN).astype(BF16)
-    dn2_part = (dot(a.dg, mlp_w[0], NN) + dot(a.du, mlp_w[1], NN)).astype(BF16)
-    out_part = dot(a.hid, mlp_w[2], NN).astype(BF16)
+    m = middle(
+        n_seq, n_fsdp, a.hid, a.dg, a.du, a.n2_out, a.grad_out, mlp_w, a.middle, out_grad[0], a.gain_m
+    )
     b = back_one(
-        n_seq, n_fsdp, dn2_part.reshape(n_fsdp, tok, model), a.middle, out_grad[0], a.gain_m,
-        w_qkv, w_o, a.o_out, a.n1_out, (a.q, a.k, a.v, a.lse, *tables), (grad_down, grad_gate),
-    )
-    grad_down, grad_gate = b.g_out
+        n_seq, n_fsdp, m.da_cols, w_qkv, w_o, a.o_out, a.n1_out,
+        (a.q, a.k, a.v, a.lse, *tables), m.out_part, a.middle, m.grads[0],
+    )
     c = back_two(
         n_seq, n_fsdp, b.dn1_part, b.dw_qkv.reshape(n_fsdp, -1, 3 * share), b.dw_o,
-        out_part.reshape(n_fsdp, tok, model), a.middle, hidden_in[0], b.dh1, a.gain_a, b.gain,
-        grad_up,
-    )
-    own_rows, units = b.dw_o.shape[0], grad_up.shape[0]
-    step = min(own_rows, 64)
-    attn_grad = grid_call(
-        widen_attn_kernel,
-        "widen_attn",
-        (own_rows // step,),
-        (c.dw_qkv_all, c.dw_o_all),
+        hidden_in[0], m.dh1, a.gain_a, m.gain, m.grads[1],
+    )
+    own_rows, units = b.dw_o.shape[0], c.g_out.shape[0]
+    steps = 8
+    u, a_rows, t = units // steps, own_rows // steps, tok // steps
+    flat = pl.BlockSpec((u, model), lambda i: (i, 0))
+    row = pl.BlockSpec((t, model), lambda i: (i, 0))
+    whole = pl.BlockSpec(c.gains.shape, lambda i: (0, 0))
+    mlp_grad, attn_grad, block_out, grad_in, gains = grid_call(
+        finish_kernel,
+        "finish",
+        (steps,),
+        (b.g_out, c.g_out, m.grad_down, c.dw_qkv_all, c.dw_o_all, b.block_out, c.grad_in, c.gains),
+        [flat] * 3
+        + [pl.BlockSpec((n_seq, a_rows, n * share), lambda i: (0, i, 0)) for n in (3, 1)]
+        + [row, row, whole],
         [
-            pl.BlockSpec((n_seq, step, 3 * share), lambda i: (0, i, 0)),
-            pl.BlockSpec((n_seq, step, share), lambda i: (0, i, 0)),
+            like((3, units, model), F32),
+            like((own_rows, 4, model), F32),
+            like((tok, model)),
+            like((tok, model)),
+            like(c.gains.shape, F32),
         ],
-        like((own_rows, 4, model), F32),
-        pl.BlockSpec((step, 4, model), lambda i: (i, 0, 0)),
-    )
-    step = min(units, 128)
-    mlp_grad = grid_call(
-        widen_mlp_kernel,
-        "widen_mlp",
-        (units // step,),
-        (grad_gate, c.g_out, grad_down),
-        [pl.BlockSpec((step, model), lambda i: (i, 0))] * 3,
-        like((3, units, model), F32),
-        pl.BlockSpec((3, step, model), lambda i: (0, i, 0)),
+        [
+            pl.BlockSpec((3, u, model), lambda i: (0, i, 0)),
+            pl.BlockSpec((a_rows, 4, model), lambda i: (i, 0, 0)),
+            row,
+            row,
+            whole,
+        ],
     )
     mlp_grad = mlp_grad.transpose(1, 0, 2)
-    return (c.block_out[None], c.grad_in[None], c.gains[0], attn_grad, c.gains[1], mlp_grad)
+    return (block_out[None], grad_in[None], gains[0], attn_grad, gains[1], mlp_grad)
 
 
 def solution(mesh):

time: 597 us -> 542 us (0.908)
  matrix products: 41.3 us -> 0 us
    dot_general x6 -> x0, matrix products: 41.3 us -> none  [dot(): return lax.dot_general(a, b, (dims, ((), ())), preferred_element_type=F32)]
    pallas_call x3 -> x4, Pallas kernels: 511 us -> 506 us  [run(): pl.pallas_call(kernel, out_shape=self.outs, in_specs=self.in_specs, out_s...]
    pallas_call x2 -> x1, Pallas kernels: 17.1 us -> 16.3 us  [grid_call(): pl.pallas_call(kernel, grid=grid, out_shape=outs, in_specs=in_specs, out_...]
where the time goes in v3:
time: 542 us; the launch traced here: 536 us
  Pallas kernels  523 us (96%)
  local copies, waits for them, and re-layouts  12 us (2%)
    pallas_call x4, Pallas kernels, run(): pl.pallas_call(kernel, out_shape=self.outs, in_specs=self.in_specs, out_s...  506 us
    pallas_call x1, Pallas kernels, grid_call(): pl.pallas_call(kernel, grid=grid, out_shape=outs, in_specs=in_specs, out_...  16.3 us

profile of v3, /device:TPU:8, one launch (start us, length us, event | category | flops | bytes accessed | tf_op | source)
XLA Modules:
  0.0 535.5 jit_solution(15363374157623219072)
XLA Ops:
  0.6 1.2 broadcast_in_dim.12.refs_1_
  1.9 1.2 broadcast_in_dim.13.refs_2_
  3.1 1.3 copy.14.refs_4_
  4.4 1.6 constant_dynamic-slice_fusion
  6.0 1.2 copy.15
  7.2 153.4 %front.1 = (bf16[8,256,1536]{2,1,0:T(8,128)(2,1)}, bf16[8,256,512]{2,1,0:T(8,128)(2,1)}, bf16[4,512,512]{2,1,0:T(8,128)(2,1)}, bf16[4,512,512]{2,1,0:T(8,128)(2,...) custom-call(bf16[128,2048]{1,0:T(8,128)(2,1)} %bitcast.21, ...), custom_call_target="tpu_custom_call" | custom-call | tf_op jit(solution)/shard_map/front/pallas_call | solution.py:578
  160.6 114.4 %middle.1 = (bf16[1024,2048]{1,0:T(8,128)(2,1)}, bf16[1024,2048]{1,0:T(8,128)(2,1)}, bf16[1024,2048]{1,0:T(8,128)(2,1)}, bf16[8,128,2048]{2,1,0:T(8,128)(2,1)}, ...) custom-call(f32[128,2048]{1,0:T(8,128)} %get-tuple-element.50.refs_0_.refs_1_, ...), custom_call_target="tpu_custom_call" | custom-call | tf_op jit(solution)/shard_map/middle/pallas_call | solution.py:578
  275.1 108.4 %back_one.1 = (bf16[1024,2048]{1,0:T(8,128)(2,1)}, bf16[2048,1536]{1,0:T(8,128)(2,1)}, bf16[4,128,2048]{2,1,0:T(8,128)(2,1)}, bf16[256,512]{1,0:T(8,128)(2,1)}, bf16[128,2048]{1,0:T(8,128)(2,1)}) custom-call(bf16[512,512]{1,0:T(8,128)(2,1)} %get-tuple-element.57.refs_0_, f32[128,2048]{1,0:T(8,128)} %get-tuple-element.50.refs_0_.refs_1_, ...), custom_call_target="tpu_custom_call" | custom-call | tf_op jit(solution)/shard_map/back_one/pallas_call | solution.py:578
  383.5 0.0 copy-start.2
  383.6 130.0 %back_two.1 = (bf16[1024,2048]{1,0:T(8,128)(2,1)}, bf16[4,256,1536]{2,1,0:T(8,128)(2,1)}, bf16[4,256,512]{2,1,0:T(8,128)(2,1)}, bf16[128,2048]{1,0:T(8,128)(2,1)}, f32[8,256]{1,0:T(8,128)}) custom-call(bf16[4,128,2048]{2,1,0:T(8,128)(2,1)} %get-tuple-element.75.refs_0_, bf16[128,2048]{1,0:T(8,128)(2,1)} %bitcast.22, f32[128,2048]{1,0:T(8,128)} %get-tuple-element.76.refs_2_, ...), custom_call_target="tpu_custom_call" | custom-call | tf_op jit(solution)/shard_map/back_two/pallas_call | solution.py:578
  513.6 0.0 copy-done.2
  513.6 0.0 copy-start
  513.6 1.9 copy-done
  515.5 0.0 copy-start.1
  515.5 1.2 copy-done.1
  516.7 0.0 copy-start.3
  516.7 1.0 copy-done.3
  517.7 0.0 copy-start.4
  517.7 0.7 copy-done.4
  518.4 16.3 %finish.1 = (f32[3,1024,2048]{2,1,0:T(8,128)}, f32[256,4,2048]{2,1,0:T(4,128)}, bf16[128,2048]{1,0:T(8,128)(2,1)}, bf16[128,2048]{1,0:T(8,128)(2,1)}, f32[8,256]{1,0:T(8,128)S(1)}) custom-call(bf16[1024,2048]{1,0:T(8,128)(2,1)} %get-tuple-element.74.gate, bf16[1024,2048]{1,0:T(8,128)(2,1)} %get-tuple-element.82.up, ...), custom_call_target="tpu_custom_call" | custom-call | tf_op jit(solution)/shard_map/finish/pallas_call | solution.py:1376
  534.8 0.6 fusion
Async XLA Ops:
  383.5 130.0 %copy-start.2 = (bf16[128,2048]{1,0:T(8,128)(2,1)S(1)}, bf16[128,2048]{1,0:T(8,128)(2,1)}, u32[]{:S(2)}) copy-start(bf16[128,2048]{1,0:T(8,128)(2,1)} %get-tuple-element.86.rows_out) | copy-start | bytes 1572868
  513.6 1.9 copy-start
  515.5 1.2 copy-start.1
  516.7 1.0 copy-start.3
  517.7 0.7 copy-start.4

commit v4 on v3

--- a/solution.py
+++ b/solution.py
@@ -212,33 +212,33 @@
             for one in loads:
                 one.wait()
         yield
-        for j in range(line - 1):
+        for t in range(line - 1):
             for k in range(parts):
-                b = line - 1 - j
-
-                @pl.when(b > r)
+                high, low = line - 1 - t + r, t - (line - 1 - r)
+
+                @pl.when(high < line)
                 def _():
-                    to_sister(b, k).wait_recv()
+                    to_sister(high, k).wait_recv()
 
                     @pl.when(r > 0)
                     def _():
-                        go_up(b, k).wait_recv()
-                        add(b, k, [b])
-
-                    pl.when(r == 0)(lambda: add(b, k, []))
-                    go_up(b, k).start()
-
-                @pl.when(j < r)
+                        go_up(high, k).wait_recv()
+                        add(high, k, [high])
+
+                    pl.when(r == 0)(lambda: add(high, k, []))
+                    go_up(high, k).start()
+
+                @pl.when(low >= 0)
                 def _():
-                    to_sister(j, k).wait_recv()
+                    to_sister(low, k).wait_recv()
 
                     @pl.when(r < line - 1)
                     def _():
-                        go_down(j, k, -1).wait_recv()
-                        add(j, k, [j])
-
-                    pl.when(r == line - 1)(lambda: add(j, k, []))
-                    go_down(j, k, r - 1).start()
+                        go_down(low, k, -1).wait_recv()
+                        add(low, k, [low])
+
+                    pl.when(r == line - 1)(lambda: add(low, k, []))
+                    go_down(low, k, r - 1).start()
 
             yield
         for k in range(parts):
@@ -538,6 +538,7 @@
     def __init__(self):
         self.args, self.in_specs, self.outs, self.out_specs, self.scratch = [], [], [], [], []
         self.names = ([], [], [])
+        self.brought, self.posted = [], []
 
     def note(self, group, name, x):
         many = isinstance(x, (list, tuple))
@@ -559,6 +560,17 @@
     def keep(self, **kinds):
         for name, x in kinds.items():
             self.scratch += self.note(2, name, x)
+
+    def bring(self, **arrays):
+        names = list(arrays)
+        self.take(ANY, **{far(n): x for n, x in arrays.items()})
+        self.keep(**{n: pltpu.VMEM(x.shape, x.dtype) for n, x in arrays.items()})
+        self.brought = names
+
+    def post(self, **shapes):
+        self.give(ANY, **{far(n): x for n, x in shapes.items()})
+        self.keep(**{n: pltpu.VMEM(x.shape, x.dtype) for n, x in shapes.items()})
+        self.posted = list(shapes)
 
     def bind(self, refs, groups):
         table, refs = types.SimpleNamespace(), list(refs)
@@ -570,10 +582,39 @@
         return table
 
     def run(self, body, name, collective_id, n_seq, n_fsdp):
+        if self.brought:
+            self.keep(brought_s=DMA((len(self.brought),)))
+        if self.posted:
+            self.keep(posted_s=DMA((len(self.posted),)))
+
         def kernel(*refs):
             at = Place(n_seq, n_fsdp)
+            r = self.bind(refs, (0, 1, 2))
+            loads = [
+                pltpu.make_async_copy(getattr(r, far(n)), getattr(r, n), r.brought_s.at[i])
+                for i, n in enumerate(self.brought)
+            ]
+            stores = [
+                pltpu.make_async_copy(getattr(r, n), getattr(r, far(n)), r.posted_s.at[i])
+                for i, n in enumerate(self.posted)
+            ]
+            for one in loads:
+                one.start()
+
+            def arrive():
+                for one in loads:
+                    one.wait()
+
+            def leave(*mine):
+                for n, one in zip(self.posted, stores):
+                    if any(getattr(r, n) is ref for ref in mine):
+                        one.start()
+
+            r.arrive, r.leave = arrive, leave
             at.greet()
-            body(at, self.bind(refs, (0, 1, 2)))
+            body(at, r)
+            for one in stores:
+                one.wait()
 
         out = pl.pallas_call(
             kernel,
@@ -586,7 +627,14 @@
             ),
             name=name,
         )(*self.args)
-        return self.bind(out, (1,))
+        results = self.bind(out, (1,))
+        for n in self.posted:
+            setattr(results, n, getattr(results, far(n)))
+        return results
+
+
+def far(name):
+    return name + "_far"
 
 
 def like(shape, dtype=BF16):
@@ -669,13 +717,13 @@
 
 def fill_tables(slots, docs, r):
     length = docs.shape[1]
-    block = length // (2 * slots.shape[0])
+    block = length // (2 * slots.shape[1])
 
     def place(shape, axis):
         i = lax.broadcasted_iota(jnp.int32, shape, axis)
         slot = jnp.zeros(shape, jnp.int32)
-        for j in range(2 * slots.shape[0]):
-            slot = jnp.where(i // block == j, slots[j // 2, j % 2], slot)
+        for j in range(2 * slots.shape[1]):
+            slot = jnp.where(i // block == j, slots[j % 2, j // 2], slot)
         return slot * block + i % block
 
     r.pos_col[...] = place((length, 1), 0)
@@ -733,17 +781,19 @@
         dg=like((n_fsdp * tok, units)),
         du=like((n_fsdp * tok, units)),
     )
-    rooms.give(
-        VMEM,
+    rooms.post(
         q=like((length, share)),
         k=like((length, share)),
         v=like((length, share)),
         lse=like((length, 128), F32),
         middle=like((tok, model), F32),
+        cos=like((length, 128), F32),
+        sin=like((length, 128), F32),
+    )
+    rooms.give(
+        VMEM,
         gain_a=like((1, model), F32),
         gain_m=like((1, model), F32),
-        cos=like((length, 128), F32),
-        sin=like((length, 128), F32),
         pos_col=like((length, 1), jnp.int32),
         pos_row=like((1, length), jnp.int32),
         doc_col=like((length, 1), jnp.int32),
@@ -871,11 +921,13 @@
             for one in loads:
                 one.start()
             r.act[...] = jnp.zeros_like(r.act)
-            for i, gain in enumerate(r.own_gains):
-                r.gains[16 * i : 16 * i + 16] = jnp.broadcast_to(gain[...], (16, rows_f))
+            for i in range(2):
+                gain = r.own_gains[i : i + 1]
+                r.gains[16 * i : 16 * i + 16] = jnp.broadcast_to(gain, (16, rows_f)).astype(BF16)
             gain_steps = get_gain.steps(at, r.gains, r.gains_all, r.get_gain)
             next(gain_steps)
             fill_tables(r.slots, r.docs, r)
+            r.leave(r.cos, r.sin)
             for _ in gain_steps:
                 pass
             for f in range(n_fsdp):
@@ -908,6 +960,7 @@
                     field = r.act[total(c, slice(0, length), slice(j, j + 128))]
                     out[:, j : j + 128] = turned(field, r.cos[...], r.sin[...]).astype(BF16)
             r.v[...] = r.act[total(2, slice(0, length), slice(0, share))].astype(BF16)
+            r.leave(r.q, r.k, r.v)
             projected.append(True)
             yield
             for pair in range(n_pairs):
@@ -915,6 +968,7 @@
                 for d in reversed(range(1, n_seq)):
                     go_o(pair, d, at.s).start()
                 yield
+            r.leave(r.lse)
             for _ in out_weights:
                 pass
             for d in range(n_seq):
@@ -955,6 +1009,7 @@
                 return carry
 
             lax.fori_loop(0, tok // 16, middle, 0)
+            r.leave(r.middle)
             yield
             tokens = get_n2.steps(at, r.n2, r.n2_all, r.get_n2, activate)
             next(tokens)
@@ -1006,7 +1061,8 @@
     share, length, line = model // n_seq, n_seq * tok, n_fsdp // 2
     step = min(256, units)
     rooms = Rooms()
-    rooms.take(VMEM, h1=h1, out_grad=out_grad, gain_m=gain_m)
+    rooms.bring(h1=h1, out_grad=out_grad)
+    rooms.take(VMEM, gain_m=gain_m)
     rooms.take(ANY, far=[hid, grad_all, dg, du, n2_all], mlp_w=mlp_w)
     rooms.give(
         ANY,
@@ -1062,6 +1118,7 @@
                 part = dot(dg[rows], gate_w[...], NN) + dot(du[rows], up_w[...], NN)
                 r.dn2_part[2 * b : 2 * b + 2] = part.astype(BF16).reshape(2, tok, model)
             yield from scatter.steps(at, [r.dn2_part, r.dn2] + r.scatter)
+            r.arrive()
             h1, out_grad, gain_m = r.h1, r.out_grad, r.gain_m
             dn2, dh1, da, gain = r.dn2, r.dh1, r.da, r.gain
             gain[...] = jnp.zeros_like(gain)
@@ -1139,9 +1196,9 @@
     (length, share), model = q.shape, w_qkv.shape[0]
     tok = length // n_seq
     rooms = Rooms()
+    rooms.bring(h1=h1, q=q, k=k, v=v, lse=lse, cos=cos, sin=sin)
     rooms.take(
-        VMEM, da_cols=da_cols, h1=h1, q=q, k=k, v=v, lse=lse,
-        cos=cos, sin=sin, pos_col=pos_col, pos_row=pos_row, doc_col=doc_col, doc_row=doc_row,
+        VMEM, da_cols=da_cols, pos_col=pos_col, pos_row=pos_row, doc_col=doc_col, doc_row=doc_row
     )
     rooms.take(ANY, w_qkv=w_qkv, w_o=w_o, o_all=o_all, n1=n1, out_part=out_part, g_in=grad)
     rooms.give(ANY, g_out=like(grad.shape), dw_qkv=like((model, 3 * share)))
@@ -1177,6 +1234,8 @@
     )
 
     def body(at, r):
+        begun = []
+
         def chain():
             loads = [
                 pltpu.make_async_copy(a, b, r.load.at[i])
@@ -1205,6 +1264,8 @@
             loads[3].start()
             running[1] = line_o.steps(at, [dw_o, r.dw_o] + r.line_o)
             yield
+            r.arrive()
+            begun.append(True)
             for _ in exchange:
                 yield
             do = r.do
@@ -1243,6 +1304,8 @@
 
         def rows_out():
             yield from line_out.steps(at, [r.out_part, r.mlp_out] + r.line_out)
+            while not begun:
+                yield
             h1, mlp_out, block_out = r.h1, r.mlp_out, r.block_out
 
             def add(i, carry):
@@ -1279,9 +1342,9 @@
     spread, spread_o = SpreadSeq(n_seq), SpreadSeq(n_seq)
     gather = GatherSeq(n_seq)
     rooms.take(
-        VMEM, dn1_part=dn1_part, source=source, dh1=dh1,
-        gain_a=gain_a, gain_m_term=gain_m_term,
-    )
+        VMEM, dn1_part=dn1_part, gain_a=gain_a, gain_m_term=gain_m_term,
+    )
+    rooms.bring(source=source, dh1=dh1)
     rooms.take(ANY, dw_qkv=dw_qkv, dw_o=dw_o, g_in=grad)
     rooms.give(
         ANY,
@@ -1317,6 +1380,7 @@
 
         def rows_in():
             yield from scatter.steps(at, r.dn1_part, r.dn1, r.scatter)
+            r.arrive()
             source, dh1, dn1 = r.source, r.dh1, r.dn1
             gain_a, grad_in, gain_sum = r.gain_a, r.grad_in, r.gain_sum
             gain_sum[...] = jnp.zeros_like(gain_sum)
@@ -1381,7 +1445,7 @@
         out_specs=out_specs,
         scratch_shapes=list(scratch),
         input_output_aliases=aliases or {},
-        compiler_params=pltpu.CompilerParams(vmem_limit_bytes=48 * 2**20),
+        compiler_params=pltpu.CompilerParams(vmem_limit_bytes=62 * 2**20),
         name=name,
     )(*args)
 
@@ -1396,8 +1460,9 @@
     w_own = lax.dynamic_slice_in_dim(attn_weights, start, share, 2).reshape(-1, 4 * share)
     mlp_w = mlp_weights.transpose(1, 0, 2)
     a = front(
-        n_seq, n_fsdp, w_own, hidden_in[0], [gain_attn[None], gain_mlp[None]], out_grad[0], mlp_w,
-        block_slots, doc_ids,
+        n_seq, n_fsdp, w_own, hidden_in[0], jnp.stack([gain_attn, gain_mlp]).astype(F32), out_grad[0],
+        mlp_w,
+        block_slots.T, doc_ids,
     )
     tables = (a.cos, a.sin, a.pos_col, a.pos_row, a.doc_col, a.doc_row)
     w_qkv, w_o = a.w_qkv_out.reshape(model, -1), a.w_o_out.reshape(model, -1)

time: 542 us -> 507 us (0.935)
  Pallas kernels: 523 us -> 490 us
  local copies, waits for them, and re-layouts: 12 us -> 5.49 us
    pallas_call x4, Pallas kernels: 506 us -> 470 us  [run(): pl.pallas_call(kernel, out_shape=self.outs, in_specs=self.in_specs, out_s...]
    unnamed x12 -> x1, local copies, waits for them, and re-layouts: 7.43 us -> 1.25 us
where the time goes in v4:
time: 507 us; the launch traced here: 497 us
  Pallas kernels  490 us (97%)
  local copies, waits for them, and re-layouts  5.49 us (1%)
    pallas_call x4, Pallas kernels, run(): pl.pallas_call(kernel, out_shape=self.outs, in_specs=self.in_specs, out_s...  470 us
    pallas_call x1, Pallas kernels, grid_call(): pl.pallas_call(kernel, grid=grid, out_shape=outs, in_specs=in_specs, out_...  19.3 us

profile of v4, /device:TPU:8, one launch (start us, length us, event | category | flops | bytes accessed | tf_op | source)
XLA Modules:
  0.0 496.6 jit_solution(4545707035117683635)
XLA Ops:
  0.6 0.7 stack.9
  1.3 0.7 stack.10
  2.0 0.6 maximum_convert_fusion.refs_1_
  2.5 1.6 constant_dynamic-slice_fusion
  4.1 1.2 copy.14
  5.4 152.4 %front.1 = (bf16[8,256,1536]{2,1,0:T(8,128)(2,1)}, bf16[8,256,512]{2,1,0:T(8,128)(2,1)}, bf16[4,512,512]{2,1,0:T(8,128)(2,1)}, bf16[4,512,512]{2,1,0:T(8,128)(2,...) custom-call(bf16[128,2048]{1,0:T(8,128)(2,1)} %bitcast.22, ...), custom_call_target="tpu_custom_call" | custom-call | tf_op jit(solution)/shard_map/front/pallas_call | solution.py:619
  157.8 94.0 %middle.1 = (bf16[1024,2048]{1,0:T(8,128)(2,1)}, bf16[1024,2048]{1,0:T(8,128)(2,1)}, bf16[1024,2048]{1,0:T(8,128)(2,1)}, bf16[8,128,2048]{2,1,0:T(8,128)(2,1)}, ...) custom-call(f32[128,2048]{1,0:T(8,128)} %get-tuple-element.50.refs_0_, ...), custom_call_target="tpu_custom_call" | custom-call | tf_op jit(solution)/shard_map/middle/pallas_call | solution.py:619
  251.8 96.9 %back_one.1 = (bf16[1024,2048]{1,0:T(8,128)(2,1)}, bf16[2048,1536]{1,0:T(8,128)(2,1)}, bf16[4,128,2048]{2,1,0:T(8,128)(2,1)}, bf16[256,512]{1,0:T(8,128)(2,1)}, bf16[128,2048]{1,0:T(8,128)(2,1)}) custom-call(f32[128,2048]{1,0:T(8,128)} %get-tuple-element.50.refs_0_, bf16[512,512]{1,0:T(8,128)(2,1)} %get-tuple-element.51.refs_1_, ...), custom_call_target="tpu_custom_call" | custom-call | tf_op jit(solution)/shard_map/back_one/pallas_call | solution.py:619
  348.7 127.1 %back_two.1 = (bf16[1024,2048]{1,0:T(8,128)(2,1)}, bf16[4,256,1536]{2,1,0:T(8,128)(2,1)}, bf16[4,256,512]{2,1,0:T(8,128)(2,1)}, bf16[128,2048]{1,0:T(8,128)(2,1)}, f32[8,256]{1,0:T(8,128)}) custom-call(bf16[4,128,2048]{2,1,0:T(8,128)(2,1)} %get-tuple-element.75.refs_0_, f32[1,2048]{1,0:T(1,128)} %get-tuple-element.76.refs_1_, ...), custom_call_target="tpu_custom_call" | custom-call | tf_op jit(solution)/shard_map/back_two/pallas_call | solution.py:619
  475.8 19.3 %finish.1 = (f32[3,1024,2048]{2,1,0:T(8,128)}, f32[256,4,2048]{2,1,0:T(4,128)}, bf16[128,2048]{1,0:T(8,128)(2,1)}, bf16[128,2048]{1,0:T(8,128)(2,1)}, f32[8,256]{1,0:T(8,128)}) custom-call(bf16[1024,2048]{1,0:T(8,128)(2,1)} %get-tuple-element.74.gate, bf16[1024,2048]{1,0:T(8,128)(2,1)} %get-tuple-element.82.up, bf16[1024,2048]{1,0:T(8,128)(2,1)} %get-tuple-element.83.down, ...), custom_call_target="tpu_custom_call" | custom-call | tf_op jit(solution)/shard_map/finish/pallas_call | solution.py:1440
  495.1 1.3 fusion

commit v5 on v4

--- a/solution.py
+++ b/solution.py
@@ -1052,7 +1052,8 @@
     return rooms.run(body, "front", 1, n_seq, n_fsdp)
 
 
-MIDDLE_ORDER = [0, 0, 1, 1, 2, 2, 2, 2, 0, 1, 1, 2, 2, 0, 1, 1, 2, 2, 0, 1, 1, 0, 1, 1]
+MIDDLE_ORDER = [0, 0, 1, 1, 2, 0, 1, 1, 2, 0, 1, 1, 2, 0, 1, 1, 2, 0, 1, 1, 2, 0, 1, 1, 2, 2, 2, 2, 2, 2]
+MIDDLE_ORDER += [2]
 
 
 def middle(n_seq, n_fsdp, hid, dg, du, n2_all, grad_all, mlp_w, h1, out_grad, gain_m):
@@ -1187,8 +1188,8 @@
     return rooms.run(body, "middle", 4, n_seq, n_fsdp)
 
 
-BACK_ONE_ORDER = [2, 0, 3, 0, 1, 2, 2, 3, 2, 2, 1, 0, 2, 2, 3, 2, 0, 2, 1, 0, 2, 0, 2, 3, 0, 2, 0, 2]
-BACK_ONE_ORDER += [0, 1, 2, 0, 2, 3, 0, 2, 0, 2, 0]
+BACK_ONE_ORDER = [2, 0, 3, 0, 1, 2, 2, 3, 2, 2, 1, 0, 2, 2, 0, 2, 3, 0, 1, 0, 0, 2, 2, 3, 0, 0, 2, 1, 0, 0]
+BACK_ONE_ORDER += [2, 2, 0, 0, 3, 0, 2]
 
 
 def back_one(n_seq, n_fsdp, da_cols, w_qkv, w_o, o_all, n1, saved, out_part, h1, grad):
@@ -1325,8 +1326,8 @@
     return rooms.run(body, "back_one", 2, n_seq, n_fsdp)
 
 
-BACK_TWO_ORDER = [0, 2, 1, 3, 0, 2, 1, 1, 3, 2, 1, 1, 0, 2, 2, 1, 1, 2, 1, 1, 2, 0, 2, 1, 1, 0, 0, 2, 2]
-BACK_TWO_ORDER += [1, 1, 1, 1, 3, 3, 0, 1, 1, 0]
+BACK_TWO_ORDER = [0, 2, 3, 1, 0, 2, 1, 1, 3, 2, 1, 1, 0, 2, 2, 2, 1, 1, 2, 1, 1, 2, 0, 0, 0, 1, 1, 2, 2, 1]
+BACK_TWO_ORDER += [1, 0, 1, 1, 3, 0]
 
 
 def back_two(

time: 507 us -> 503 us (level)
  no operation moved by 1% of the time
where the time goes in v5:
time: 503 us; the launch traced here: 496 us
  Pallas kernels  489 us (97%)
  local copies, waits for them, and re-layouts  5.49 us (1%)
    pallas_call x4, Pallas kernels, run(): pl.pallas_call(kernel, out_shape=self.outs, in_specs=self.in_specs, out_s...  470 us
    pallas_call x1, Pallas kernels, grid_call(): pl.pallas_call(kernel, grid=grid, out_shape=outs, in_specs=in_specs, out_...  19.3 us

profile of v5, /device:TPU:8, one launch (start us, length us, event | category | flops | bytes accessed | tf_op | source)
XLA Modules:
  0.0 496.1 jit_solution(15390844731256457354)
XLA Ops:
  0.6 0.7 stack.9
  1.3 0.7 stack.10
  2.0 0.6 maximum_convert_fusion.refs_1_
  2.5 1.6 constant_dynamic-slice_fusion
  4.1 1.2 copy.14
  5.4 152.5 %front.1 = (bf16[8,256,1536]{2,1,0:T(8,128)(2,1)}, bf16[8,256,512]{2,1,0:T(8,128)(2,1)}, bf16[4,512,512]{2,1,0:T(8,128)(2,1)}, bf16[4,512,512]{2,1,0:T(8,128)(2,...) custom-call(bf16[128,2048]{1,0:T(8,128)(2,1)} %bitcast.22, ...), custom_call_target="tpu_custom_call" | custom-call | tf_op jit(solution)/shard_map/front/pallas_call | solution.py:619
  157.9 95.3 %middle.1 = (bf16[1024,2048]{1,0:T(8,128)(2,1)}, bf16[1024,2048]{1,0:T(8,128)(2,1)}, bf16[1024,2048]{1,0:T(8,128)(2,1)}, bf16[8,128,2048]{2,1,0:T(8,128)(2,1)}, ...) custom-call(f32[128,2048]{1,0:T(8,128)} %get-tuple-element.50.refs_0_, ...), custom_call_target="tpu_custom_call" | custom-call | tf_op jit(solution)/shard_map/middle/pallas_call | solution.py:619
  253.2 96.6 %back_one.1 = (bf16[1024,2048]{1,0:T(8,128)(2,1)}, bf16[2048,1536]{1,0:T(8,128)(2,1)}, bf16[4,128,2048]{2,1,0:T(8,128)(2,1)}, bf16[256,512]{1,0:T(8,128)(2,1)}, bf16[128,2048]{1,0:T(8,128)(2,1)}) custom-call(f32[128,2048]{1,0:T(8,128)} %get-tuple-element.50.refs_0_, bf16[512,512]{1,0:T(8,128)(2,1)} %get-tuple-element.51.refs_1_, ...), custom_call_target="tpu_custom_call" | custom-call | tf_op jit(solution)/shard_map/back_one/pallas_call | solution.py:619
  349.8 125.5 %back_two.1 = (bf16[1024,2048]{1,0:T(8,128)(2,1)}, bf16[4,256,1536]{2,1,0:T(8,128)(2,1)}, bf16[4,256,512]{2,1,0:T(8,128)(2,1)}, bf16[128,2048]{1,0:T(8,128)(2,1)}, f32[8,256]{1,0:T(8,128)}) custom-call(bf16[4,128,2048]{2,1,0:T(8,128)(2,1)} %get-tuple-element.75.refs_0_, f32[1,2048]{1,0:T(1,128)} %get-tuple-element.76.refs_1_, ...), custom_call_target="tpu_custom_call" | custom-call | tf_op jit(solution)/shard_map/back_two/pallas_call | solution.py:619
  475.4 19.3 %finish.1 = (f32[3,1024,2048]{2,1,0:T(8,128)}, f32[256,4,2048]{2,1,0:T(4,128)}, bf16[128,2048]{1,0:T(8,128)(2,1)}, bf16[128,2048]{1,0:T(8,128)(2,1)}, f32[8,256]{1,0:T(8,128)}) custom-call(bf16[1024,2048]{1,0:T(8,128)(2,1)} %get-tuple-element.74.gate, bf16[1024,2048]{1,0:T(8,128)(2,1)} %get-tuple-element.82.up, bf16[1024,2048]{1,0:T(8,128)(2,1)} %get-tuple-element.83.down, ...), custom_call_target="tpu_custom_call" | custom-call | tf_op jit(solution)/shard_map/finish/pallas_call | solution.py:1441
  494.6 1.3 fusion

commit v6 on v5

--- a/solution.py
+++ b/solution.py
@@ -41,8 +41,8 @@
         self.f = lax.axis_index("fsdp")
         self.r = lax.div(self.f, 2)
         self.c = lax.rem(self.f, 2)
-        self.up = (self.s, self.f + 2)
-        self.down = (self.s, self.f - 2)
+        self.up = (self.s, lax.rem(self.f + 2, n_fsdp))
+        self.down = (self.s, lax.rem(self.f + n_fsdp - 2, n_fsdp))
         self.sister = (self.s, 2 * self.r + 1 - self.c)
 
     def peer(self, d):

time: 503 us -> 503 us (level)
  no operation moved by 1% of the time
where the time goes in v6:
time: 503 us; the launch traced here: 496 us
  Pallas kernels  489 us (97%)
  local copies, waits for them, and re-layouts  5.49 us (1%)
    pallas_call x4, Pallas kernels, run(): pl.pallas_call(kernel, out_shape=self.outs, in_specs=self.in_specs, out_s...  470 us
    pallas_call x1, Pallas kernels, grid_call(): pl.pallas_call(kernel, grid=grid, out_shape=outs, in_specs=in_specs, out_...  19.3 us

profile of v6, /device:TPU:8, one launch (start us, length us, event | category | flops | bytes accessed | tf_op | source)
XLA Modules:
  0.0 496.1 jit_solution(8198895662293922521)
XLA Ops:
  0.6 0.7 stack.9
  1.3 0.7 stack.10
  2.0 0.6 maximum_convert_fusion.refs_1_
  2.5 1.6 constant_dynamic-slice_fusion
  4.1 1.2 copy.14
  5.4 152.5 %front.1 = (bf16[8,256,1536]{2,1,0:T(8,128)(2,1)}, bf16[8,256,512]{2,1,0:T(8,128)(2,1)}, bf16[4,512,512]{2,1,0:T(8,128)(2,1)}, bf16[4,512,512]{2,1,0:T(8,128)(2,...) custom-call(bf16[128,2048]{1,0:T(8,128)(2,1)} %bitcast.22, ...), custom_call_target="tpu_custom_call" | custom-call | tf_op jit(solution)/shard_map/front/pallas_call | solution.py:619
  157.9 95.3 %middle.1 = (bf16[1024,2048]{1,0:T(8,128)(2,1)}, bf16[1024,2048]{1,0:T(8,128)(2,1)}, bf16[1024,2048]{1,0:T(8,128)(2,1)}, bf16[8,128,2048]{2,1,0:T(8,128)(2,1)}, ...) custom-call(f32[128,2048]{1,0:T(8,128)} %get-tuple-element.50.refs_0_, ...), custom_call_target="tpu_custom_call" | custom-call | tf_op jit(solution)/shard_map/middle/pallas_call | solution.py:619
  253.2 96.6 %back_one.1 = (bf16[1024,2048]{1,0:T(8,128)(2,1)}, bf16[2048,1536]{1,0:T(8,128)(2,1)}, bf16[4,128,2048]{2,1,0:T(8,128)(2,1)}, bf16[256,512]{1,0:T(8,128)(2,1)}, bf16[128,2048]{1,0:T(8,128)(2,1)}) custom-call(f32[128,2048]{1,0:T(8,128)} %get-tuple-element.50.refs_0_, bf16[512,512]{1,0:T(8,128)(2,1)} %get-tuple-element.51.refs_1_, ...), custom_call_target="tpu_custom_call" | custom-call | tf_op jit(solution)/shard_map/back_one/pallas_call | solution.py:619
  349.8 125.5 %back_two.1 = (bf16[1024,2048]{1,0:T(8,128)(2,1)}, bf16[4,256,1536]{2,1,0:T(8,128)(2,1)}, bf16[4,256,512]{2,1,0:T(8,128)(2,1)}, bf16[128,2048]{1,0:T(8,128)(2,1)}, f32[8,256]{1,0:T(8,128)}) custom-call(bf16[4,128,2048]{2,1,0:T(8,128)(2,1)} %get-tuple-element.75.refs_0_, f32[1,2048]{1,0:T(1,128)} %get-tuple-element.76.refs_1_, ...), custom_call_target="tpu_custom_call" | custom-call | tf_op jit(solution)/shard_map/back_two/pallas_call | solution.py:619
  475.3 19.3 %finish.1 = (f32[3,1024,2048]{2,1,0:T(8,128)}, f32[256,4,2048]{2,1,0:T(4,128)}, bf16[128,2048]{1,0:T(8,128)(2,1)}, bf16[128,2048]{1,0:T(8,128)(2,1)}, f32[8,256]{1,0:T(8,128)}) custom-call(bf16[1024,2048]{1,0:T(8,128)(2,1)} %get-tuple-element.74.gate, bf16[1024,2048]{1,0:T(8,128)(2,1)} %get-tuple-element.82.up, bf16[1024,2048]{1,0:T(8,128)(2,1)} %get-tuple-element.83.down, ...), custom_call_target="tpu_custom_call" | custom-call | tf_op jit(solution)/shard_map/finish/pallas_call | solution.py:1441
  494.6 1.3 fusion
